TPU v7x, 512 devices: a whole 4x8x8 slice. The times are simulated.
512 devices in a mesh: lat: 8 (over x, core), rad: 64 (over z, y).
Axes of the slice: x: 4, y: 8, z: 8, core: 2. Of those that a mesh axis runs over, the one named last changes fastest.
Arguments:
- forcing: bfloat16 [512, 768, 1024], P('rad', 'lat'), may hold values from -6 to 6
- legendre: bfloat16 [256, 512, 768], P('rad', None, 'lat'), may hold values from -0.3125 to 0.3125
- assign: int32 [256], replicated, may hold values from 0 to 511, as said below
- inverse: float32 [512, 512, 512], P(('lat', 'rad')), may hold values from -0.25 to 0.25
- previous: bfloat16 [512, 512, 512], P('rad', 'lat'), may hold values from -6 to 6
Outputs:
- new_state: bfloat16 [512, 512, 512], P('rad', 'lat')
Inputs may be any that keep to these rules, and one draw needn't show every extreme that they name: `assign`: the 256 orders are distinct; 0 and 511 are among them.
All inputs are finite; a program needn't handle non-finite values.
Results may differ from a plain program's by a relative error of at most 0.01.
Values may be sent and summed in bfloat16 or wider, within the bound.
No kernel may reach another device: no remote copies, remote signals or barrier semaphores. Data moves between devices by JAX's collectives and lax.ppermute only.
A program may use at most 64 MiB of HBM per device.

v0:
```python
import math

import jax
import jax.numpy as jnp
from jax import lax
from jax.sharding import PartitionSpec as P

NR = 512
L = 512


time_step = 0.5


def fourier_table(assign, lon_count):
    longitude = jnp.arange(lon_count, dtype=jnp.int32)
    phases = assign[:, None] * longitude[None, :] % lon_count
    angles = phases.astype(jnp.float32) * (2.0 * math.pi / lon_count)
    norm_scale = 1.0 / math.sqrt(lon_count)
    stacked = jnp.stack([jnp.cos(angles), -jnp.sin(angles)], axis=1) * norm_scale
    return stacked.reshape(2 * assign.shape[0], lon_count).T.astype(jnp.bfloat16)


def shards(forcing, legendre, assign, inverse, previous):
    rad_count = lax.axis_size("rad")
    lat_count = lax.axis_size("lat")
    radii_here, lats_here, lon_count = forcing.shape
    slot_count = legendre.shape[0]
    order_total = assign.shape[0]
    table_values = fourier_table(assign, lon_count)
    fourier = jnp.dot(
        forcing.reshape(radii_here * lats_here, lon_count),
        table_values,
        preferred_element_type=jnp.float32,
    )
    fourier = fourier.astype(jnp.bfloat16).reshape(radii_here, lats_here, 2 * order_total)
    arrivals = lax.all_to_all(fourier, "rad", split_axis=2, concat_axis=0, tiled=True)
    order_data = arrivals.reshape(NR, lats_here, slot_count, 2)
    my_orders = lax.dynamic_slice_in_dim(assign, lax.axis_index("rad") * slot_count, slot_count)
    band_rows = L // lat_count
    ell_index = jnp.arange(L, dtype=jnp.int32)
    keep_mask = (ell_index[None, :, None] >= my_orders[:, None, None]).astype(jnp.bfloat16)
    product = jnp.einsum(
        "kel,rlkc->ekcr", legendre * keep_mask, order_data, preferred_element_type=jnp.float32
    )
    summed = lax.psum(product.astype(jnp.bfloat16).reshape(L, slot_count * 2 * NR), "lat").astype(
        jnp.float32
    )
    spectrum = lax.dynamic_slice_in_dim(summed, lax.axis_index("lat") * band_rows, band_rows, 0)
    spectrum = spectrum.reshape(band_rows, slot_count, 2 * NR)
    owned_modes = lax.all_to_all(
        spectrum.astype(jnp.bfloat16), "rad", split_axis=0, concat_axis=1, tiled=True
    ).astype(spectrum.dtype)
    degree_count = owned_modes.shape[0]
    owned_modes = owned_modes.reshape(degree_count, order_total, 2, NR)
    old_state = lax.all_to_all(previous, "rad", split_axis=1, concat_axis=0, tiled=True)
    prior_modes = (
        old_state.astype(jnp.float32)
        .reshape(NR, degree_count, order_total, 2)
        .transpose(1, 2, 3, 0)
    )
    right_side = prior_modes + time_step * owned_modes
    solved = jnp.einsum("ekcr,esr->ekcs", right_side, inverse, precision=lax.Precision.HIGHEST)
    first_degree = (lax.axis_index("lat") * rad_count + lax.axis_index("rad")) * degree_count
    ell_index = first_degree + jnp.arange(degree_count, dtype=jnp.int32)
    valid_mask = (assign[None, :] <= ell_index[:, None]).astype(jnp.float32)
    solved = solved * valid_mask[:, :, None, None]
    outgoing = (
        solved.astype(jnp.bfloat16).transpose(3, 0, 1, 2).reshape(NR, degree_count, 2 * order_total)
    )
    return lax.all_to_all(outgoing, "rad", split_axis=0, concat_axis=1, tiled=True)


def solution(mesh):
    placed = (
        P("rad", "lat", None),
        P("rad", None, "lat"),
        P(),
        P(("lat", "rad"), None, None),
        P("rad", "lat", None),
    )
    return jax.shard_map(
        shards, mesh=mesh, in_specs=placed, out_specs=P("rad", "lat", None), check_vma=False
    )
```

profile of v0, /device:TPU:15, one launch (start us, length us, event | category | flops | bytes accessed | tf_op | source)
XLA Modules:
  0.0 245.0 jit_solution(16525156709318100811)
XLA Ops:
  6.5 0.0 copy-start
  6.5 5.0 %fusion.13 = (f32[256,1,1024]{2,0,1:T(8,128)S(1)}, f32[256,1,1024]{2,0,1:T(8,128)S(1)}) fusion(s32[256]{0:T(256)} %param.7), kind=kLoop, calls=%fused_computation.26 | loop fusion | flops 3932160 | bytes 2098176 | tf_op jit(solution)/shard_map/cos | solution.py:20
  11.5 0.3 fusion
  11.8 1.1 copy.52
  12.9 1.2 convert_element_type.98
  14.1 0.0 copy-done
  14.1 2.2 fusion.2
  16.4 0.3 copy.53
  16.6 0.0 copy-start.4
  16.7 1.4 copy.54
  18.1 16.2 %all-to-all-start.1 = ((bf16[8,96,512]{1,0,2:T(8,128)(2,1)}), bf16[8,96,512]{1,0,2:T(8,128)(2,1)S(1)}, u32[]{:S(2)}, u32[]{:S(2)}) async-start(bf16[8,96,512]{1,0,2:T(8,128)(2,1)} %copy.54), calls=%async_computation.1 | async-start | bytes 2097152 | tf_op jit(solution)/shard_map/all_to_all | solution.py:37
  34.3 0.0 all-reduce.2.cloned.1.call-start
  34.3 0.0 copy-done.4
  34.3 0.1 dynamic_slice.6
  34.4 0.1 fusion.17
  34.5 27.9 %all-to-all-done.1 = bf16[8,96,512]{1,0,2:T(8,128)(2,1)S(1)} async-done(((bf16[8,96,512]{1,0,2:T(8,128)(2,1)}), bf16[8,96,512]{1,0,2:T(8,128)(2,1)S(1)}, u32[]{:S(2)}, u32[]{:S(2)}) %all-to-all-start.1) | async-done | bytes 786464 | tf_op jit(solution)/shard_map/all_to_all | solution.py:37
  62.4 0.2 copy.56
  62.6 0.0 copy-done.2
  62.6 3.2 %convolution_convert_fusion = bf16[4,512,2,512]{3,1,2,0:T(8,128)(2,1)} fusion(bf16[512,96,4,2]{1,0,3,2:T(8,128)(2,1)S(1)} %bitcast.53, bf16[4,512,96]{1,2,0:T(8,128)(2,1)S(1)} %copy-done.2, bf16[4,512]{1,0:T(4,128)(2,1)S(1)} %fusion.17), kind=kOutput, calls=%fused_computation | convolution fusion | flops 404946944 | bytes 5378048 | tf_op jit(solution)/shard_map/kel,rlkc->ekcr/dot_general | solution.py:43
  65.8 6.4 %copy.66 = bf16[512,4096]{1,0:T(8,128)(2,1)} copy(bf16[512,4096]{0,1:T(8,128)(2,1)} %bitcast.52) | data formatting | bytes 8388608 | tf_op jit(solution)/shard_map/reshape | solution.py:46
  72.2 0.0 all-reduce.2.cloned.1.call-update
  72.2 1.0 copy-done.3
  73.3 1.1 copy.50
  74.4 7.0 %all-to-all-start = ((bf16[8,64,512]{2,0,1:T(8,128)(2,1)}), bf16[8,64,512]{2,0,1:T(8,128)(2,1)S(1)}, u32[]{:S(2)}, u32[]{:S(2)}) async-start(bf16[8,64,512]{2,0,1:T(8,128)(2,1)} %copy.50), calls=%async_computation | async-start | bytes 1048576 | tf_op jit(solution)/shard_map/all_to_all | solution.py:56
  81.4 70.7 %all-reduce.2.cloned.1.call-done = bf16[512,4096]{1,0:T(8,128)(2,1)} async-done(((bf16[512,4096]{1,0:T(8,128)(2,1)}), bf16[512,4096]{1,0:T(8,128)(2,1)}) %all-reduce.2.cloned.1.call-update) | async-done | bytes 4194320 | tf_op jit(solution)/shard_map/psum | solution.py:46
  152.1 1.1 convert_convert_fusion
  153.2 1.2 convert_element_type.106
  154.4 0.0 all-to-all-done
  154.4 13.0 %all-to-all-start.2 = ((bf16[64,4,1024]{2,1,0:T(4,128)(2,1)}), bf16[64,4,1024]{2,1,0:T(4,128)(2,1)}, u32[]{:S(2)}, u32[]{:S(2)}) async-start(bf16[64,4,1024]{2,1,0:T(4,128)(2,1)} %convert_element_type.106), calls=%async_computation.2 | async-start | bytes 1048576 | tf_op jit(solution)/shard_map/all_to_all | solution.py:51
  167.4 0.1 convert_bitcast_fusion
  167.5 13.5 %copy.51 = f32[64,8,1,512]{1,0,3,2:T(8,128)} copy(f32[64,8,1,512]{3,1,0,2:T(8,128)S(1)} %convert_bitcast_fusion) | data formatting | bytes 2097152 | tf_op jit(solution)/shard_map/transpose | solution.py:60
  181.0 12.2 %reshape.213 = f32[512,1,256,2]{0,3,2,1:T(2,128)S(1)} reshape(f32[64,8,1,512]{1,0,3,2:T(8,128)} %copy.51) | data formatting | bytes 2097152 | tf_op jit(solution)/shard_map/transpose | solution.py:60
  193.2 0.0 all-to-all-done.2
  193.2 2.3 convert_multiply_fusion
  195.5 3.3 %mul.103 = f32[1,256,2,512]{3,2,1,0:T(2,128)} reshape(f32[64,4,1024]{2,1,0:T(4,128)} %convert_multiply_fusion) | data formatting | bytes 2097152 | tf_op jit(solution)/shard_map/mul | solution.py:62
  198.9 1.9 fusion.8
  200.7 0.0 copy-done.1
  200.7 1.9 fusion.3
  202.6 0.5 copy.60
  203.2 0.2 reshape.212
  203.4 0.5 broadcast.144
  203.9 1.0 reduce
  204.9 0.2 copy.72
  205.2 0.2 reshape.217
  205.4 31.1 %all_to_all.51 = bf16[64,2,2048]{2,1,0:T(2,128)(2,1)S(1)} all-to-all(bf16[64,2,2048]{2,1,0:T(2,128)(2,1)S(1)} %reshape.217), channel_id=1, replica_groups=mesh['lat'=8,'rad'=64] {'rad'}, dimensions={0} | all-to-all | bytes 1048576 | tf_op jit(solution)/shard_map/all_to_all | solution.py:71
  236.5 0.5 reshape.218
  237.0 0.1 copy.71
  237.2 0.9 copy.62
  (4 shorter events, 0.0 us)
Async XLA Ops:
  6.5 7.6 %copy-start = (bf16[8,96,1024]{2,1,0:T(8,128)(2,1)S(1)}, bf16[8,96,1024]{2,1,0:T(8,128)(2,1)}, u32[]{:S(2)}) copy-start(bf16[8,96,1024]{2,1,0:T(8,128)(2,1)} %param.5) | copy-start | bytes 4718596
  16.6 17.7 %copy-start.4 = (s32[256]{0:T(256)S(1)}, s32[256]{0:T(256)}, u32[]{:S(2)}) copy-start(s32[256]{0:T(256)} %param.7) | copy-start | bytes 3076
  18.1 44.5 %copy-start.2 = (bf16[4,512,96]{1,2,0:T(8,128)(2,1)S(1)}, bf16[4,512,96]{1,2,0:T(8,128)(2,1)}, u32[]{:S(2)}) copy-start(bf16[4,512,96]{1,2,0:T(8,128)(2,1)} %param.6) | copy-start | bytes 1179652
  18.1 44.3 %all-to-all-start.1 = ((bf16[8,96,512]{1,0,2:T(8,128)(2,1)}), bf16[8,96,512]{1,0,2:T(8,128)(2,1)S(1)}, u32[]{:S(2)}, u32[]{:S(2)}) async-start(bf16[8,96,512]{1,0,2:T(8,128)(2,1)} %copy.54), calls=%async_computation.1 | async-start | bytes 2097152 | tf_op jit(solution)/shard_map/all_to_all | solution.py:37
  34.3 117.9 %all-reduce.2.cloned.1.call-start = ((), (), s32[]{:S(2)}) async-start(), calls=%async_computation.4 | async-start | bytes 8388608 | tf_op jit(solution)/shard_map/psum | solution.py:46
  72.2 1.0 copy-start.3
  74.4 80.0 %all-to-all-start = ((bf16[8,64,512]{2,0,1:T(8,128)(2,1)}), bf16[8,64,512]{2,0,1:T(8,128)(2,1)S(1)}, u32[]{:S(2)}, u32[]{:S(2)}) async-start(bf16[8,64,512]{2,0,1:T(8,128)(2,1)} %copy.50), calls=%async_computation | async-start | bytes 1048576 | tf_op jit(solution)/shard_map/all_to_all | solution.py:56
  154.4 38.9 %all-to-all-start.2 = ((bf16[64,4,1024]{2,1,0:T(4,128)(2,1)}), bf16[64,4,1024]{2,1,0:T(4,128)(2,1)}, u32[]{:S(2)}, u32[]{:S(2)}) async-start(bf16[64,4,1024]{2,1,0:T(4,128)(2,1)} %convert_element_type.106), calls=%async_computation.2 | async-start | bytes 1048576 | tf_op jit(solution)/shard_map/all_to_all | solution.py:51
  198.9 1.9 copy-start.1
Sparse Core Ops, SparseCore 0:
  72.4 79.7 all-reduce.1
where the time goes:
time: 246 us; the launch traced here: 245 us
  waiting for transfers between devices  98.6 us (40%)
  local copies, waits for them, and re-layouts  46.3 us (19%)
  starting transfers between devices  36.2 us (15%)
  blocking collectives  31.1 us (13%)
  between operations  13.6 us (6%)
  other arithmetic  11.7 us (5%)
  matrix products  7.38 us (3%)
    psum x1, waiting for transfers between devices, shards(): lax.psum(product.astype(jnp.bfloat16).reshape(L, slot_count * 2 * NR), 'l...  70.7 us
    all_to_all x1, blocking collectives, shards(): lax.all_to_all(outgoing, 'rad', split_axis=0, concat_axis=1, tiled=True)  31.1 us
    all_to_all x1, waiting for transfers between devices, shards(): lax.all_to_all(fourier, 'rad', split_axis=2, concat_axis=0, tiled=True)  27.9 us
    transpose x2, local copies, waits for them, and re-layouts, shards(): prior_modes = old_state.astype(jnp.float32).reshape(NR, degree_count, ord...  25.7 us
    all_to_all x1, starting transfers between devices, shards(): lax.all_to_all(fourier, 'rad', split_axis=2, concat_axis=0, tiled=True)  16.2 us
    all_to_all x1, starting transfers between devices, shards(): lax.all_to_all(spectrum.astype(jnp.bfloat16), 'rad', split_axis=0, concat...  13 us
    all_to_all x1, starting transfers between devices, shards(): lax.all_to_all(previous, 'rad', split_axis=1, concat_axis=0, tiled=True)  7.03 us
    reshape x1, local copies, waits for them, and re-layouts, shards(): product.astype(jnp.bfloat16).reshape(L, slot_count * 2 * NR)  6.39 us
  transfers between devices with their start and end apart: 4, of which 2 were waited for; matrix products, arithmetic and copies ran while one was open for 12% of the time, Pallas kernels for 0%

commit v1 on v0

v1 whole, which is shorter than its diff:
```python
import math

import jax
import jax.numpy as jnp
from jax import lax
from jax.experimental import pallas as pl
from jax.experimental.pallas import tpu as pltpu
from jax.sharding import Mesh, PartitionSpec as P

NR = 512
L = 512
LON = 1024
BF = jnp.bfloat16
F32 = jnp.float32
RAD = ("z", "y")
LAT = ("x", "core")


def nt_dot(a, b):
    return lax.dot_general(a, b, (((1,), (1,)), ((), ())), preferred_element_type=F32)


def iota(shape, dim):
    return lax.broadcasted_iota(jnp.int32, shape, dim)


def regroup():
    row, column = iota((512, 512), 0), iota((512, 512), 1)
    return column == (row & 63) * 8 + (row >> 6)


def cos_sin(phase):
    quadrant = ((phase + 128) >> 8) & 3
    rest = ((phase + 128) & 255) - 128
    x = rest.astype(F32) * (2.0 * math.pi / LON)
    x2 = x * x
    sin_x = x * (1.0 + x2 * (-1.0 / 6 + x2 * (1.0 / 120 + x2 * (-1.0 / 5040 + x2 * (1.0 / 362880)))))
    cos_x = 1.0 + x2 * (-0.5 + x2 * (1.0 / 24 + x2 * (-1.0 / 720 + x2 * (1.0 / 40320))))
    swap = (quadrant & 1) == 1
    cos_part = jnp.where(swap, sin_x, cos_x)
    sin_part = jnp.where(swap, cos_x, sin_x)
    cos_sign = jnp.where((quadrant == 1) | (quadrant == 2), -1.0, 1.0)
    sin_sign = jnp.where(quadrant >= 2, -1.0, 1.0)
    return cos_part * cos_sign, sin_part * sin_sign


def fourier_kernel(assign_ref, forcing_ref, previous_ref, out_ref, table_ref):
    row, lane = iota((256, 256), 0), iota((256, 256), 1)
    mine = lane == (row & 63) * 4 + (row >> 6)
    orders = jnp.sum(jnp.where(mine, assign_ref[...], 0), axis=1, keepdims=True)
    lane = iota((256, 128), 1)
    cos_low, sin_low = cos_sin((orders * lane) & (LON - 1))
    cos_high, sin_high = cos_sin((orders * 128 * lane) & (LON - 1))
    scale = LON**-0.5
    cos_low, sin_low = cos_low * scale, sin_low * scale
    for q in range(LON // 128):
        ch, sh = cos_high[:, q : q + 1], sin_high[:, q : q + 1]
        real = (cos_low * ch - sin_low * sh).astype(BF)
        imag = (-(sin_low * ch + cos_low * sh)).astype(BF)
        for x in range(4):
            table_ref[x * 128 : x * 128 + 64, q * 128 : q * 128 + 128] = real[x * 64 : x * 64 + 64]
            table_ref[x * 128 + 64 : x * 128 + 128, q * 128 : q * 128 + 128] = imag[x * 64 : x * 64 + 64]
    table = table_ref[...]
    for h in range(3):
        part = forcing_ref[:, h * 32 : h * 32 + 32, :].reshape(256, LON)
        out_ref[:, h * 256 : h * 256 + 256] = nt_dot(table, part).astype(BF)
    out_ref[:, 768:1280] = nt_dot(regroup().astype(BF), previous_ref[...].reshape(512, 512)).astype(BF)


def legendre_kernel(assign_ref, place_ref, legendre_ref, out_ref):
    slot = place_ref[0]
    lane = iota((1, 256), 1)
    order = jnp.sum(jnp.where(lane == slot, assign_ref[...], 0), axis=1, keepdims=True)
    row, column = iota((512, 512), 0), iota((512, 512), 1)
    degree = (row & 7) * 64 + (row >> 3)
    pick = column == degree
    kept = jnp.where(pick & (degree >= order), 1.0, 0.0).astype(BF)
    for h in range(3):
        for quad in range(2):
            pieces = []
            for i in range(4):
                g = quad * 4 + i
                pieces.append(legendre_ref[g % 2, g // 2, h * 32 : h * 32 + 32, :])
            at = h * 256 + quad * 128
            out_ref[:, at : at + 128] = nt_dot(kept, jnp.concatenate(pieces, axis=0)).astype(BF)
    out_ref[:, 768:1280] = jnp.where(pick, 2.0, 0.0).astype(BF)


def roll(a, shift):
    return pltpu.roll(a, shift, 1)


def spectrum_kernel(arrived_ref, weights_ref, out_ref, gathered_ref):
    lane = iota((64, 128), 1)
    low_half = lane < 64
    even_quarter = (lane & 32) == 0

    def tile(g, at):
        return arrived_ref[g * 64 : g * 64 + 64, at : at + 128].astype(F32)

    def place(rho, at, value):
        gathered_ref[rho * 64 : rho * 64 + 64, at : at + 128] = value.astype(BF)

    for h in range(3):
        for high in range(2):
            for quad in range(2):
                a = [tile(quad * 4 + i, h * 256 + high * 128) for i in range(4)]
                b0 = jnp.where(low_half, a[0], roll(a[2], 64))
                b2 = jnp.where(low_half, roll(a[0], 64), a[2])
                b1 = jnp.where(low_half, a[1], roll(a[3], 64))
                b3 = jnp.where(low_half, roll(a[1], 64), a[3])
                c = [
                    jnp.where(even_quarter, b0, roll(b1, 32)),
                    jnp.where(even_quarter, roll(b0, 96), b1),
                    jnp.where(even_quarter, b2, roll(b3, 32)),
                    jnp.where(even_quarter, roll(b2, 96), b3),
                ]
                for i in range(4):
                    place(high * 4 + i, h * 256 + quad * 128, c[i])
    for pair in range(4):
        for two in range(4):
            at = 768 + pair * 128
            a0, a1 = tile(two * 2, at), tile(two * 2 + 1, at)
            to = 768 + two * 128
            place(pair * 2, to, jnp.where(low_half, a0, roll(a1, 64)))
            place(pair * 2 + 1, to, jnp.where(low_half, roll(a0, 64), a1))
    out_ref[...] = nt_dot(weights_ref[...], gathered_ref[...]).astype(BF)


def inverse_kernel(assign_ref, place_ref, inverse_ref, out_ref, valid_ref):
    out_ref[...] = nt_dot(inverse_ref[0].astype(BF), regroup().astype(BF)).astype(BF)
    valid = jnp.where(assign_ref[...] <= place_ref[1], 1.0, 0.0)
    row, column = iota((256, 512), 0), iota((256, 512), 1)
    doubled = (row == (column >> 1)).astype(BF)
    valid_ref[...] = jnp.dot(
        jnp.broadcast_to(valid, (8, 256)).astype(BF), doubled, preferred_element_type=F32
    )


def solve_kernel(valid_ref, inverse_ref, right_ref, out_ref):
    solved = nt_dot(inverse_ref[...], right_ref[...]) * 0.5
    out_ref[...] = (solved * valid_ref[0:1, :]).astype(BF)


VMEM = pl.BlockSpec(memory_space=pltpu.VMEM)
SMEM = pl.BlockSpec(memory_space=pltpu.SMEM)


def call(kernel, out, ins, scratch=(), flops=0):
    return pl.pallas_call(
        kernel,
        out_shape=out,
        in_specs=ins,
        out_specs=jax.tree.map(lambda _: VMEM, out),
        scratch_shapes=list(scratch),
        compiler_params=pltpu.CompilerParams(vmem_limit_bytes=24 * 1024 * 1024),
        cost_estimate=pl.CostEstimate(flops=flops, bytes_accessed=2 * 1024 * 1024, transcendentals=0),
    )


def bf16(*shape):
    return jax.ShapeDtypeStruct(shape, BF)


def shards(forcing, legendre, assign, inverse, previous):
    rad, lat = lax.axis_index(RAD), lax.axis_index(LAT)
    orders = assign.reshape(1, 256)
    place = jnp.stack([rad * 4 + lat // 2, lat * 64 + rad]).astype(jnp.int32)

    sent = call(
        fourier_kernel, bf16(512, 1280), [VMEM] * 3, [pltpu.VMEM((512, LON), BF)], 2 * 512 * 768 * 1024
    )(orders, forcing, previous)
    sent, legendre = lax.optimization_barrier((sent, legendre))
    arrived = lax.all_to_all(sent, LAT + RAD, 0, 0, tiled=True)

    by_order = legendre.transpose(0, 2, 1)
    x = lax.axis_index("x")
    pieces = [lax.dynamic_index_in_dim(by_order, x, 0, keepdims=False)]
    for shift in range(1, 4):
        mine = lax.dynamic_index_in_dim(by_order, (x + shift) % 4, 0, keepdims=False)
        pieces.append(lax.ppermute(mine, "x", [(i, (i + shift) % 4) for i in range(4)]))
    stacked = jnp.stack(pieces)
    ordered = jnp.take(stacked, (x - jnp.arange(4)) % 4, axis=0)
    whole = lax.all_gather(ordered, "core", axis=0)
    weights = call(legendre_kernel, bf16(512, 1280), [VMEM, SMEM, VMEM], (), 2 * 512 * 512 * 768)(
        orders, place, whole
    )
    solver, valid = call(
        inverse_kernel,
        (bf16(512, 512), jax.ShapeDtypeStruct((8, 512), F32)),
        [VMEM, SMEM, VMEM],
        (),
        2 * 512**3,
    )(orders, place, inverse)

    right = call(
        spectrum_kernel, bf16(512, 512), [VMEM] * 2, [pltpu.VMEM((512, 1280), BF)], 2 * 512 * 512 * 1280
    )(arrived, weights)
    right = lax.all_to_all(right, RAD + LAT, 0, 0, tiled=True)
    solved = call(solve_kernel, bf16(512, 512), [VMEM] * 3, (), 2 * 512**3)(valid, solver, right)
    out = lax.all_to_all(solved.reshape(64, 8, 512), RAD, 0, 0, tiled=True)
    return out.transpose(1, 0, 2)


def solution(mesh):
    split = Mesh(mesh.devices.reshape(4, 2, 8, 8), LAT + RAD)
    placed = (
        P(RAD, LAT, None),
        P(RAD, None, LAT),
        P(),
        P(LAT + RAD, None, None),
        P(RAD, LAT, None),
    )
    return jax.shard_map(shards, mesh=split, in_specs=placed, out_specs=P(RAD, LAT, None), check_vma=False)
```

time: 246 us -> 136 us (0.55)
  the two profiles are of different devices: /device:TPU:15 before, /device:TPU:8 now
where the time goes in v1:
time: 136 us
  waiting for transfers between devices  44.6 us (33%)
  starting transfers between devices  40.6 us (30%)
  blocking collectives  27.5 us (20%)
  local copies, waits for them, and re-layouts  13.4 us (10%)
  Pallas kernels  6.59 us (5%)
  other arithmetic  3.04 us (2%)
    all_to_all x1, blocking collectives, shards(): out = lax.all_to_all(solved.reshape(64, 8, 512), RAD, 0, 0, tiled=True)  25.1 us
    all_to_all x1, starting transfers between devices, shards(): arrived = lax.all_to_all(sent, LAT + RAD, 0, 0, tiled=True)  21.1 us
    all_to_all x1, waiting for transfers between devices, shards(): right = lax.all_to_all(right, RAD + LAT, 0, 0, tiled=True)  21 us
    all_to_all x1, waiting for transfers between devices, shards(): arrived = lax.all_to_all(sent, LAT + RAD, 0, 0, tiled=True)  15.3 us
    unnamed x18, local copies, waits for them, and re-layouts  11.3 us
    ppermute x3, starting transfers between devices, shards(): lax.ppermute(mine, 'x', [(i, (i + shift) % 4) for i in range(4)])  10.1 us
    all_to_all x1, starting transfers between devices, shards(): right = lax.all_to_all(right, RAD + LAT, 0, 0, tiled=True)  9.33 us
    ppermute x3, waiting for transfers between devices, shards(): lax.ppermute(mine, 'x', [(i, (i + shift) % 4) for i in range(4)])  8.32 us
  transfers between devices with their start and end apart: 5, of which 5 were waited for; matrix products, arithmetic and copies ran while one was open for 1% of the time, Pallas kernels for 2%

profile of v1, /device:TPU:8, one launch (start us, length us, event | category | flops | bytes accessed | tf_op | source)
XLA Modules:
  0.0 135.9 jit_solution(15758046370514771344)
XLA Ops:
  0.0 0.0 copy-start
  0.0 1.4 %copy-done = bf16[8,96,1024]{2,1,0:T(8,128)(2,1)S(1)} copy-done((bf16[8,96,1024]{2,1,0:T(8,128)(2,1)S(1)}, bf16[8,96,1024]{2,1,0:T(8,128)(2,1)}, u32[]{:S(2)}) %copy-start) | copy-done | bytes 1572888
  1.4 0.0 copy-start.2
  1.4 1.0 copy-done.2
  2.5 0.0 copy-start.3
  2.5 0.7 copy-done.3
  3.1 2.1 %shard_map.56 = bf16[512,1280]{1,0:T(8,128)(2,1)S(1)} custom-call(s32[1,256]{1,0:T(1,128)S(1)} %bitcast.39, bf16[8,96,1024]{2,1,0:T(8,128)(2,1)S(1)} %copy-done, bf16[8,64,512]{2,1,0:T(8,128)(2,1)S(1)} %copy-done.2), custom_call_target="tpu_custom_call" | custom-call | flops 805306368 | bytes 2097152 | tf_op jit(solution)/shard_map/pallas_call | solution.py:170
  5.2 0.6 broadcast.119
  5.8 1.7 %reduce = bf16[512,1280]{1,0:T(8,128)(2,1)S(1)} reduce(bf16[512,1,1280]{2,0,1:T(8,128)(2,1)S(1)} %bitcast.34, bf16[]{:T(256)} %broadcast.119), dimensions={1}, to_apply=%copy.10.reduce_sub_computation | reduce | bytes 2621442 | tf_op jit(solution)/shard_map/all_to_all | solution.py:174
  7.5 1.3 reshape.81
  8.7 0.0 copy-start.5
  8.7 21.1 %all-to-all-start = ((bf16[512,2,640]{2,1,0:T(2,128)(2,1)}), bf16[512,2,640]{2,1,0:T(2,128)(2,1)S(1)}, u32[]{:S(2)}, u32[]{:S(2)}) async-start(bf16[512,2,640]{2,1,0:T(2,128)(2,1)} %reshape.81), calls=%async_computation | async-start | bytes 2621440 | tf_op jit(solution)/shard_map/all_to_all | solution.py:174
  29.9 0.0 copy-done.5
  30.0 4.6 %collective-permute-start.2 = (bf16[96,512]{1,0:T(8,128)(2,1)S(1)}, bf16[96,512]{1,0:T(8,128)(2,1)S(1)}, u32[]{:S(2)}, u32[]{:S(2)}) collective-permute-start(bf16[96,512]{1,0:T(8,128)(2,1)S(1)} %get-tuple-element.14), channel_id=1, source_target_pairs={{0,384},{128,0},{256,128},{384,256},{1,385},{129,1},{257,129},{385... | collective-permute-start | bytes 294920 | tf_op jit(solution)/shard_map/ppermute | solution.py:181
  34.6 2.8 %collective-permute-start.1 = (bf16[96,512]{1,0:T(8,128)(2,1)S(1)}, bf16[96,512]{1,0:T(8,128)(2,1)S(1)}, u32[]{:S(2)}, u32[]{:S(2)}) collective-permute-start(bf16[96,512]{1,0:T(8,128)(2,1)S(1)} %get-tuple-element.15), channel_id=1, source_target_pairs={{0,256},{128,384},{256,0},{384,128},{1,257},{129,385},{257,1},{385... | collective-permute-start | bytes 294920 | tf_op jit(solution)/shard_map/ppermute | solution.py:181
  37.3 2.8 %collective-permute-start = (bf16[96,512]{1,0:T(8,128)(2,1)S(1)}, bf16[96,512]{1,0:T(8,128)(2,1)S(1)}, u32[]{:S(2)}, u32[]{:S(2)}) collective-permute-start(bf16[96,512]{1,0:T(8,128)(2,1)S(1)} %get-tuple-element.16), channel_id=1, source_target_pairs={{0,128},{128,256},{256,384},{384,0},{1,129},{129,257},{257,385},{3... | collective-permute-start | bytes 294920 | tf_op jit(solution)/shard_map/ppermute | solution.py:181
  40.2 0.1 pad_add_fusion.place_ref
  40.2 2.8 %collective-permute-done.2 = bf16[96,512]{1,0:T(8,128)(2,1)S(1)} collective-permute-done((bf16[96,512]{1,0:T(8,128)(2,1)S(1)}, bf16[96,512]{1,0:T(8,128)(2,1)S(1)}, u32[]{:S(2)}, u32[]{:S(2)}) %collective-permute-start.2) | collective-permute-done | bytes 98336 | tf_op jit(solution)/shard_map/ppermute | solution.py:181
  43.0 2.4 %collective-permute-done.1 = bf16[96,512]{1,0:T(8,128)(2,1)S(1)} collective-permute-done((bf16[96,512]{1,0:T(8,128)(2,1)S(1)}, bf16[96,512]{1,0:T(8,128)(2,1)S(1)}, u32[]{:S(2)}, u32[]{:S(2)}) %collective-permute-start.1) | collective-permute-done | bytes 98336 | tf_op jit(solution)/shard_map/ppermute | solution.py:181
  45.5 3.1 %collective-permute-done = bf16[96,512]{1,0:T(8,128)(2,1)S(1)} collective-permute-done((bf16[96,512]{1,0:T(8,128)(2,1)S(1)}, bf16[96,512]{1,0:T(8,128)(2,1)S(1)}, u32[]{:S(2)}, u32[]{:S(2)}) %collective-permute-start) | collective-permute-done | bytes 98336 | tf_op jit(solution)/shard_map/ppermute | solution.py:181
  48.6 0.1 pad_maximum_fusion
  48.6 0.0 copy-start.4
  48.6 0.6 gather_fusion
  49.2 0.1 bitcast_select_fusion
  49.3 2.4 %all_gather.4.legendre_ref = bf16[2,4,96,512]{3,2,1,0:T(8,128)(2,1)S(1)} all-gather(bf16[1,4,96,512]{3,2,1,0:T(8,128)(2,1)S(1)} %bitcast_select_fusion), channel_id=1, replica_groups=mesh['x'=4,'core'=2,'z'=8,'y'=8] {'core'}, dimensions={0}, use_global_device_ids=true | all-gather | bytes 1179648 | tf_op jit(solution)/shard_map/all_gather | solution.py:184
  51.7 0.0 copy-done.4
  51.7 1.6 %shard_map.57.weights_ref = bf16[512,1280]{1,0:T(8,128)(2,1)S(1)} custom-call(s32[1,256]{1,0:T(1,128)S(1)} %bitcast.40, s32[2]{0:T(128)S(1)} %pad_add_fusion.place_ref, bf16[2,4,96,512]{3,2,1,0:T(8,128)(2,1)S(1)} %all_gather.4.legendre_ref), custom_call_target="tpu_custom_call" | custom-call | flops 402653184 | bytes 2097152 | tf_op jit(solution)/shard_map/pallas_call | solution.py:185
  53.3 15.3 %all-to-all-done = bf16[512,2,640]{2,1,0:T(2,128)(2,1)S(1)} async-done(((bf16[512,2,640]{2,1,0:T(2,128)(2,1)}), bf16[512,2,640]{2,1,0:T(2,128)(2,1)S(1)}, u32[]{:S(2)}, u32[]{:S(2)}) %all-to-all-start) | async-done | bytes 1310752 | tf_op jit(solution)/shard_map/all_to_all | solution.py:174
  68.6 3.5 %reshape.82 = bf16[512,1,1280]{2,1,0:T(2,128)(2,1)} reshape(bf16[512,2,640]{2,1,0:T(2,128)(2,1)S(1)} %all-to-all-done) | data formatting | bytes 2621440
  72.1 1.9 %copy.17 = bf16[512,1,1280]{2,0,1:T(8,128)(2,1)S(1)} copy(bf16[512,1,1280]{2,1,0:T(2,128)(2,1)} %reshape.82) | data formatting | bytes 2621440
  74.0 1.4 %shard_map.58 = bf16[512,512]{1,0:T(8,128)(2,1)S(1)} custom-call(bf16[512,1280]{1,0:T(8,128)(2,1)S(1)} %bitcast.35, bf16[512,1280]{1,0:T(8,128)(2,1)S(1)} %shard_map.57.weights_ref), custom_call_target="tpu_custom_call" | custom-call | flops 671088640 | bytes 2097152 | tf_op jit(solution)/shard_map/pallas_call | solution.py:196
  75.4 1.1 reduce.1
  76.5 0.0 copy-start.1
  76.5 0.9 reshape.83
  77.4 9.3 %all-to-all-start.1 = ((bf16[512,2,256]{2,1,0:T(2,128)(2,1)}), bf16[512,2,256]{2,1,0:T(2,128)(2,1)S(1)}, u32[]{:S(2)}, u32[]{:S(2)}) async-start(bf16[512,2,256]{2,1,0:T(2,128)(2,1)} %reshape.83), calls=%async_computation.1 | async-start | bytes 1048576 | tf_op jit(solution)/shard_map/all_to_all | solution.py:199
  86.8 0.0 copy-done.1
  86.8 1.0 shard_map.55
  87.8 21.0 %all-to-all-done.1 = bf16[512,2,256]{2,1,0:T(2,128)(2,1)S(1)} async-done(((bf16[512,2,256]{2,1,0:T(2,128)(2,1)}), bf16[512,2,256]{2,1,0:T(2,128)(2,1)S(1)}, u32[]{:S(2)}, u32[]{:S(2)}) %all-to-all-start.1) | async-done | bytes 524320 | tf_op jit(solution)/shard_map/all_to_all | solution.py:199
  108.8 0.4 reshape.84
  109.3 0.1 copy.18
  109.4 0.5 shard_map.59
  109.9 25.1 %all_to_all.27 = bf16[64,8,512]{2,1,0:T(8,128)(2,1)S(1)} all-to-all(bf16[64,8,512]{2,1,0:T(8,128)(2,1)S(1)} %bitcast.37), channel_id=1, replica_groups=mesh['x'=4,'core'=2,'z'=8,'y'=8] {'z','y'}, dimensions={0} | all-to-all | bytes 1048576 | tf_op jit(solution)/shard_map/all_to_all | solution.py:201
  135.0 0.9 copy.12
  (4 shorter events, 0.1 us)
Async XLA Ops:
  0.0 1.4 %copy-start = (bf16[8,96,1024]{2,1,0:T(8,128)(2,1)S(1)}, bf16[8,96,1024]{2,1,0:T(8,128)(2,1)}, u32[]{:S(2)}) copy-start(bf16[8,96,1024]{2,1,0:T(8,128)(2,1)} %forcing_ref.1) | copy-start | bytes 4718596
  1.4 1.0 copy-start.2
  2.5 0.7 copy-start.3
  8.7 21.2 %copy-start.5 = (bf16[4,512,96]{1,2,0:T(8,128)(2,1)S(1)}, bf16[4,512,96]{1,2,0:T(8,128)(2,1)}, u32[]{:S(2)}) copy-start(bf16[4,512,96]{1,2,0:T(8,128)(2,1)} %param.6) | copy-start | bytes 1179652
  8.7 59.8 %all-to-all-start = ((bf16[512,2,640]{2,1,0:T(2,128)(2,1)}), bf16[512,2,640]{2,1,0:T(2,128)(2,1)S(1)}, u32[]{:S(2)}, u32[]{:S(2)}) async-start(bf16[512,2,640]{2,1,0:T(2,128)(2,1)} %reshape.81), calls=%async_computation | async-start | bytes 2621440 | tf_op jit(solution)/shard_map/all_to_all | solution.py:174
  30.0 13.1 %collective-permute-start.2 = (bf16[96,512]{1,0:T(8,128)(2,1)S(1)}, bf16[96,512]{1,0:T(8,128)(2,1)S(1)}, u32[]{:S(2)}, u32[]{:S(2)}) collective-permute-start(bf16[96,512]{1,0:T(8,128)(2,1)S(1)} %get-tuple-element.14), channel_id=1, source_target_pairs={{0,384},{128,0},{256,128},{384,256},{1,385},{129,1},{257,129},{385... | collective-permute-start | bytes 294920 | tf_op jit(solution)/shard_map/ppermute | solution.py:181
  34.6 10.9 %collective-permute-start.1 = (bf16[96,512]{1,0:T(8,128)(2,1)S(1)}, bf16[96,512]{1,0:T(8,128)(2,1)S(1)}, u32[]{:S(2)}, u32[]{:S(2)}) collective-permute-start(bf16[96,512]{1,0:T(8,128)(2,1)S(1)} %get-tuple-element.15), channel_id=1, source_target_pairs={{0,256},{128,384},{256,0},{384,128},{1,257},{129,385},{257,1},{385... | collective-permute-start | bytes 294920 | tf_op jit(solution)/shard_map/ppermute | solution.py:181
  37.3 11.2 %collective-permute-start = (bf16[96,512]{1,0:T(8,128)(2,1)S(1)}, bf16[96,512]{1,0:T(8,128)(2,1)S(1)}, u32[]{:S(2)}, u32[]{:S(2)}) collective-permute-start(bf16[96,512]{1,0:T(8,128)(2,1)S(1)} %get-tuple-element.16), channel_id=1, source_target_pairs={{0,128},{128,256},{256,384},{384,0},{1,129},{129,257},{257,385},{3... | collective-permute-start | bytes 294920 | tf_op jit(solution)/shard_map/ppermute | solution.py:181
  48.6 3.1 %copy-start.4 = (s32[256]{0:T(256)S(1)}, s32[256]{0:T(256)}, u32[]{:S(2)}) copy-start(s32[256]{0:T(256)} %param.7) | copy-start | bytes 3076
  76.5 10.3 %copy-start.1 = (f32[1,512,512]{2,1,0:T(8,128)S(1)}, f32[1,512,512]{2,1,0:T(8,128)}, u32[]{:S(2)}) copy-start(f32[1,512,512]{2,1,0:T(8,128)} %inverse_ref.1) | copy-start | bytes 3145732
  77.4 31.4 %all-to-all-start.1 = ((bf16[512,2,256]{2,1,0:T(2,128)(2,1)}), bf16[512,2,256]{2,1,0:T(2,128)(2,1)S(1)}, u32[]{:S(2)}, u32[]{:S(2)}) async-start(bf16[512,2,256]{2,1,0:T(2,128)(2,1)} %reshape.83), calls=%async_computation.1 | async-start | bytes 1048576 | tf_op jit(solution)/shard_map/all_to_all | solution.py:199

commit v2 on v1

v2 whole, which is shorter than its diff:
```python
import math

import jax
import jax.numpy as jnp
from jax import lax
from jax.experimental import pallas as pl
from jax.experimental.pallas import tpu as pltpu
from jax.sharding import Mesh, PartitionSpec as P

NR = 512
L = 512
LON = 1024
BF = jnp.bfloat16
F32 = jnp.float32
RAD = ("z", "y")
LAT = ("x", "core")


def nt_dot(a, b):
    return lax.dot_general(a, b, (((1,), (1,)), ((), ())), preferred_element_type=F32)


def iota(shape, dim):
    return lax.broadcasted_iota(jnp.int32, shape, dim)


def degree_of(row):
    return ((row >> 6) & 3) * 128 + (row >> 8) * 64 + (row & 63)


def cos_sin(phase):
    quadrant = ((phase + 128) >> 8) & 3
    rest = ((phase + 128) & 255) - 128
    x = rest.astype(F32) * (2.0 * math.pi / LON)
    x2 = x * x
    sin_x = x * (1.0 + x2 * (-1.0 / 6 + x2 * (1.0 / 120 + x2 * (-1.0 / 5040 + x2 * (1.0 / 362880)))))
    cos_x = 1.0 + x2 * (-0.5 + x2 * (1.0 / 24 + x2 * (-1.0 / 720 + x2 * (1.0 / 40320))))
    swap = (quadrant & 1) == 1
    cos_part = jnp.where(swap, sin_x, cos_x)
    sin_part = jnp.where(swap, cos_x, sin_x)
    cos_sign = jnp.where((quadrant == 1) | (quadrant == 2), -1.0, 1.0)
    sin_sign = jnp.where(quadrant >= 2, -1.0, 1.0)
    return cos_part * cos_sign, sin_part * sin_sign


def fourier_kernel(assign_ref, forcing_hbm, previous_hbm, out_ref, forcing_ref, previous_ref, table_ref, sems):
    forcing_copy = pltpu.make_async_copy(forcing_hbm, forcing_ref, sems.at[0])
    previous_copy = pltpu.make_async_copy(previous_hbm, previous_ref, sems.at[1])
    forcing_copy.start()
    previous_copy.start()
    row, lane = iota((512, 256), 0), iota((512, 256), 1)
    mine = lane == ((row >> 1) & 63) * 4 + (row >> 7)
    orders = jnp.sum(jnp.where(mine, assign_ref[...], 0), axis=1, keepdims=True)
    row, lane = iota((512, 128), 0), iota((512, 128), 1)
    cos_low, sin_low = cos_sin((orders * lane + (row & 1) * (LON // 4)) & (LON - 1))
    cos_high, sin_high = cos_sin((orders * 128 * lane) & (LON - 1))
    scale = LON**-0.5
    cos_low, sin_low = cos_low * scale, sin_low * scale
    for q in range(LON // 128):
        turned = cos_low * cos_high[:, q : q + 1] - sin_low * sin_high[:, q : q + 1]
        table_ref[:, q * 128 : q * 128 + 128] = turned.astype(BF)
    table = table_ref[...]
    row, column = iota((512, 512), 0), iota((512, 512), 1)
    reorder = (column == ((row >> 1) & 63) * 8 + (row >> 7) * 2 + (row & 1)).astype(BF)
    previous_copy.wait()
    before = nt_dot(reorder, previous_ref[...].reshape(512, 512)).astype(BF)
    forcing_copy.wait()
    parts = []
    for h in range(3):
        part = forcing_ref[:, h * 32 : h * 32 + 32, :].reshape(256, LON)
        parts.append(nt_dot(table, part).astype(BF))
    for half in range(2):
        pieces = [part[:, half * 128 : half * 128 + 128] for part in parts]
        pieces.append(before[:, half * 256 : half * 256 + 256])
        out_ref[half * 256 : half * 256 + 256] = jnp.concatenate(pieces, axis=1).reshape(256, 2, 640)


def legendre_kernel(assign_ref, place_ref, legendre_ref, out_ref):
    slot = place_ref[0]
    lane = iota((1, 256), 1)
    order = jnp.sum(jnp.where(lane == slot, assign_ref[...], 0), axis=1, keepdims=True)
    row, column = iota((512, 512), 0), iota((512, 512), 1)
    degree = degree_of(row)
    kept = jnp.where((column == degree) & (degree >= order), 1.0, 0.0).astype(BF)
    for h in range(3):
        for core in range(2):
            pieces = [legendre_ref[core, x, h * 32 : h * 32 + 32, :] for x in range(4)]
            at = h * 256 + core * 128
            out_ref[:, at : at + 128] = nt_dot(kept, jnp.concatenate(pieces, axis=0)).astype(BF)
    out_ref[:, 768:1280] = jnp.where(row == column, 2.0, 0.0).astype(BF)


def roll(a, shift):
    return pltpu.roll(a, shift, 1)


def spectrum_kernel(arrived_ref, weights_ref, out_ref, rows_ref, gathered_ref):
    rows_ref[...] = arrived_ref[...].reshape(1024, 640)
    lane = iota((128, 128), 1)
    low_half = lane < 64
    even_quarter = (lane & 32) == 0

    def tile(block, at):
        return rows_ref[block * 128 : block * 128 + 128, at : at + 128].astype(F32)

    def place(rho, at, value):
        gathered_ref[rho * 128 : rho * 128 + 128, at : at + 128] = value.astype(BF)

    for h in range(3):
        for core in range(2):
            a = [tile(core * 4 + x, h * 128) for x in range(4)]
            b0 = jnp.where(low_half, a[0], roll(a[2], 64))
            b2 = jnp.where(low_half, roll(a[0], 64), a[2])
            b1 = jnp.where(low_half, a[1], roll(a[3], 64))
            b3 = jnp.where(low_half, roll(a[1], 64), a[3])
            at = h * 256 + core * 128
            place(0, at, jnp.where(even_quarter, b0, roll(b1, 32)))
            place(1, at, jnp.where(even_quarter, roll(b0, 96), b1))
            place(2, at, jnp.where(even_quarter, b2, roll(b3, 32)))
            place(3, at, jnp.where(even_quarter, roll(b2, 96), b3))
    for pair in range(2):
        for two in range(4):
            at = 384 + pair * 128
            a0, a1 = tile(two * 2, at), tile(two * 2 + 1, at)
            to = 768 + two * 128
            place(pair * 2, to, jnp.where(low_half, a0, roll(a1, 64)))
            place(pair * 2 + 1, to, jnp.where(low_half, roll(a0, 64), a1))
    right = nt_dot(weights_ref[...], gathered_ref[...]).astype(BF)
    out_ref[...] = right.reshape(512, 2, 256)


def inverse_kernel(assign_ref, place_ref, inverse_ref, out_ref, valid_ref):
    inverse = inverse_ref[0].astype(BF)
    row, column = iota((512, 512), 0), iota((512, 512), 1)
    for c in range(2):
        for half in range(2):
            radius = ((row >> 1) & 63) * 8 + half * 4 + (row >> 7)
            spread = ((column == radius) & ((row & 1) == c)).astype(BF)
            out_ref[c * 2 + half] = nt_dot(inverse, spread).astype(BF)
    valid = jnp.where(assign_ref[...] <= place_ref[1], 1.0, 0.0)
    row, column = iota((256, 512), 0), iota((256, 512), 1)
    doubled = (row == (column >> 1)).astype(BF)
    valid_ref[...] = jnp.dot(
        jnp.broadcast_to(valid, (8, 256)).astype(BF), doubled, preferred_element_type=F32
    )


def solve_kernel(valid_ref, inverse_ref, right_ref, out_ref):
    right = right_ref[...].reshape(512, 512)
    parts = []
    for c in range(2):
        solved = nt_dot(inverse_ref[c * 2], right[:256]) + nt_dot(inverse_ref[c * 2 + 1], right[256:])
        parts.append((solved * 0.5).astype(BF))
    row, column = iota((512, 512), 0), iota((512, 512), 1)
    order = (column == (row & 63) * 8 + ((row >> 6) & 3) * 2 + (row >> 8)).astype(BF)
    solved = jnp.dot(jnp.concatenate(parts, axis=1), order, preferred_element_type=F32)
    out_ref[...] = (solved * valid_ref[0:1, :]).astype(BF)


VMEM = pl.BlockSpec(memory_space=pltpu.VMEM)
SMEM = pl.BlockSpec(memory_space=pltpu.SMEM)
HBM = pl.BlockSpec(memory_space=pltpu.HBM)


def call(kernel, out, ins, scratch=(), flops=0, vmem=24):
    return pl.pallas_call(
        kernel,
        out_shape=out,
        in_specs=ins,
        out_specs=jax.tree.map(lambda _: VMEM, out),
        scratch_shapes=list(scratch),
        compiler_params=pltpu.CompilerParams(vmem_limit_bytes=vmem * 1024 * 1024),
        cost_estimate=pl.CostEstimate(flops=flops, bytes_accessed=2 * 1024 * 1024, transcendentals=0),
    )


def bf16(*shape):
    return jax.ShapeDtypeStruct(shape, BF)


def shards(forcing, legendre, assign, inverse, previous):
    rad, lat = lax.axis_index(RAD), lax.axis_index(LAT)
    orders = assign.reshape(1, 256)
    place = jnp.stack([rad * 4 + lat // 2, lat * 64 + rad]).astype(jnp.int32)

    sent = call(
        fourier_kernel,
        bf16(512, 2, 640),
        [VMEM, HBM, HBM],
        [
            pltpu.VMEM((8, 96, LON), BF),
            pltpu.VMEM((8, 64, 512), BF),
            pltpu.VMEM((512, LON), BF),
            pltpu.SemaphoreType.DMA((2,)),
        ],
        2 * 512 * 768 * 1024,
        60,
    )(orders, forcing, previous)
    sent, legendre = lax.optimization_barrier((sent, legendre))
    arrived = lax.all_to_all(sent, ("core", "x") + RAD, 0, 0, tiled=True)

    by_order = legendre.transpose(0, 2, 1)
    x = lax.axis_index("x")
    pieces = [lax.dynamic_index_in_dim(by_order, x, 0, keepdims=False)]
    for shift in range(1, 4):
        mine = lax.dynamic_index_in_dim(by_order, (x + shift) % 4, 0, keepdims=False)
        pieces.append(lax.ppermute(mine, "x", [(i, (i + shift) % 4) for i in range(4)]))
    stacked = jnp.stack(pieces)
    ordered = jnp.take(stacked, (x - jnp.arange(4)) % 4, axis=0)
    whole = lax.all_gather(ordered, "core", axis=0)
    weights = call(legendre_kernel, bf16(512, 1280), [VMEM, SMEM, VMEM], (), 2 * 512 * 512 * 768)(
        orders, place, whole
    )
    solver, valid = call(
        inverse_kernel,
        (bf16(4, 512, 512), jax.ShapeDtypeStruct((8, 512), F32)),
        [VMEM, SMEM, VMEM],
        (),
        2 * 512**3,
    )(orders, place, inverse)

    right = call(
        spectrum_kernel,
        bf16(512, 2, 256),
        [VMEM] * 2,
        [pltpu.VMEM((1024, 640), BF), pltpu.VMEM((512, 1280), BF)],
        2 * 512 * 512 * 1280,
    )(arrived, weights)
    right = lax.all_to_all(right, ("core", "x") + RAD, 0, 0, tiled=True)
    solved = call(solve_kernel, bf16(512, 512), [VMEM] * 3, (), 2 * 512**3)(valid, solver, right)
    out = lax.all_to_all(solved.reshape(64, 8, 512), RAD, 0, 0, tiled=True)
    return out.transpose(1, 0, 2)


def solution(mesh):
    split = Mesh(mesh.devices.reshape(4, 2, 8, 8), LAT + RAD)
    placed = (
        P(RAD, LAT, None),
        P(RAD, None, LAT),
        P(),
        P(LAT + RAD, None, None),
        P(RAD, LAT, None),
    )
    return jax.shard_map(shards, mesh=split, in_specs=placed, out_specs=P(RAD, LAT, None), check_vma=False)
```

time: 136 us -> 127 us (0.934)
  local copies, waits for them, and re-layouts: 13.4 us -> 2.79 us
  Pallas kernels: 6.59 us -> 13.4 us
  other arithmetic: 3.04 us -> 0.27 us
  waiting for transfers between devices: 44.6 us -> 42 us
    unnamed x18 -> x6, local copies, waits for them, and re-layouts: 11.3 us -> 1.23 us
    pallas_call x3, Pallas kernels: 4.53 us -> 10.7 us  [the longest x1 6.15 us: shards(): call(fourier_kernel, bf16(512, 2, 640), [VMEM, HBM, HBM], [pltpu.VMEM((8,...]
    all_to_all x2 -> x0, other arithmetic: 2.77 us -> none  [the longest x1 1.7 us: shards(): arrived = lax.all_to_all(sent, LAT + RAD, 0, 0, tiled=True)]
    all_to_all x2, waiting for transfers between devices: 36.2 us -> 33.6 us  [the longest x1 18.7 us: shards(): right = lax.all_to_all(right, ('core', 'x') + RAD, 0, 0, tiled=True)]
  transfers between devices with their start and end apart: 5 -> 5, of which waited for: 5 -> 5; matrix products, arithmetic and copies ran while one was open for 1% -> 1% of each run, Pallas kernels for 2% -> 3%
where the time goes in v2:
time: 127 us
  waiting for transfers between devices  42 us (33%)
  starting transfers between devices  40.7 us (32%)
  blocking collectives  27.6 us (22%)
  Pallas kernels  13.4 us (11%)
  local copies, waits for them, and re-layouts  2.79 us (2%)
    all_to_all x1, blocking collectives, shards(): out = lax.all_to_all(solved.reshape(64, 8, 512), RAD, 0, 0, tiled=True)  25.3 us
    all_to_all x1, starting transfers between devices, shards(): arrived = lax.all_to_all(sent, ('core', 'x') + RAD, 0, 0, tiled=True)  21.1 us
    all_to_all x1, waiting for transfers between devices, shards(): right = lax.all_to_all(right, ('core', 'x') + RAD, 0, 0, tiled=True)  18.7 us
    all_to_all x1, waiting for transfers between devices, shards(): arrived = lax.all_to_all(sent, ('core', 'x') + RAD, 0, 0, tiled=True)  14.9 us
    ppermute x3, starting transfers between devices, shards(): lax.ppermute(mine, 'x', [(i, (i + shift) % 4) for i in range(4)])  10.1 us
    all_to_all x1, starting transfers between devices, shards(): right = lax.all_to_all(right, ('core', 'x') + RAD, 0, 0, tiled=True)  9.44 us
    ppermute x3, waiting for transfers between devices, shards(): lax.ppermute(mine, 'x', [(i, (i + shift) % 4) for i in range(4)])  8.42 us
    pallas_call x1, Pallas kernels, shards(): call(fourier_kernel, bf16(512, 2, 640), [VMEM, HBM, HBM], [pltpu.VMEM((8,...  6.15 us
  transfers between devices with their start and end apart: 5, of which 5 were waited for; matrix products, arithmetic and copies ran while one was open for 1% of the time, Pallas kernels for 3%

profile of v2, /device:TPU:8, one launch (start us, length us, event | category | flops | bytes accessed | tf_op | source)
XLA Modules:
  0.0 126.9 jit_solution(11461384020937121169)
XLA Ops:
  0.0 6.2 %shard_map.56 = bf16[512,2,640]{2,1,0:T(2,128)(2,1)} custom-call(s32[1,256]{1,0:T(1,128)} %bitcast.27, bf16[8,96,1024]{2,1,0:T(8,128)(2,1)} %forcing_hbm.1, bf16[8,64,512]{2,1,0:T(8,128)(2,1)} %previous_hbm.1), custom_call_target="tpu_custom_call" | custom-call | flops 805306368 | bytes 2097152 | tf_op jit(solution)/shard_map/pallas_call | solution.py:186
  6.2 0.0 copy-start.2
  6.2 21.1 %all-to-all-start = ((bf16[512,2,640]{2,1,0:T(2,128)(2,1)}), bf16[512,2,640]{2,1,0:T(2,128)(2,1)S(1)}, u32[]{:S(2)}, u32[]{:S(2)}) async-start(bf16[512,2,640]{2,1,0:T(2,128)(2,1)} %shard_map.56), calls=%async_computation | async-start | bytes 2621440 | tf_op jit(solution)/shard_map/all_to_all | solution.py:200
  27.3 0.0 copy-done.2
  27.4 4.6 %collective-permute-start.2 = (bf16[96,512]{1,0:T(8,128)(2,1)S(1)}, bf16[96,512]{1,0:T(8,128)(2,1)S(1)}, u32[]{:S(2)}, u32[]{:S(2)}) collective-permute-start(bf16[96,512]{1,0:T(8,128)(2,1)S(1)} %get-tuple-element.14), channel_id=1, source_target_pairs={{0,384},{128,0},{256,128},{384,256},{1,385},{129,1},{257,129},{385... | collective-permute-start | bytes 294920 | tf_op jit(solution)/shard_map/ppermute | solution.py:207
  32.0 2.8 %collective-permute-start.1 = (bf16[96,512]{1,0:T(8,128)(2,1)S(1)}, bf16[96,512]{1,0:T(8,128)(2,1)S(1)}, u32[]{:S(2)}, u32[]{:S(2)}) collective-permute-start(bf16[96,512]{1,0:T(8,128)(2,1)S(1)} %get-tuple-element.15), channel_id=1, source_target_pairs={{0,256},{128,384},{256,0},{384,128},{1,257},{129,385},{257,1},{385... | collective-permute-start | bytes 294920 | tf_op jit(solution)/shard_map/ppermute | solution.py:207
  34.8 2.8 %collective-permute-start = (bf16[96,512]{1,0:T(8,128)(2,1)S(1)}, bf16[96,512]{1,0:T(8,128)(2,1)S(1)}, u32[]{:S(2)}, u32[]{:S(2)}) collective-permute-start(bf16[96,512]{1,0:T(8,128)(2,1)S(1)} %get-tuple-element.16), channel_id=1, source_target_pairs={{0,128},{128,256},{256,384},{384,0},{1,129},{129,257},{257,385},{3... | collective-permute-start | bytes 294920 | tf_op jit(solution)/shard_map/ppermute | solution.py:207
  37.6 0.1 pad_add_fusion.place_ref
  37.7 2.8 %collective-permute-done.2 = bf16[96,512]{1,0:T(8,128)(2,1)S(1)} collective-permute-done((bf16[96,512]{1,0:T(8,128)(2,1)S(1)}, bf16[96,512]{1,0:T(8,128)(2,1)S(1)}, u32[]{:S(2)}, u32[]{:S(2)}) %collective-permute-start.2) | collective-permute-done | bytes 98336 | tf_op jit(solution)/shard_map/ppermute | solution.py:207
  40.5 2.9 %collective-permute-done.1 = bf16[96,512]{1,0:T(8,128)(2,1)S(1)} collective-permute-done((bf16[96,512]{1,0:T(8,128)(2,1)S(1)}, bf16[96,512]{1,0:T(8,128)(2,1)S(1)}, u32[]{:S(2)}, u32[]{:S(2)}) %collective-permute-start.1) | collective-permute-done | bytes 98336 | tf_op jit(solution)/shard_map/ppermute | solution.py:207
  43.4 2.7 %collective-permute-done = bf16[96,512]{1,0:T(8,128)(2,1)S(1)} collective-permute-done((bf16[96,512]{1,0:T(8,128)(2,1)S(1)}, bf16[96,512]{1,0:T(8,128)(2,1)S(1)}, u32[]{:S(2)}, u32[]{:S(2)}) %collective-permute-start) | collective-permute-done | bytes 98336 | tf_op jit(solution)/shard_map/ppermute | solution.py:207
  46.1 0.1 pad_maximum_fusion
  46.2 0.0 copy-start.1
  46.2 0.6 gather_fusion
  46.8 0.1 bitcast_select_fusion
  46.9 2.4 %all_gather.4.legendre_ref = bf16[2,4,96,512]{3,2,1,0:T(8,128)(2,1)S(1)} all-gather(bf16[1,4,96,512]{3,2,1,0:T(8,128)(2,1)S(1)} %bitcast_select_fusion), channel_id=1, replica_groups=mesh['x'=4,'core'=2,'z'=8,'y'=8] {'core'}, dimensions={0}, use_global_device_ids=true | all-gather | bytes 1179648 | tf_op jit(solution)/shard_map/all_gather | solution.py:210
  49.2 0.0 copy-done.1
  49.2 1.6 %shard_map.57.weights_ref = bf16[512,1280]{1,0:T(8,128)(2,1)S(1)} custom-call(s32[1,256]{1,0:T(1,128)S(1)} %bitcast.28, s32[2]{0:T(128)S(1)} %pad_add_fusion.place_ref, bf16[2,4,96,512]{3,2,1,0:T(8,128)(2,1)S(1)} %all_gather.4.legendre_ref), custom_call_target="tpu_custom_call" | custom-call | flops 402653184 | bytes 2097152 | tf_op jit(solution)/shard_map/pallas_call | solution.py:211
  50.9 14.9 %all-to-all-done.arrived_ref = bf16[512,2,640]{2,1,0:T(2,128)(2,1)S(1)} async-done(((bf16[512,2,640]{2,1,0:T(2,128)(2,1)}), bf16[512,2,640]{2,1,0:T(2,128)(2,1)S(1)}, u32[]{:S(2)}, u32[]{:S(2)}) %all-to-all-start) | async-done | bytes 1310752 | tf_op jit(solution)/shard_map/all_to_all | solution.py:200
  65.7 2.6 %shard_map.58 = bf16[512,2,256]{2,1,0:T(2,128)(2,1)} custom-call(bf16[512,2,640]{2,1,0:T(2,128)(2,1)S(1)} %all-to-all-done.arrived_ref, bf16[512,1280]{1,0:T(8,128)(2,1)S(1)} %shard_map.57.weights_ref), custom_call_target="tpu_custom_call" | custom-call | flops 671088640 | bytes 2097152 | tf_op jit(solution)/shard_map/pallas_call | solution.py:222
  68.3 9.4 %all-to-all-start.1 = ((bf16[512,2,256]{2,1,0:T(2,128)(2,1)}), bf16[512,2,256]{2,1,0:T(2,128)(2,1)S(1)}, u32[]{:S(2)}, u32[]{:S(2)}) async-start(bf16[512,2,256]{2,1,0:T(2,128)(2,1)} %shard_map.58), calls=%async_computation.1 | async-start | bytes 1048576 | tf_op jit(solution)/shard_map/all_to_all | solution.py:229
  77.8 0.0 copy-start
  77.8 1.2 copy-done
  79.0 1.9 %shard_map.55 = (bf16[4,512,512]{2,1,0:T(8,128)(2,1)S(1)}, f32[8,512]{1,0:T(8,128)S(1)}) custom-call(s32[1,256]{1,0:T(1,128)S(1)} %bitcast.29, s32[2]{0:T(128)S(1)} %pad_add_fusion.place_ref, f32[1,512,512]{2,1,0:T(8,128)S(1)} %copy-done), custom_call_target="tpu_custom_call" | custom-call | flops 268435456 | bytes 2097152 | tf_op jit(solution)/shard_map/pallas_call | solution.py:214
  80.9 18.7 %all-to-all-done.1.right_ref = bf16[512,2,256]{2,1,0:T(2,128)(2,1)S(1)} async-done(((bf16[512,2,256]{2,1,0:T(2,128)(2,1)}), bf16[512,2,256]{2,1,0:T(2,128)(2,1)S(1)}, u32[]{:S(2)}, u32[]{:S(2)}) %all-to-all-start.1) | async-done | bytes 524320 | tf_op jit(solution)/shard_map/all_to_all | solution.py:229
  99.6 1.1 shard_map.59
  100.7 25.3 %all_to_all.15 = bf16[64,8,512]{2,1,0:T(8,128)(2,1)S(1)} all-to-all(bf16[64,8,512]{2,1,0:T(8,128)(2,1)S(1)} %bitcast.26), channel_id=1, replica_groups=mesh['x'=4,'core'=2,'z'=8,'y'=8] {'z','y'}, dimensions={0} | all-to-all | bytes 1048576 | tf_op jit(solution)/shard_map/all_to_all | solution.py:231
  126.0 0.9 copy.7
  (4 shorter events, 0.1 us)
Async XLA Ops:
  6.2 21.2 %copy-start.2 = (bf16[4,512,96]{1,2,0:T(8,128)(2,1)S(1)}, bf16[4,512,96]{1,2,0:T(8,128)(2,1)}, u32[]{:S(2)}) copy-start(bf16[4,512,96]{1,2,0:T(8,128)(2,1)} %param.6) | copy-start | bytes 1179652
  6.2 59.5 %all-to-all-start = ((bf16[512,2,640]{2,1,0:T(2,128)(2,1)}), bf16[512,2,640]{2,1,0:T(2,128)(2,1)S(1)}, u32[]{:S(2)}, u32[]{:S(2)}) async-start(bf16[512,2,640]{2,1,0:T(2,128)(2,1)} %shard_map.56), calls=%async_computation | async-start | bytes 2621440 | tf_op jit(solution)/shard_map/all_to_all | solution.py:200
  27.4 13.1 %collective-permute-start.2 = (bf16[96,512]{1,0:T(8,128)(2,1)S(1)}, bf16[96,512]{1,0:T(8,128)(2,1)S(1)}, u32[]{:S(2)}, u32[]{:S(2)}) collective-permute-start(bf16[96,512]{1,0:T(8,128)(2,1)S(1)} %get-tuple-element.14), channel_id=1, source_target_pairs={{0,384},{128,0},{256,128},{384,256},{1,385},{129,1},{257,129},{385... | collective-permute-start | bytes 294920 | tf_op jit(solution)/shard_map/ppermute | solution.py:207
  32.0 11.4 %collective-permute-start.1 = (bf16[96,512]{1,0:T(8,128)(2,1)S(1)}, bf16[96,512]{1,0:T(8,128)(2,1)S(1)}, u32[]{:S(2)}, u32[]{:S(2)}) collective-permute-start(bf16[96,512]{1,0:T(8,128)(2,1)S(1)} %get-tuple-element.15), channel_id=1, source_target_pairs={{0,256},{128,384},{256,0},{384,128},{1,257},{129,385},{257,1},{385... | collective-permute-start | bytes 294920 | tf_op jit(solution)/shard_map/ppermute | solution.py:207
  34.8 11.3 %collective-permute-start = (bf16[96,512]{1,0:T(8,128)(2,1)S(1)}, bf16[96,512]{1,0:T(8,128)(2,1)S(1)}, u32[]{:S(2)}, u32[]{:S(2)}) collective-permute-start(bf16[96,512]{1,0:T(8,128)(2,1)S(1)} %get-tuple-element.16), channel_id=1, source_target_pairs={{0,128},{128,256},{256,384},{384,0},{1,129},{129,257},{257,385},{3... | collective-permute-start | bytes 294920 | tf_op jit(solution)/shard_map/ppermute | solution.py:207
  46.2 3.1 %copy-start.1 = (s32[256]{0:T(256)S(1)}, s32[256]{0:T(256)}, u32[]{:S(2)}) copy-start(s32[256]{0:T(256)} %param.7) | copy-start | bytes 3076
  68.3 31.3 %all-to-all-start.1 = ((bf16[512,2,256]{2,1,0:T(2,128)(2,1)}), bf16[512,2,256]{2,1,0:T(2,128)(2,1)S(1)}, u32[]{:S(2)}, u32[]{:S(2)}) async-start(bf16[512,2,256]{2,1,0:T(2,128)(2,1)} %shard_map.58), calls=%async_computation.1 | async-start | bytes 1048576 | tf_op jit(solution)/shard_map/all_to_all | solution.py:229
  77.8 1.2 copy-start

commit v3 on v1

v3 whole, which is shorter than its diff:
```python
import math

import jax
import jax.numpy as jnp
from jax import lax
from jax.experimental import pallas as pl
from jax.experimental.pallas import tpu as pltpu
from jax.sharding import Mesh, PartitionSpec as P

NR = 512
L = 512
LON = 1024
BF = jnp.bfloat16
F32 = jnp.float32
RAD = ("zh", "zl", "y")
LAT = ("x", "core")


def nt_dot(a, b):
    return lax.dot_general(a, b, (((1,), (1,)), ((), ())), preferred_element_type=F32)


def iota(shape, dim):
    return lax.broadcasted_iota(jnp.int32, shape, dim)


def cos_sin(phase):
    quadrant = ((phase + 128) >> 8) & 3
    rest = ((phase + 128) & 255) - 128
    x = rest.astype(F32) * (2.0 * math.pi / LON)
    x2 = x * x
    sin_x = x * (1.0 + x2 * (-1.0 / 6 + x2 * (1.0 / 120 + x2 * (-1.0 / 5040 + x2 * (1.0 / 362880)))))
    cos_x = 1.0 + x2 * (-0.5 + x2 * (1.0 / 24 + x2 * (-1.0 / 720 + x2 * (1.0 / 40320))))
    swap = (quadrant & 1) == 1
    cos_part = jnp.where(swap, sin_x, cos_x)
    sin_part = jnp.where(swap, cos_x, sin_x)
    cos_sign = jnp.where((quadrant == 1) | (quadrant == 2), -1.0, 1.0)
    sin_sign = jnp.where(quadrant >= 2, -1.0, 1.0)
    return cos_part * cos_sign, sin_part * sin_sign


def fourier_kernel(
    assign_ref, forcing_hbm, previous_hbm, out_hbm, forcing_ref, previous_ref, table_ref, out_ref, in_sems, out_sems
):
    previous_copy = pltpu.make_async_copy(previous_hbm, previous_ref, in_sems.at[3])
    previous_copy.start()
    forcing_copies = []
    for h in range(3):
        part = pl.ds(h * 32, 32)
        copy = pltpu.make_async_copy(forcing_hbm.at[:, part, :], forcing_ref.at[:, part, :], in_sems.at[h])
        copy.start()
        forcing_copies.append(copy)
    row = iota((512, 1), 0)
    slot = ((row >> 4) & 3) * 64 + (row >> 8) * 32 + ((row >> 1) & 7) * 4 + ((row >> 6) & 3)
    orders = jnp.sum(jnp.where(iota((512, 256), 1) == slot, assign_ref[...], 0), axis=1, keepdims=True)
    lane = iota((512, 128), 1)
    cos_low, sin_low = cos_sin((orders * lane + (row & 1) * (LON // 4)) & (LON - 1))
    cos_high, sin_high = cos_sin((orders * 128 * lane) & (LON - 1))
    scale = LON**-0.5
    cos_low, sin_low = cos_low * scale, sin_low * scale
    for q in range(LON // 128):
        turned = cos_low * cos_high[:, q : q + 1] - sin_low * sin_high[:, q : q + 1]
        table_ref[:, q * 128 : q * 128 + 128] = turned.astype(BF)
    table = table_ref[...]
    reorder = (iota((512, 512), 1) == slot * 2 + (row & 1)).astype(BF)
    out_copies = []

    def send(at, width, value):
        out_ref[:, :, at : at + width] = value.astype(BF).reshape(256, 2, width)
        part = pl.ds(at, width)
        copy = pltpu.make_async_copy(out_ref.at[:, :, part], out_hbm.at[:, :, part], out_sems.at[len(out_copies)])
        copy.start()
        out_copies.append(copy)

    previous_copy.wait()
    send(768, 512, nt_dot(reorder, previous_ref[...].reshape(512, 512)))
    for h in range(3):
        forcing_copies[h].wait()
        part = forcing_ref[:, h * 32 : h * 32 + 32, :].reshape(256, LON)
        send(h * 256, 256, nt_dot(table, part))
    for copy in out_copies:
        copy.wait()


def legendre_kernel(assign_ref, place_ref, legendre_ref, out_ref, parted_ref):
    order = jnp.sum(jnp.where(iota((1, 256), 1) == place_ref[0], assign_ref[...], 0), axis=1, keepdims=True)
    row = iota((512, 1), 0)
    core, x = (row >> 5) & 1, row & 3
    inner = ((row >> 6) & 3) * 16 + (row >> 8) * 8 + ((row >> 2) & 7)
    degree = (2 * x + core) * 64 + inner
    column = iota((512, 512), 1)
    kept = jnp.where((column == degree) & (degree >= order), 1.0, 0.0).astype(BF)
    for h in range(3):
        for core_from in range(2):
            pieces = [legendre_ref[core_from, x_from, h * 32 : h * 32 + 32, :] for x_from in range(4)]
            at = h * 256 + core_from * 128
            out_ref[:, at : at + 128] = nt_dot(kept, jnp.concatenate(pieces, axis=0)).astype(BF)
    out_ref[:, 768:1280] = jnp.where(column == core * 256 + x * 64 + inner, 2.0, 0.0).astype(BF)
    parted_ref[...] = (column == (row & 1) * 256 + (row >> 1)).astype(BF)


def roll(a, shift):
    return pltpu.roll(a, shift, 1)


def spectrum_kernel(arrived_ref, weights_ref, parted_ref, out_ref, gathered_ref):
    lane = iota((64, 128), 1)
    low_half = lane < 64
    even_quarter = (lane & 32) == 0

    def tile(block, at):
        return arrived_ref[block * 32 : block * 32 + 32, :, at : at + 128].reshape(64, 128).astype(F32)

    def place(rho, at, value):
        gathered_ref[rho * 64 : rho * 64 + 64, at : at + 128] = value.astype(BF)

    for h in range(3):
        for high in range(2):
            for core in range(2):
                a = [tile(core * 4 + x, h * 256 + high * 128) for x in range(4)]
                b0 = jnp.where(low_half, a[0], roll(a[2], 64))
                b2 = jnp.where(low_half, roll(a[0], 64), a[2])
                b1 = jnp.where(low_half, a[1], roll(a[3], 64))
                b3 = jnp.where(low_half, roll(a[1], 64), a[3])
                at, rho = h * 256 + core * 128, high * 4
                place(rho, at, jnp.where(even_quarter, b0, roll(b1, 32)))
                place(rho + 1, at, jnp.where(even_quarter, roll(b0, 96), b1))
                place(rho + 2, at, jnp.where(even_quarter, b2, roll(b3, 32)))
                place(rho + 3, at, jnp.where(even_quarter, roll(b2, 96), b3))
    for pair in range(4):
        for two in range(4):
            at = 768 + pair * 128
            a0, a1 = tile(two * 2, at), tile(two * 2 + 1, at)
            to = 768 + two * 128
            place(pair * 2, to, jnp.where(low_half, a0, roll(a1, 64)))
            place(pair * 2 + 1, to, jnp.where(low_half, roll(a0, 64), a1))
    right = nt_dot(weights_ref[...], gathered_ref[...]).astype(BF)
    right = jnp.dot(right, parted_ref[...], preferred_element_type=F32).astype(BF)
    out_ref[...] = right.reshape(512, 2, 256)


def inverse_kernel(assign_ref, place_ref, inverse_ref, out_ref, valid_ref):
    inverse = inverse_ref[0].astype(BF)
    row, column = iota((256, 512), 0), iota((256, 512), 1)
    for zl in range(2):
        radius = ((row >> 3) & 3) * 128 + zl * 64 + (row & 7) * 8 + (row >> 5)
        out_ref[zl] = nt_dot(inverse, (column == radius).astype(BF)).astype(BF)
    valid = jnp.where(assign_ref[...] <= place_ref[1], 1.0, 0.0)
    doubled = (row == (column >> 1)).astype(BF)
    valid_ref[...] = jnp.dot(
        jnp.broadcast_to(valid, (8, 256)).astype(BF), doubled, preferred_element_type=F32
    )


def solve_kernel(valid_ref, inverse_ref, right_ref, out_ref):
    right = right_ref[...].reshape(1024, 256)
    solved = nt_dot(inverse_ref[0], right[:512]) + nt_dot(inverse_ref[1], right[512:])
    out_ref[...] = (solved * (valid_ref[0:1, :] * 0.5)).astype(BF)


VMEM = pl.BlockSpec(memory_space=pltpu.VMEM)
SMEM = pl.BlockSpec(memory_space=pltpu.SMEM)
HBM = pl.BlockSpec(memory_space=pltpu.HBM)


def call(kernel, out, ins, scratch=(), flops=0, vmem=24, outs=None):
    return pl.pallas_call(
        kernel,
        out_shape=out,
        in_specs=ins,
        out_specs=outs or jax.tree.map(lambda _: VMEM, out),
        scratch_shapes=list(scratch),
        compiler_params=pltpu.CompilerParams(vmem_limit_bytes=vmem * 1024 * 1024),
        cost_estimate=pl.CostEstimate(flops=flops, bytes_accessed=2 * 1024 * 1024, transcendentals=0),
    )


def bf16(*shape):
    return jax.ShapeDtypeStruct(shape, BF)


def shards(forcing, legendre, assign, inverse, previous):
    x, core = lax.axis_index("x"), lax.axis_index("core")
    zh, zl, y = lax.axis_index("zh"), lax.axis_index("zl"), lax.axis_index("y")
    orders = assign.reshape(1, 256)
    slot = zh * 64 + core * 32 + y * 4 + x
    degree = (x * 2 + core) * 64 + zh * 16 + zl * 8 + y
    place = jnp.stack([slot, degree]).astype(jnp.int32)

    sent = call(
        fourier_kernel,
        bf16(256, 2, 1280),
        [VMEM, HBM, HBM],
        [
            pltpu.VMEM((8, 96, LON), BF),
            pltpu.VMEM((8, 64, 512), BF),
            pltpu.VMEM((512, LON), BF),
            pltpu.VMEM((256, 2, 1280), BF),
            pltpu.SemaphoreType.DMA((4,)),
            pltpu.SemaphoreType.DMA((4,)),
        ],
        2 * 512 * 768 * 1024,
        60,
        HBM,
    )(orders, forcing, previous)
    sent, legendre = lax.optimization_barrier((sent, legendre))
    arrived = lax.all_to_all(sent, ("core", "x", "zh", "y"), 0, 0, tiled=True)

    by_order = legendre.transpose(0, 2, 1)
    pieces = [lax.dynamic_index_in_dim(by_order, x, 0, keepdims=False)]
    for shift in range(1, 4):
        mine = lax.dynamic_index_in_dim(by_order, (x + shift) % 4, 0, keepdims=False)
        pieces.append(lax.ppermute(mine, "x", [(i, (i + shift) % 4) for i in range(4)]))
    stacked = jnp.stack(pieces)
    ordered = jnp.take(stacked, (x - jnp.arange(4)) % 4, axis=0)
    whole = lax.all_gather(ordered, "core", axis=0)
    other = lax.ppermute(whole, ("core", "zl"), [(0, 1), (3, 2)])
    whole = jnp.where(core == zl, whole, other)
    weights, parted = call(
        legendre_kernel, (bf16(512, 1280), bf16(512, 512)), [VMEM, SMEM, VMEM], (), 2 * 512 * 512 * 768
    )(orders, place, whole)
    solver, valid = call(
        inverse_kernel,
        (bf16(2, 512, 256), jax.ShapeDtypeStruct((8, 512), F32)),
        [VMEM, SMEM, VMEM],
        (),
        2 * 512**3,
    )(orders, place, inverse)

    right = call(
        spectrum_kernel,
        bf16(512, 2, 256),
        [VMEM] * 3,
        [pltpu.VMEM((512, 1280), BF)],
        2 * 512 * 512 * 1792,
    )(arrived, weights, parted)
    right = lax.all_to_all(right, ("zl", "zh", "core", "y", "x"), 0, 0, tiled=True)
    solved = call(solve_kernel, bf16(512, 512), [VMEM] * 3, (), 2 * 512**3)(valid, solver, right)
    out = lax.all_to_all(solved.reshape(64, 8, 512), RAD, 0, 0, tiled=True)
    return out.transpose(1, 0, 2)


def solution(mesh):
    split = Mesh(mesh.devices.reshape(4, 2, 4, 2, 8), LAT + RAD)
    placed = (
        P(RAD, LAT, None),
        P(RAD, None, LAT),
        P(),
        P(LAT + RAD, None, None),
        P(RAD, LAT, None),
    )
    return jax.shard_map(shards, mesh=split, in_specs=placed, out_specs=P(RAD, LAT, None), check_vma=False)
```

time: 136 us -> 137 us (level)
  starting transfers between devices: 40.6 us -> 52 us
  local copies, waits for them, and re-layouts: 13.4 us -> 2.79 us
  Pallas kernels: 6.59 us -> 13.1 us
  waiting for transfers between devices: 44.6 us -> 38.8 us
  other arithmetic: 3.04 us -> 0.35 us
    all_to_all x2, waiting for transfers between devices: 36.2 us -> 18.4 us  [the longest x1 18.4 us: shards(): lax.all_to_all(right, ('zl', 'zh', 'core', 'y', 'x'), 0, 0, tiled=True)]
    ppermute x0 -> x1, waiting for transfers between devices: none -> 11.8 us  [shards(): other = lax.ppermute(whole, ('core', 'zl'), [(0, 1), (3, 2)])]
    unnamed x18 -> x6, local copies, waits for them, and re-layouts: 11.3 us -> 1.23 us
    all_to_all x2, starting transfers between devices: 30.4 us -> 37.1 us  [the longest x1 21.5 us: shards(): arrived = lax.all_to_all(sent, ('core', 'x', 'zh', 'y'), 0, 0, tiled=True)]
    pallas_call x4, Pallas kernels: 6.12 us -> 12.6 us  [the longest x1 6.67 us: shards(): call(fourier_kernel, bf16(256, 2, 1280), [VMEM, HBM, HBM], [pltpu.VMEM((8...]
    ppermute x0 -> x1, starting transfers between devices: none -> 3.93 us  [shards(): other = lax.ppermute(whole, ('core', 'zl'), [(0, 1), (3, 2)])]
    all_to_all x2 -> x0, other arithmetic: 2.77 us -> none  [the longest x1 1.7 us: shards(): arrived = lax.all_to_all(sent, LAT + RAD, 0, 0, tiled=True)]
  transfers between devices with their start and end apart: 5 -> 6, of which waited for: 5 -> 3; matrix products, arithmetic and copies ran while one was open for 1% -> 1% of each run, Pallas kernels for 2% -> 2%
where the time goes in v3:
time: 137 us; the launch traced here: 136 us
  starting transfers between devices  52 us (38%)
  waiting for transfers between devices  38.8 us (28%)
  blocking collectives  28.8 us (21%)
  Pallas kernels  13.1 us (10%)
  local copies, waits for them, and re-layouts  2.79 us (2%)
    all_to_all x1, blocking collectives, shards(): out = lax.all_to_all(solved.reshape(64, 8, 512), RAD, 0, 0, tiled=True)  26.4 us
    all_to_all x1, starting transfers between devices, shards(): arrived = lax.all_to_all(sent, ('core', 'x', 'zh', 'y'), 0, 0, tiled=True)  21.5 us
    all_to_all x1, waiting for transfers between devices, shards(): lax.all_to_all(right, ('zl', 'zh', 'core', 'y', 'x'), 0, 0, tiled=True)  18.4 us
    all_to_all x1, starting transfers between devices, shards(): lax.all_to_all(right, ('zl', 'zh', 'core', 'y', 'x'), 0, 0, tiled=True)  15.6 us
    ppermute x1, waiting for transfers between devices, shards(): other = lax.ppermute(whole, ('core', 'zl'), [(0, 1), (3, 2)])  11.8 us
    ppermute x3, starting transfers between devices, shards(): lax.ppermute(mine, 'x', [(i, (i + shift) % 4) for i in range(4)])  11 us
    ppermute x3, waiting for transfers between devices, shards(): lax.ppermute(mine, 'x', [(i, (i + shift) % 4) for i in range(4)])  8.68 us
    pallas_call x1, Pallas kernels, shards(): call(fourier_kernel, bf16(256, 2, 1280), [VMEM, HBM, HBM], [pltpu.VMEM((8...  6.67 us
  transfers between devices with their start and end apart: 6, of which 3 were waited for; matrix products, arithmetic and copies ran while one was open for 1% of the time, Pallas kernels for 2%

profile of v3, /device:TPU:8, one launch (start us, length us, event | category | flops | bytes accessed | tf_op | source)
XLA Modules:
  0.0 136.2 jit_solution(14896460150433605290)
XLA Ops:
  0.0 6.7 %shard_map.56 = bf16[256,2,1280]{2,1,0:T(2,128)(2,1)} custom-call(s32[1,256]{1,0:T(1,128)} %bitcast.27, bf16[8,96,1024]{2,1,0:T(8,128)(2,1)} %forcing_hbm.1, bf16[8,64,512]{2,1,0:T(8,128)(2,1)} %previous_hbm.1), custom_call_target="tpu_custom_call" | custom-call | flops 805306368 | bytes 2097152 | tf_op jit(solution)/shard_map/pallas_call | solution.py:190
  6.7 0.0 copy-start.2
  6.7 21.5 %all-to-all-start = ((bf16[256,2,1280]{2,1,0:T(2,128)(2,1)}), bf16[256,2,1280]{2,1,0:T(2,128)(2,1)S(1)}, u32[]{:S(2)}, u32[]{:S(2)}) async-start(bf16[256,2,1280]{2,1,0:T(2,128)(2,1)} %shard_map.56), calls=%async_computation | async-start | bytes 2621440 | tf_op jit(solution)/shard_map/all_to_all | solution.py:207
  28.2 0.0 copy-done.2
  28.3 5.1 %collective-permute-start.2 = (bf16[96,512]{1,0:T(8,128)(2,1)S(1)}, bf16[96,512]{1,0:T(8,128)(2,1)S(1)}, u32[]{:S(2)}, u32[]{:S(2)}) collective-permute-start(bf16[96,512]{1,0:T(8,128)(2,1)S(1)} %get-tuple-element.18), channel_id=1, source_target_pairs={{0,384},{128,0},{256,128},{384,256},{1,385},{129,1},{257,129},{385... | collective-permute-start | bytes 294920 | tf_op jit(solution)/shard_map/ppermute | solution.py:213
  33.4 1.9 %collective-permute-start = (bf16[96,512]{1,0:T(8,128)(2,1)S(1)}, bf16[96,512]{1,0:T(8,128)(2,1)S(1)}, u32[]{:S(2)}, u32[]{:S(2)}) collective-permute-start(bf16[96,512]{1,0:T(8,128)(2,1)S(1)} %get-tuple-element.20), channel_id=1, source_target_pairs={{0,128},{128,256},{256,384},{384,0},{1,129},{129,257},{257,385},{3... | collective-permute-start | bytes 294920 | tf_op jit(solution)/shard_map/ppermute | solution.py:213
  35.3 4.0 %collective-permute-start.1 = (bf16[96,512]{1,0:T(8,128)(2,1)S(1)}, bf16[96,512]{1,0:T(8,128)(2,1)S(1)}, u32[]{:S(2)}, u32[]{:S(2)}) collective-permute-start(bf16[96,512]{1,0:T(8,128)(2,1)S(1)} %get-tuple-element.19), channel_id=1, source_target_pairs={{0,256},{128,384},{256,0},{384,128},{1,257},{129,385},{257,1},{385... | collective-permute-start | bytes 294920 | tf_op jit(solution)/shard_map/ppermute | solution.py:213
  39.4 0.0 collective-permute-done.2
  39.4 8.7 %collective-permute-done = bf16[96,512]{1,0:T(8,128)(2,1)S(1)} collective-permute-done((bf16[96,512]{1,0:T(8,128)(2,1)S(1)}, bf16[96,512]{1,0:T(8,128)(2,1)S(1)}, u32[]{:S(2)}, u32[]{:S(2)}) %collective-permute-start) | collective-permute-done | bytes 98336 | tf_op jit(solution)/shard_map/ppermute | solution.py:213
  48.1 0.0 collective-permute-done.1
  48.1 0.1 pad_maximum_fusion
  48.1 0.6 gather_fusion
  48.7 0.1 bitcast_select_fusion
  48.8 2.4 %all_gather.4 = bf16[2,4,96,512]{3,2,1,0:T(8,128)(2,1)S(1)} all-gather(bf16[1,4,96,512]{3,2,1,0:T(8,128)(2,1)S(1)} %bitcast_select_fusion), channel_id=1, replica_groups=mesh['x'=4,'core'=2,'zh'=4,'zl'=2,'y'=8] {'core'}, dimensions={0}, use_global_device_ids=true | all-gather | bytes 1179648 | tf_op jit(solution)/shard_map/all_gather | solution.py:216
  51.2 0.0 copy-start.1
  51.2 3.9 %collective-permute-start.3 = (bf16[2,4,96,512]{3,2,1,0:T(8,128)(2,1)S(1)}, bf16[2,4,96,512]{3,2,1,0:T(8,128)(2,1)S(1)}, u32[]{:S(2)}, u32[]{:S(2)}) collective-permute-start(bf16[2,4,96,512]{3,2,1,0:T(8,128)(2,1)S(1)} %all_gather.4), channel_id=1, source_target_pairs={{0,8},{72,64},{1,9},{73,65},{2,10},{74,66},{3,11},{75,67},{4,12},{... | collective-permute-start | bytes 2359304 | tf_op jit(solution)/shard_map/ppermute | solution.py:217
  55.1 0.1 pad_add_fusion.place_ref
  55.2 11.8 %collective-permute-done.3 = bf16[2,4,96,512]{3,2,1,0:T(8,128)(2,1)S(1)} collective-permute-done((bf16[2,4,96,512]{3,2,1,0:T(8,128)(2,1)S(1)}, bf16[2,4,96,512]{3,2,1,0:T(8,128)(2,1)S(1)}, u32[]{:S(2)}, u32[]{:S(2)}) %collective-permute-start.3) | collective-permute-done | bytes 786464 | tf_op jit(solution)/shard_map/ppermute | solution.py:217
  67.0 0.1 broadcast_select_fusion.legendre_ref
  67.1 0.0 copy-done.1
  67.1 1.9 %shard_map.57 = (bf16[512,1280]{1,0:T(8,128)(2,1)S(1)}, bf16[512,512]{1,0:T(8,128)(2,1)S(1)}) custom-call(s32[1,256]{1,0:T(1,128)S(1)} %bitcast.28, s32[2]{0:T(128)S(1)} %pad_add_fusion.place_ref, bf16[2,4,96,512]{3,2,1,0:T(8,128)(2,1)S(1)} %broadcast_select_fusion.legendre_ref), custom_call_target="tpu_custom_call" | custom-call | flops 402653184 | bytes 2097152 | tf_op jit(solution)/shard_map/pallas_call | solution.py:219
  68.9 0.0 all-to-all-done.arrived_ref
  69.0 3.1 %shard_map.58 = bf16[512,2,256]{2,1,0:T(2,128)(2,1)} custom-call(bf16[256,2,1280]{2,1,0:T(2,128)(2,1)S(1)} %all-to-all-done.arrived_ref, bf16[512,1280]{1,0:T(8,128)(2,1)S(1)} %get-tuple-element.15.weights_ref, bf16[512,512]{1,0:T(8,128)(2,1)S(1)} %get-tuple-element.16.parted_ref), custom_call_target="tpu_custom_call" | custom-call | flops 939524096 | bytes 2097152 | tf_op jit(solution)/shard_map/pallas_call | solution.py:230
  72.0 15.6 %all-to-all-start.1 = ((bf16[512,2,256]{2,1,0:T(2,128)(2,1)}), bf16[512,2,256]{2,1,0:T(2,128)(2,1)S(1)}, u32[]{:S(2)}, u32[]{:S(2)}) async-start(bf16[512,2,256]{2,1,0:T(2,128)(2,1)} %shard_map.58), calls=%async_computation.1 | async-start | bytes 1048576 | tf_op jit(solution)/shard_map/all_to_all | solution.py:237
  87.7 0.0 copy-start
  87.7 1.2 copy-done
  88.9 1.0 shard_map.55
  89.9 18.4 %all-to-all-done.1.right_ref = bf16[512,2,256]{2,1,0:T(2,128)(2,1)S(1)} async-done(((bf16[512,2,256]{2,1,0:T(2,128)(2,1)}), bf16[512,2,256]{2,1,0:T(2,128)(2,1)S(1)}, u32[]{:S(2)}, u32[]{:S(2)}) %all-to-all-start.1) | async-done | bytes 524320 | tf_op jit(solution)/shard_map/all_to_all | solution.py:237
  108.3 0.5 shard_map.59
  108.8 26.4 %all_to_all.15 = bf16[64,8,512]{2,1,0:T(8,128)(2,1)S(1)} all-to-all(bf16[64,8,512]{2,1,0:T(8,128)(2,1)S(1)} %bitcast.26), channel_id=1, replica_groups=mesh['x'=4,'core'=2,'zh'=4,'zl'=2,'y'=8] {'zh','zl','y'}, dimensions={0} | all-to-all | bytes 1048576 | tf_op jit(solution)/shard_map/all_to_all | solution.py:239
  135.2 0.9 copy.7
  (4 shorter events, 0.1 us)
Async XLA Ops:
  6.7 21.5 %copy-start.2 = (bf16[4,512,96]{1,2,0:T(8,128)(2,1)S(1)}, bf16[4,512,96]{1,2,0:T(8,128)(2,1)}, u32[]{:S(2)}) copy-start(bf16[4,512,96]{1,2,0:T(8,128)(2,1)} %param.6) | copy-start | bytes 1179652
  6.7 62.3 %all-to-all-start = ((bf16[256,2,1280]{2,1,0:T(2,128)(2,1)}), bf16[256,2,1280]{2,1,0:T(2,128)(2,1)S(1)}, u32[]{:S(2)}, u32[]{:S(2)}) async-start(bf16[256,2,1280]{2,1,0:T(2,128)(2,1)} %shard_map.56), calls=%async_computation | async-start | bytes 2621440 | tf_op jit(solution)/shard_map/all_to_all | solution.py:207
  28.3 11.1 %collective-permute-start.2 = (bf16[96,512]{1,0:T(8,128)(2,1)S(1)}, bf16[96,512]{1,0:T(8,128)(2,1)S(1)}, u32[]{:S(2)}, u32[]{:S(2)}) collective-permute-start(bf16[96,512]{1,0:T(8,128)(2,1)S(1)} %get-tuple-element.18), channel_id=1, source_target_pairs={{0,384},{128,0},{256,128},{384,256},{1,385},{129,1},{257,129},{385... | collective-permute-start | bytes 294920 | tf_op jit(solution)/shard_map/ppermute | solution.py:213
  33.4 14.7 %collective-permute-start = (bf16[96,512]{1,0:T(8,128)(2,1)S(1)}, bf16[96,512]{1,0:T(8,128)(2,1)S(1)}, u32[]{:S(2)}, u32[]{:S(2)}) collective-permute-start(bf16[96,512]{1,0:T(8,128)(2,1)S(1)} %get-tuple-element.20), channel_id=1, source_target_pairs={{0,128},{128,256},{256,384},{384,0},{1,129},{129,257},{257,385},{3... | collective-permute-start | bytes 294920 | tf_op jit(solution)/shard_map/ppermute | solution.py:213
  35.3 12.7 %collective-permute-start.1 = (bf16[96,512]{1,0:T(8,128)(2,1)S(1)}, bf16[96,512]{1,0:T(8,128)(2,1)S(1)}, u32[]{:S(2)}, u32[]{:S(2)}) collective-permute-start(bf16[96,512]{1,0:T(8,128)(2,1)S(1)} %get-tuple-element.19), channel_id=1, source_target_pairs={{0,256},{128,384},{256,0},{384,128},{1,257},{129,385},{257,1},{385... | collective-permute-start | bytes 294920 | tf_op jit(solution)/shard_map/ppermute | solution.py:213
  51.2 15.9 %copy-start.1 = (s32[256]{0:T(256)S(1)}, s32[256]{0:T(256)}, u32[]{:S(2)}) copy-start(s32[256]{0:T(256)} %param.7) | copy-start | bytes 3076
  51.2 15.8 %collective-permute-start.3 = (bf16[2,4,96,512]{3,2,1,0:T(8,128)(2,1)S(1)}, bf16[2,4,96,512]{3,2,1,0:T(8,128)(2,1)S(1)}, u32[]{:S(2)}, u32[]{:S(2)}) collective-permute-start(bf16[2,4,96,512]{3,2,1,0:T(8,128)(2,1)S(1)} %all_gather.4), channel_id=1, source_target_pairs={{0,8},{72,64},{1,9},{73,65},{2,10},{74,66},{3,11},{75,67},{4,12},{... | collective-permute-start | bytes 2359304 | tf_op jit(solution)/shard_map/ppermute | solution.py:217
  72.0 36.2 %all-to-all-start.1 = ((bf16[512,2,256]{2,1,0:T(2,128)(2,1)}), bf16[512,2,256]{2,1,0:T(2,128)(2,1)S(1)}, u32[]{:S(2)}, u32[]{:S(2)}) async-start(bf16[512,2,256]{2,1,0:T(2,128)(2,1)} %shard_map.58), calls=%async_computation.1 | async-start | bytes 1048576 | tf_op jit(solution)/shard_map/all_to_all | solution.py:237
  87.7 1.2 copy-start

commit v4 on v3

--- a/solution.py
+++ b/solution.py
@@ -42,47 +42,45 @@
 def fourier_kernel(
     assign_ref, forcing_hbm, previous_hbm, out_hbm, forcing_ref, previous_ref, table_ref, out_ref, in_sems, out_sems
 ):
-    previous_copy = pltpu.make_async_copy(previous_hbm, previous_ref, in_sems.at[3])
+    previous_copy = pltpu.make_async_copy(previous_hbm, previous_ref, in_sems.at[1])
     previous_copy.start()
-    forcing_copies = []
-    for h in range(3):
-        part = pl.ds(h * 32, 32)
-        copy = pltpu.make_async_copy(forcing_hbm.at[:, part, :], forcing_ref.at[:, part, :], in_sems.at[h])
-        copy.start()
-        forcing_copies.append(copy)
+    forcing_copy = pltpu.make_async_copy(forcing_hbm, forcing_ref, in_sems.at[0])
+    forcing_copy.start()
     row = iota((512, 1), 0)
     slot = ((row >> 4) & 3) * 64 + (row >> 8) * 32 + ((row >> 1) & 7) * 4 + ((row >> 6) & 3)
     orders = jnp.sum(jnp.where(iota((512, 256), 1) == slot, assign_ref[...], 0), axis=1, keepdims=True)
     lane = iota((512, 128), 1)
-    cos_low, sin_low = cos_sin((orders * lane + (row & 1) * (LON // 4)) & (LON - 1))
-    cos_high, sin_high = cos_sin((orders * 128 * lane) & (LON - 1))
-    scale = LON**-0.5
-    cos_low, sin_low = cos_low * scale, sin_low * scale
+    cos_now, sin_now = cos_sin((orders * lane + (row & 1) * (LON // 4)) & (LON - 1))
+    cos_half, sin_half = cos_now[:, 64:65], sin_now[:, 64:65]
+    sign = (1 - 2 * (row & 1)).astype(F32)
+    cos_step = jnp.broadcast_to(sign * (1.0 - 2.0 * sin_half * sin_half), (512, 128))
+    sin_step = jnp.broadcast_to(sign * (2.0 * sin_half * cos_half), (512, 128))
+    cos_now, sin_now = cos_now * LON**-0.5, sin_now * LON**-0.5
     for q in range(LON // 128):
-        turned = cos_low * cos_high[:, q : q + 1] - sin_low * sin_high[:, q : q + 1]
-        table_ref[:, q * 128 : q * 128 + 128] = turned.astype(BF)
+        table_ref[:, q * 128 : q * 128 + 128] = cos_now.astype(BF)
+        cos_now, sin_now = cos_now * cos_step - sin_now * sin_step, sin_now * cos_step + cos_now * sin_step
     table = table_ref[...]
     reorder = (iota((512, 512), 1) == slot * 2 + (row & 1)).astype(BF)
+    previous_copy.wait()
+    previous = previous_ref[...].reshape(512, 512)
+    forcing_copy.wait()
     out_copies = []
-
-    def send(at, width, value):
-        out_ref[:, :, at : at + width] = value.astype(BF).reshape(256, 2, width)
-        part = pl.ds(at, width)
-        copy = pltpu.make_async_copy(out_ref.at[:, :, part], out_hbm.at[:, :, part], out_sems.at[len(out_copies)])
+    for block in range(2):
+        rows = slice(block * 256, block * 256 + 256)
+        dests = pl.ds(block * 128, 128)
+        for h in range(3):
+            part = forcing_ref[:, h * 32 : h * 32 + 32, :].reshape(256, LON)
+            part = nt_dot(table[rows], part).astype(BF)
+            out_ref[dests, :, h * 256 : h * 256 + 256] = part.reshape(128, 2, 256)
+        out_ref[dests, :, 768:1280] = nt_dot(reorder[rows], previous).astype(BF).reshape(128, 2, 512)
+        copy = pltpu.make_async_copy(out_ref.at[dests], out_hbm.at[dests], out_sems.at[block])
         copy.start()
         out_copies.append(copy)
-
-    previous_copy.wait()
-    send(768, 512, nt_dot(reorder, previous_ref[...].reshape(512, 512)))
-    for h in range(3):
-        forcing_copies[h].wait()
-        part = forcing_ref[:, h * 32 : h * 32 + 32, :].reshape(256, LON)
-        send(h * 256, 256, nt_dot(table, part))
     for copy in out_copies:
         copy.wait()
 
 
-def legendre_kernel(assign_ref, place_ref, legendre_ref, out_ref, parted_ref):
+def legendre_kernel(assign_ref, place_ref, same_ref, crossed_ref, out_ref, parted_ref):
     order = jnp.sum(jnp.where(iota((1, 256), 1) == place_ref[0], assign_ref[...], 0), axis=1, keepdims=True)
     row = iota((512, 1), 0)
     core, x = (row >> 5) & 1, row & 3
@@ -90,9 +88,15 @@
     degree = (2 * x + core) * 64 + inner
     column = iota((512, 512), 1)
     kept = jnp.where((column == degree) & (degree >= order), 1.0, 0.0).astype(BF)
+    x_here, straight = place_ref[2], place_ref[3] == 0
     for h in range(3):
+        rows = pl.ds(h * 32, 32)
         for core_from in range(2):
-            pieces = [legendre_ref[core_from, x_from, h * 32 : h * 32 + 32, :] for x_from in range(4)]
+            pieces = []
+            for x_from in range(4):
+                at = (x_here - x_from) & 3
+                near, far = same_ref[at, rows, :], crossed_ref[at, rows, :]
+                pieces.append(jnp.where(straight == (core_from == 0), near, far))
             at = h * 256 + core_from * 128
             out_ref[:, at : at + 128] = nt_dot(kept, jnp.concatenate(pieces, axis=0)).astype(BF)
     out_ref[:, 768:1280] = jnp.where(column == core * 256 + x * 64 + inner, 2.0, 0.0).astype(BF)
@@ -103,13 +107,14 @@
     return pltpu.roll(a, shift, 1)
 
 
-def spectrum_kernel(arrived_ref, weights_ref, parted_ref, out_ref, gathered_ref):
+def spectrum_kernel(arrived_ref, weights_ref, parted_ref, out_ref, rows_ref, gathered_ref):
+    rows_ref[...] = arrived_ref[...].reshape(512, 1280)
     lane = iota((64, 128), 1)
     low_half = lane < 64
     even_quarter = (lane & 32) == 0
 
     def tile(block, at):
-        return arrived_ref[block * 32 : block * 32 + 32, :, at : at + 128].reshape(64, 128).astype(F32)
+        return rows_ref[block * 64 : block * 64 + 64, at : at + 128].astype(F32)
 
     def place(rho, at, value):
         gathered_ref[rho * 64 : rho * 64 + 64, at : at + 128] = value.astype(BF)
@@ -185,7 +190,7 @@
     orders = assign.reshape(1, 256)
     slot = zh * 64 + core * 32 + y * 4 + x
     degree = (x * 2 + core) * 64 + zh * 16 + zl * 8 + y
-    place = jnp.stack([slot, degree]).astype(jnp.int32)
+    place = jnp.stack([slot, degree, x, zl]).astype(jnp.int32)
 
     sent = call(
         fourier_kernel,
@@ -196,8 +201,8 @@
             pltpu.VMEM((8, 64, 512), BF),
             pltpu.VMEM((512, LON), BF),
             pltpu.VMEM((256, 2, 1280), BF),
-            pltpu.SemaphoreType.DMA((4,)),
-            pltpu.SemaphoreType.DMA((4,)),
+            pltpu.SemaphoreType.DMA((2,)),
+            pltpu.SemaphoreType.DMA((2,)),
         ],
         2 * 512 * 768 * 1024,
         60,
@@ -207,18 +212,16 @@
     arrived = lax.all_to_all(sent, ("core", "x", "zh", "y"), 0, 0, tiled=True)
 
     by_order = legendre.transpose(0, 2, 1)
-    pieces = [lax.dynamic_index_in_dim(by_order, x, 0, keepdims=False)]
-    for shift in range(1, 4):
-        mine = lax.dynamic_index_in_dim(by_order, (x + shift) % 4, 0, keepdims=False)
-        pieces.append(lax.ppermute(mine, "x", [(i, (i + shift) % 4) for i in range(4)]))
-    stacked = jnp.stack(pieces)
-    ordered = jnp.take(stacked, (x - jnp.arange(4)) % 4, axis=0)
-    whole = lax.all_gather(ordered, "core", axis=0)
-    other = lax.ppermute(whole, ("core", "zl"), [(0, 1), (3, 2)])
-    whole = jnp.where(core == zl, whole, other)
+    rolled = jnp.take(by_order, (x + jnp.arange(4)) % 4, axis=0)
+    two_on = lax.ppermute(rolled[2:], "x", [(i, (i + 2) % 4) for i in range(4)])
+    one_on = jnp.stack([rolled[1], two_on[1]])
+    one_on = lax.ppermute(one_on, "x", [(i, (i + 1) % 4) for i in range(4)])
+    gathered = jnp.stack([rolled[0], one_on[0], two_on[0], one_on[1]])
+    same = lax.ppermute(gathered, ("core", "zl"), [(0, 0), (1, 2), (2, 1), (3, 3)])
+    crossed = lax.ppermute(gathered, ("core", "zl"), [(0, 1), (1, 3), (2, 0), (3, 2)])
     weights, parted = call(
-        legendre_kernel, (bf16(512, 1280), bf16(512, 512)), [VMEM, SMEM, VMEM], (), 2 * 512 * 512 * 768
-    )(orders, place, whole)
+        legendre_kernel, (bf16(512, 1280), bf16(512, 512)), [VMEM, SMEM, VMEM, VMEM], (), 2 * 512 * 512 * 768
+    )(orders, place, same, crossed)
     solver, valid = call(
         inverse_kernel,
         (bf16(2, 512, 256), jax.ShapeDtypeStruct((8, 512), F32)),
@@ -231,7 +234,7 @@
         spectrum_kernel,
         bf16(512, 2, 256),
         [VMEM] * 3,
-        [pltpu.VMEM((512, 1280), BF)],
+        [pltpu.VMEM((512, 1280), BF)] * 2,
         2 * 512 * 512 * 1792,
     )(arrived, weights, parted)
     right = lax.all_to_all(right, ("zl", "zh", "core", "y", "x"), 0, 0, tiled=True)

time: 137 us -> 142 us (1.036)
  waiting for transfers between devices: 38.8 us -> 45.3 us
  local copies, waits for them, and re-layouts: 2.79 us -> 6.3 us
  blocking collectives: 28.8 us -> 26.4 us
  Pallas kernels: 13.1 us -> 10.7 us
    ppermute x4, waiting for transfers between devices: 20.4 us -> 27 us  [the longest x1 10.6 us: shards(): one_on = lax.ppermute(one_on, 'x', [(i, (i + 1) % 4) for i in range(4)])]
    unnamed x6 -> x14, local copies, waits for them, and re-layouts: 1.23 us -> 4.72 us
    all_gather x1 -> x0, blocking collectives: 2.37 us -> none  [shards(): whole = lax.all_gather(ordered, 'core', axis=0)]
    pallas_call x1, Pallas kernels: 6.67 us -> 4.6 us  [shards(): call(fourier_kernel, bf16(256, 2, 1280), [VMEM, HBM, HBM], [pltpu.VMEM((8...]
    all_to_all x1, starting transfers between devices: 15.6 us -> 17.2 us  [shards(): lax.all_to_all(right, ('zl', 'zh', 'core', 'y', 'x'), 0, 0, tiled=True)]
    ppermute x4, starting transfers between devices: 15 us -> 13.5 us  [the longest x1 5.2 us: shards(): two_on = lax.ppermute(rolled[2:], 'x', [(i, (i + 2) % 4) for i in range(4)])]
  transfers between devices with their start and end apart: 6 -> 6, of which waited for: 3 -> 4; matrix products, arithmetic and copies ran while one was open for 1% -> 1% of each run, Pallas kernels for 2% -> 2%
where the time goes in v4:
time: 142 us; the launch traced here: 141 us
  starting transfers between devices  51.9 us (37%)
  waiting for transfers between devices  45.3 us (32%)
  blocking collectives  26.4 us (19%)
  Pallas kernels  10.7 us (8%)
  local copies, waits for them, and re-layouts  6.3 us (4%)
    all_to_all x1, blocking collectives, shards(): out = lax.all_to_all(solved.reshape(64, 8, 512), RAD, 0, 0, tiled=True)  26.4 us
    all_to_all x1, starting transfers between devices, shards(): arrived = lax.all_to_all(sent, ('core', 'x', 'zh', 'y'), 0, 0, tiled=True)  21.3 us
    all_to_all x1, waiting for transfers between devices, shards(): lax.all_to_all(right, ('zl', 'zh', 'core', 'y', 'x'), 0, 0, tiled=True)  18.4 us
    all_to_all x1, starting transfers between devices, shards(): lax.all_to_all(right, ('zl', 'zh', 'core', 'y', 'x'), 0, 0, tiled=True)  17.2 us
    ppermute x1, waiting for transfers between devices, shards(): one_on = lax.ppermute(one_on, 'x', [(i, (i + 1) % 4) for i in range(4)])  10.6 us
    ppermute x1, waiting for transfers between devices, shards(): two_on = lax.ppermute(rolled[2:], 'x', [(i, (i + 2) % 4) for i in range(4)])  10.1 us
    ppermute x1, waiting for transfers between devices, shards(): lax.ppermute(gathered, ('core', 'zl'), [(0, 1), (1, 3), (2, 0), (3, 2)])  6.19 us
    ppermute x1, starting transfers between devices, shards(): two_on = lax.ppermute(rolled[2:], 'x', [(i, (i + 2) % 4) for i in range(4)])  5.2 us
  transfers between devices with their start and end apart: 6, of which 4 were waited for; matrix products, arithmetic and copies ran while one was open for 1% of the time, Pallas kernels for 2%

profile of v4, /device:TPU:8, one launch (start us, length us, event | category | flops | bytes accessed | tf_op | source)
XLA Modules:
  0.0 141.2 jit_solution(2519227443997987649)
XLA Ops:
  0.0 0.0 copy-start
  0.0 4.6 %shard_map.56 = bf16[256,2,1280]{2,1,0:T(2,128)(2,1)} custom-call(s32[1,256]{1,0:T(1,128)} %bitcast.12, bf16[8,96,1024]{2,1,0:T(8,128)(2,1)} %forcing_hbm.1, bf16[8,64,512]{2,1,0:T(8,128)(2,1)} %previous_hbm.1), custom_call_target="tpu_custom_call" | custom-call | flops 805306368 | bytes 2097152 | tf_op jit(solution)/shard_map/pallas_call | solution.py:195
  4.6 21.3 %all-to-all-start = ((bf16[256,2,1280]{2,1,0:T(2,128)(2,1)}), bf16[256,2,1280]{2,1,0:T(2,128)(2,1)S(1)}, u32[]{:S(2)}, u32[]{:S(2)}) async-start(bf16[256,2,1280]{2,1,0:T(2,128)(2,1)} %shard_map.56), calls=%async_computation | async-start | bytes 2621440 | tf_op jit(solution)/shard_map/all_to_all | solution.py:212
  26.0 0.0 copy-done
  26.0 0.6 gather_fusion
  26.6 0.1 broadcast_select_fusion
  26.7 0.0 copy-start.2
  26.7 5.2 %collective-permute-start = (bf16[2,96,512]{2,1,0:T(8,128)(2,1)S(1)}, bf16[2,96,512]{2,1,0:T(8,128)(2,1)S(1)}, u32[]{:S(2)}, u32[]{:S(2)}) collective-permute-start(bf16[2,96,512]{2,1,0:T(8,128)(2,1)S(1)} %slice.32), channel_id=1, source_target_pairs={{0,256},{128,384},{256,0},{384,128},{1,257},{129,385},{257,1},{385... | collective-permute-start | bytes 589832 | tf_op jit(solution)/shard_map/ppermute | solution.py:216
  32.0 10.1 %collective-permute-done = bf16[2,96,512]{2,1,0:T(8,128)(2,1)S(1)} collective-permute-done((bf16[2,96,512]{2,1,0:T(8,128)(2,1)S(1)}, bf16[2,96,512]{2,1,0:T(8,128)(2,1)S(1)}, u32[]{:S(2)}, u32[]{:S(2)}) %collective-permute-start) | collective-permute-done | bytes 196640 | tf_op jit(solution)/shard_map/ppermute | solution.py:216
  42.2 3.1 %collective-permute-start.1 = (bf16[2,96,512]{2,1,0:T(8,128)(2,1)S(1)}, bf16[2,96,512]{2,1,0:T(8,128)(2,1)S(1)}, u32[]{:S(2)}, u32[]{:S(2)}) collective-permute-start(bf16[2,96,512]{2,1,0:T(8,128)(2,1)S(1)} %pad_maximum_fusion.1), channel_id=1, source_target_pairs={{0,128},{128,256},{256,384},{384,0},{1,129},{129,257},{257,385},{3... | collective-permute-start | bytes 589832 | tf_op jit(solution)/shard_map/ppermute | solution.py:218
  45.3 10.6 %collective-permute-done.1 = bf16[2,96,512]{2,1,0:T(8,128)(2,1)S(1)} collective-permute-done((bf16[2,96,512]{2,1,0:T(8,128)(2,1)S(1)}, bf16[2,96,512]{2,1,0:T(8,128)(2,1)S(1)}, u32[]{:S(2)}, u32[]{:S(2)}) %collective-permute-start.1) | collective-permute-done | bytes 196640 | tf_op jit(solution)/shard_map/ppermute | solution.py:218
  56.0 0.1 pad_maximum_fusion
  56.0 0.7 collective-permute-start.2
  56.7 4.4 %collective-permute-start.3 = (bf16[4,96,512]{2,1,0:T(8,128)(2,1)S(1)}, bf16[4,96,512]{2,1,0:T(8,128)(2,1)S(1)}, u32[]{:S(2)}, u32[]{:S(2)}) collective-permute-start(bf16[4,96,512]{2,1,0:T(8,128)(2,1)S(1)} %pad_maximum_fusion), channel_id=1, source_target_pairs={{0,8},{8,72},{64,0},{72,64},{1,9},{9,73},{65,1},{73,65},{2,10},{10... | collective-permute-start | bytes 1179656 | tf_op jit(solution)/shard_map/ppermute | solution.py:221
  61.2 0.1 pad_add_fusion.place_ref
  61.3 0.0 collective-permute-done.2.same_ref
  61.3 0.0 copy-start.3
  61.3 0.7 copy-done.3
  62.0 6.2 %collective-permute-done.3.crossed_ref = bf16[4,96,512]{2,1,0:T(8,128)(2,1)S(1)} collective-permute-done((bf16[4,96,512]{2,1,0:T(8,128)(2,1)S(1)}, bf16[4,96,512]{2,1,0:T(8,128)(2,1)S(1)}, u32[]{:S(2)}, u32[]{:S(2)}) %collective-permute-start.3) | collective-permute-done | bytes 393248 | tf_op jit(solution)/shard_map/ppermute | solution.py:221
  68.2 0.0 copy-start.5
  68.2 0.7 copy-done.5
  68.9 0.0 copy-done.2
  68.9 0.0 copy-start.4
  69.0 1.0 copy-done.4
  69.9 0.0 copy-start.6
  69.9 1.0 copy-done.6
  70.9 1.9 %shard_map.57 = (bf16[512,1280]{1,0:T(8,128)(2,1)S(1)}, bf16[512,512]{1,0:T(8,128)(2,1)S(1)}) custom-call(s32[1,256]{1,0:T(1,128)S(1)} %bitcast.13, s32[4]{0:T(128)S(1)} %pad_add_fusion.place_ref, bf16[4,96,512]{2,1,0:T(8,128)(2,1)S(1)} %copy-done.4, bf16[4,96,512]{2,1,0:T(8,128)(2,1)S(1)} %copy-done.6), custom_call_target="tpu_custom_call" | custom-call | flops 402653184 | bytes 2097152 | tf_op jit(solution)/shard_map/pallas_call | solution.py:222
  72.8 0.0 all-to-all-done.arrived_ref
  72.9 2.7 %shard_map.58 = bf16[512,2,256]{2,1,0:T(2,128)(2,1)} custom-call(bf16[256,2,1280]{2,1,0:T(2,128)(2,1)S(1)} %all-to-all-done.arrived_ref, bf16[512,1280]{1,0:T(8,128)(2,1)S(1)} %get-tuple-element.15.weights_ref, bf16[512,512]{1,0:T(8,128)(2,1)S(1)} %get-tuple-element.16.parted_ref), custom_call_target="tpu_custom_call" | custom-call | flops 939524096 | bytes 2097152 | tf_op jit(solution)/shard_map/pallas_call | solution.py:233
  75.6 17.2 %all-to-all-start.1 = ((bf16[512,2,256]{2,1,0:T(2,128)(2,1)}), bf16[512,2,256]{2,1,0:T(2,128)(2,1)S(1)}, u32[]{:S(2)}, u32[]{:S(2)}) async-start(bf16[512,2,256]{2,1,0:T(2,128)(2,1)} %shard_map.58), calls=%async_computation.1 | async-start | bytes 1048576 | tf_op jit(solution)/shard_map/all_to_all | solution.py:240
  92.7 0.0 copy-start.1
  92.8 1.2 copy-done.1
  94.0 1.0 shard_map.55
  95.0 18.4 %all-to-all-done.1.right_ref = bf16[512,2,256]{2,1,0:T(2,128)(2,1)S(1)} async-done(((bf16[512,2,256]{2,1,0:T(2,128)(2,1)}), bf16[512,2,256]{2,1,0:T(2,128)(2,1)S(1)}, u32[]{:S(2)}, u32[]{:S(2)}) %all-to-all-start.1) | async-done | bytes 524320 | tf_op jit(solution)/shard_map/all_to_all | solution.py:240
  113.4 0.5 shard_map.59
  113.9 26.4 %all_to_all.15 = bf16[64,8,512]{2,1,0:T(8,128)(2,1)S(1)} all-to-all(bf16[64,8,512]{2,1,0:T(8,128)(2,1)S(1)} %bitcast.11), channel_id=1, replica_groups=mesh['x'=4,'core'=2,'zh'=4,'zl'=2,'y'=8] {'zh','zl','y'}, dimensions={0} | all-to-all | bytes 1048576 | tf_op jit(solution)/shard_map/all_to_all | solution.py:242
  140.3 0.9 copy.7
  (8 shorter events, 0.1 us)
Async XLA Ops:
  0.0 26.0 %copy-start = (bf16[4,512,96]{1,2,0:T(8,128)(2,1)S(1)}, bf16[4,512,96]{1,2,0:T(8,128)(2,1)}, u32[]{:S(2)}) copy-start(bf16[4,512,96]{1,2,0:T(8,128)(2,1)} %param.6) | copy-start | bytes 1179652
  4.6 68.2 %all-to-all-start = ((bf16[256,2,1280]{2,1,0:T(2,128)(2,1)}), bf16[256,2,1280]{2,1,0:T(2,128)(2,1)S(1)}, u32[]{:S(2)}, u32[]{:S(2)}) async-start(bf16[256,2,1280]{2,1,0:T(2,128)(2,1)} %shard_map.56), calls=%async_computation | async-start | bytes 2621440 | tf_op jit(solution)/shard_map/all_to_all | solution.py:212
  26.7 42.2 %copy-start.2 = (s32[256]{0:T(256)S(1)}, s32[256]{0:T(256)}, u32[]{:S(2)}) copy-start(s32[256]{0:T(256)} %param.7) | copy-start | bytes 3076
  26.7 15.4 %collective-permute-start = (bf16[2,96,512]{2,1,0:T(8,128)(2,1)S(1)}, bf16[2,96,512]{2,1,0:T(8,128)(2,1)S(1)}, u32[]{:S(2)}, u32[]{:S(2)}) collective-permute-start(bf16[2,96,512]{2,1,0:T(8,128)(2,1)S(1)} %slice.32), channel_id=1, source_target_pairs={{0,256},{128,384},{256,0},{384,128},{1,257},{129,385},{257,1},{385... | collective-permute-start | bytes 589832 | tf_op jit(solution)/shard_map/ppermute | solution.py:216
  42.2 13.8 %collective-permute-start.1 = (bf16[2,96,512]{2,1,0:T(8,128)(2,1)S(1)}, bf16[2,96,512]{2,1,0:T(8,128)(2,1)S(1)}, u32[]{:S(2)}, u32[]{:S(2)}) collective-permute-start(bf16[2,96,512]{2,1,0:T(8,128)(2,1)S(1)} %pad_maximum_fusion.1), channel_id=1, source_target_pairs={{0,128},{128,256},{256,384},{384,0},{1,129},{129,257},{257,385},{3... | collective-permute-start | bytes 589832 | tf_op jit(solution)/shard_map/ppermute | solution.py:218
  56.0 5.2 %collective-permute-start.2 = (bf16[4,96,512]{2,1,0:T(8,128)(2,1)S(1)}, bf16[4,96,512]{2,1,0:T(8,128)(2,1)S(1)}, u32[]{:S(2)}, u32[]{:S(2)}) collective-permute-start(bf16[4,96,512]{2,1,0:T(8,128)(2,1)S(1)} %pad_maximum_fusion), channel_id=1, source_target_pairs={{0,0},{8,64},{64,8},{72,72},{1,1},{9,65},{65,9},{73,73},{2,2},{10,... | collective-permute-start | bytes 1179656 | tf_op jit(solution)/shard_map/ppermute | solution.py:220
  56.7 11.5 %collective-permute-start.3 = (bf16[4,96,512]{2,1,0:T(8,128)(2,1)S(1)}, bf16[4,96,512]{2,1,0:T(8,128)(2,1)S(1)}, u32[]{:S(2)}, u32[]{:S(2)}) collective-permute-start(bf16[4,96,512]{2,1,0:T(8,128)(2,1)S(1)} %pad_maximum_fusion), channel_id=1, source_target_pairs={{0,8},{8,72},{64,0},{72,64},{1,9},{9,73},{65,1},{73,65},{2,10},{10... | collective-permute-start | bytes 1179656 | tf_op jit(solution)/shard_map/ppermute | solution.py:221
  61.3 0.7 copy-start.3
  68.2 0.7 copy-start.5
  68.9 1.0 copy-start.4
  69.9 1.0 copy-start.6
  75.6 37.8 %all-to-all-start.1 = ((bf16[512,2,256]{2,1,0:T(2,128)(2,1)}), bf16[512,2,256]{2,1,0:T(2,128)(2,1)S(1)}, u32[]{:S(2)}, u32[]{:S(2)}) async-start(bf16[512,2,256]{2,1,0:T(2,128)(2,1)} %shard_map.58), calls=%async_computation.1 | async-start | bytes 1048576 | tf_op jit(solution)/shard_map/all_to_all | solution.py:240
  92.7 1.2 copy-start.1

commit v5 on v4

v5 whole, which is shorter than its diff:
```python
import math

import jax
import jax.numpy as jnp
from jax import lax
from jax.experimental import pallas as pl
from jax.experimental.pallas import tpu as pltpu
from jax.sharding import Mesh, PartitionSpec as P

NR = 512
L = 512
LON = 1024
BF = jnp.bfloat16
F32 = jnp.float32
RAD = ("z", "y")
LAT = ("x", "core")


def nt_dot(a, b):
    return lax.dot_general(a, b, (((1,), (1,)), ((), ())), preferred_element_type=F32)


def iota(shape, dim):
    return lax.broadcasted_iota(jnp.int32, shape, dim)


def cos_sin(phase):
    quadrant = ((phase + 128) >> 8) & 3
    rest = ((phase + 128) & 255) - 128
    x = rest.astype(F32) * (2.0 * math.pi / LON)
    x2 = x * x
    sin_x = x * (1.0 + x2 * (-1.0 / 6 + x2 * (1.0 / 120 + x2 * (-1.0 / 5040 + x2 * (1.0 / 362880)))))
    cos_x = 1.0 + x2 * (-0.5 + x2 * (1.0 / 24 + x2 * (-1.0 / 720 + x2 * (1.0 / 40320))))
    swap = (quadrant & 1) == 1
    cos_part = jnp.where(swap, sin_x, cos_x)
    sin_part = jnp.where(swap, cos_x, sin_x)
    cos_sign = jnp.where((quadrant == 1) | (quadrant == 2), -1.0, 1.0)
    sin_sign = jnp.where(quadrant >= 2, -1.0, 1.0)
    return cos_part * cos_sign, sin_part * sin_sign


def fourier_kernel(
    assign_ref, forcing_hbm, previous_hbm, out_hbm, forcing_ref, previous_ref, table_ref, out_ref, in_sems, out_sems
):
    previous_copy = pltpu.make_async_copy(previous_hbm, previous_ref, in_sems.at[1])
    previous_copy.start()
    forcing_copy = pltpu.make_async_copy(forcing_hbm, forcing_ref, in_sems.at[0])
    forcing_copy.start()
    row = iota((512, 1), 0)
    slot = ((row >> 1) & 63) * 4 + (row >> 7)
    orders = jnp.sum(jnp.where(iota((512, 256), 1) == slot, assign_ref[...], 0), axis=1, keepdims=True)
    lane = iota((512, 128), 1)
    cos_now, sin_now = cos_sin((orders * lane + (row & 1) * (LON // 4)) & (LON - 1))
    cos_half, sin_half = cos_now[:, 64:65], sin_now[:, 64:65]
    sign = (1 - 2 * (row & 1)).astype(F32)
    cos_step = jnp.broadcast_to(sign * (1.0 - 2.0 * sin_half * sin_half), (512, 128))
    sin_step = jnp.broadcast_to(sign * (2.0 * sin_half * cos_half), (512, 128))
    cos_now, sin_now = cos_now * LON**-0.5, sin_now * LON**-0.5
    for q in range(LON // 128):
        table_ref[:, q * 128 : q * 128 + 128] = cos_now.astype(BF)
        cos_now, sin_now = cos_now * cos_step - sin_now * sin_step, sin_now * cos_step + cos_now * sin_step
    table = table_ref[...]
    reorder = (iota((512, 512), 1) == slot * 2 + (row & 1)).astype(BF)
    previous_copy.wait()
    previous = previous_ref[...].reshape(512, 512)
    forcing_copy.wait()
    out_copies = []
    for block in range(2):
        rows = slice(block * 256, block * 256 + 256)
        parts = []
        for h in range(3):
            part = forcing_ref[:, h * 32 : h * 32 + 32, :].reshape(256, LON)
            parts.append(nt_dot(table[rows], part).astype(BF))
        before = nt_dot(reorder[rows], previous).astype(BF)
        for half in range(2):
            dests = pl.ds(half * 256 + block * 128, 128)
            pieces = [part[:, half * 128 : half * 128 + 128] for part in parts]
            pieces.append(before[:, half * 256 : half * 256 + 256])
            out_ref[dests] = jnp.concatenate(pieces, axis=1).reshape(128, 2, 640)
            sem = out_sems.at[block * 2 + half]
            copy = pltpu.make_async_copy(out_ref.at[dests], out_hbm.at[dests], sem)
            copy.start()
            out_copies.append(copy)
    for copy in out_copies:
        copy.wait()


def legendre_kernel(assign_ref, place_ref, legendre_ref, out_ref, parted_ref):
    order = jnp.sum(jnp.where(iota((1, 256), 1) == place_ref[0], assign_ref[...], 0), axis=1, keepdims=True)
    row = iota((512, 1), 0)
    core, x, inner = row >> 8, row & 3, (row >> 2) & 63
    degree = (2 * x + core) * 64 + inner
    column = iota((512, 512), 1)
    kept = jnp.where((column == degree) & (degree >= order), 1.0, 0.0).astype(BF)
    x_here = place_ref[2]
    for h in range(3):
        rows = pl.ds(h * 32, 32)
        for core_from in range(2):
            pieces = [legendre_ref[core_from, (x_here - x_from) & 3, rows, :] for x_from in range(4)]
            at = h * 256 + core_from * 128
            out_ref[:, at : at + 128] = nt_dot(kept, jnp.concatenate(pieces, axis=0)).astype(BF)
    out_ref[:, 768:1280] = jnp.where(column == core * 256 + x * 64 + inner, 2.0, 0.0).astype(BF)
    parted_ref[...] = (column == (row & 1) * 256 + (row >> 1)).astype(BF)


def roll(a, shift):
    return pltpu.roll(a, shift, 1)


def spectrum_kernel(arrived_ref, weights_ref, parted_ref, out_ref, rows_ref, gathered_ref):
    rows_ref[...] = arrived_ref[...].reshape(1024, 640)
    lane = iota((128, 128), 1)
    low_half = lane < 64
    even_quarter = (lane & 32) == 0

    def tile(block, at):
        return rows_ref[block * 128 : block * 128 + 128, at : at + 128].astype(F32)

    def place(rho, at, value):
        gathered_ref[rho * 128 : rho * 128 + 128, at : at + 128] = value.astype(BF)

    for h in range(3):
        for core in range(2):
            a = [tile(core * 4 + x, h * 128) for x in range(4)]
            b0 = jnp.where(low_half, a[0], roll(a[2], 64))
            b2 = jnp.where(low_half, roll(a[0], 64), a[2])
            b1 = jnp.where(low_half, a[1], roll(a[3], 64))
            b3 = jnp.where(low_half, roll(a[1], 64), a[3])
            at = h * 256 + core * 128
            place(0, at, jnp.where(even_quarter, b0, roll(b1, 32)))
            place(1, at, jnp.where(even_quarter, roll(b0, 96), b1))
            place(2, at, jnp.where(even_quarter, b2, roll(b3, 32)))
            place(3, at, jnp.where(even_quarter, roll(b2, 96), b3))
    for pair in range(2):
        for two in range(4):
            at = 384 + pair * 128
            a0, a1 = tile(two * 2, at), tile(two * 2 + 1, at)
            to = 768 + two * 128
            place(pair * 2, to, jnp.where(low_half, a0, roll(a1, 64)))
            place(pair * 2 + 1, to, jnp.where(low_half, roll(a0, 64), a1))
    right = nt_dot(weights_ref[...], gathered_ref[...]).astype(BF)
    right = jnp.dot(right, parted_ref[...], preferred_element_type=F32).astype(BF)
    out_ref[...] = right.reshape(512, 2, 256)


def inverse_kernel(assign_ref, place_ref, inverse_ref, out_ref, valid_ref):
    inverse = inverse_ref[0].astype(BF)
    row, column = iota((256, 512), 0), iota((256, 512), 1)
    for half in range(2):
        radius = (row & 63) * 8 + half * 4 + (row >> 6)
        out_ref[half] = nt_dot(inverse, (column == radius).astype(BF)).astype(BF)
    valid = jnp.where(assign_ref[...] <= place_ref[1], 1.0, 0.0)
    doubled = (row == (column >> 1)).astype(BF)
    valid_ref[...] = jnp.dot(
        jnp.broadcast_to(valid, (8, 256)).astype(BF), doubled, preferred_element_type=F32
    )


def solve_kernel(valid_ref, inverse_ref, right_ref, out_ref):
    right = right_ref[...].reshape(1024, 256)
    solved = nt_dot(inverse_ref[0], right[:512]) + nt_dot(inverse_ref[1], right[512:])
    out_ref[...] = (solved * (valid_ref[0:1, :] * 0.5)).astype(BF)


VMEM = pl.BlockSpec(memory_space=pltpu.VMEM)
SMEM = pl.BlockSpec(memory_space=pltpu.SMEM)
HBM = pl.BlockSpec(memory_space=pltpu.HBM)


def call(kernel, out, ins, scratch=(), flops=0, vmem=24, outs=None):
    return pl.pallas_call(
        kernel,
        out_shape=out,
        in_specs=ins,
        out_specs=outs or jax.tree.map(lambda _: VMEM, out),
        scratch_shapes=list(scratch),
        compiler_params=pltpu.CompilerParams(vmem_limit_bytes=vmem * 1024 * 1024),
        cost_estimate=pl.CostEstimate(flops=flops, bytes_accessed=2 * 1024 * 1024, transcendentals=0),
    )


def bf16(*shape):
    return jax.ShapeDtypeStruct(shape, BF)


def shards(forcing, legendre, assign, inverse, previous):
    x, core, rad = lax.axis_index("x"), lax.axis_index("core"), lax.axis_index(RAD)
    orders = assign.reshape(1, 256)
    place = jnp.stack([rad * 4 + x, (x * 2 + core) * 64 + rad, x]).astype(jnp.int32)

    sent = call(
        fourier_kernel,
        bf16(512, 2, 640),
        [VMEM, HBM, HBM],
        [
            pltpu.VMEM((8, 96, LON), BF),
            pltpu.VMEM((8, 64, 512), BF),
            pltpu.VMEM((512, LON), BF),
            pltpu.VMEM((512, 2, 640), BF),
            pltpu.SemaphoreType.DMA((2,)),
            pltpu.SemaphoreType.DMA((4,)),
        ],
        2 * 512 * 768 * 1024,
        60,
        HBM,
    )(orders, forcing, previous)
    sent, legendre = lax.optimization_barrier((sent, legendre))
    arrived = lax.all_to_all(sent, ("core", "x") + RAD, 0, 0, tiled=True)

    by_order = legendre.transpose(0, 2, 1)
    pieces = [lax.dynamic_index_in_dim(by_order, x, 0, keepdims=False)]
    for shift in range(1, 4):
        mine = lax.dynamic_index_in_dim(by_order, (x + shift) % 4, 0, keepdims=False)
        pieces.append(lax.ppermute(mine, "x", [(i, (i + shift) % 4) for i in range(4)]))
    whole = lax.all_gather(jnp.stack(pieces), "core", axis=0)
    weights, parted = call(
        legendre_kernel, (bf16(512, 1280), bf16(512, 512)), [VMEM, SMEM, VMEM], (), 2 * 512 * 512 * 768
    )(orders, place, whole)
    solver, valid = call(
        inverse_kernel,
        (bf16(2, 512, 256), jax.ShapeDtypeStruct((8, 512), F32)),
        [VMEM, SMEM, VMEM],
        (),
        2 * 512**3,
    )(orders, place, inverse)

    right = call(
        spectrum_kernel,
        bf16(512, 2, 256),
        [VMEM] * 3,
        [pltpu.VMEM((1024, 640), BF), pltpu.VMEM((512, 1280), BF)],
        2 * 512 * 512 * 1792,
    )(arrived, weights, parted)
    right = lax.all_to_all(right, ("core",) + RAD + ("x",), 0, 0, tiled=True)
    solved = call(solve_kernel, bf16(512, 512), [VMEM] * 3, (), 2 * 512**3)(valid, solver, right)
    out = lax.all_to_all(solved.reshape(64, 8, 512), RAD, 0, 0, tiled=True)
    return out.transpose(1, 0, 2)


def solution(mesh):
    split = Mesh(mesh.devices.reshape(4, 2, 8, 8), LAT + RAD)
    placed = (
        P(RAD, LAT, None),
        P(RAD, None, LAT),
        P(),
        P(LAT + RAD, None, None),
        P(RAD, LAT, None),
    )
    return jax.shard_map(shards, mesh=split, in_specs=placed, out_specs=P(RAD, LAT, None), check_vma=False)
```

time: 142 us -> 125 us (0.88)
  starting transfers between devices: 51.9 us -> 41.3 us
  local copies, waits for them, and re-layouts: 6.3 us -> 2.22 us
  waiting for transfers between devices: 45.3 us -> 42.4 us
  blocking collectives: 26.4 us -> 28.2 us
    ppermute x4 -> x3, waiting for transfers between devices: 27 us -> 6.7 us  [shards(): lax.ppermute(mine, 'x', [(i, (i + shift) % 4) for i in range(4)])]
    all_to_all x2, waiting for transfers between devices: 18.4 us -> 35.7 us  [the longest x1 19.1 us: shards(): right = lax.all_to_all(right, ('core',) + RAD + ('x',), 0, 0, tiled=True)]
    all_to_all x2, starting transfers between devices: 38.5 us -> 30.5 us  [the longest x1 21.1 us: shards(): arrived = lax.all_to_all(sent, ('core', 'x') + RAD, 0, 0, tiled=True)]
    unnamed x14 -> x6, local copies, waits for them, and re-layouts: 4.72 us -> 1.23 us
    ppermute x4 -> x3, starting transfers between devices: 13.5 us -> 10.7 us  [shards(): lax.ppermute(mine, 'x', [(i, (i + shift) % 4) for i in range(4)])]
    all_gather x0 -> x1, blocking collectives: none -> 2.37 us  [shards(): whole = lax.all_gather(jnp.stack(pieces), 'core', axis=0)]
  transfers between devices with their start and end apart: 6 -> 5, of which waited for: 4 -> 4; matrix products, arithmetic and copies ran while one was open for 1% -> 0% of each run, Pallas kernels for 2% -> 2%
where the time goes in v5:
time: 125 us
  waiting for transfers between devices  42.4 us (34%)
  starting transfers between devices  41.3 us (33%)
  blocking collectives  28.2 us (23%)
  Pallas kernels  10.7 us (9%)
  local copies, waits for them, and re-layouts  2.22 us (2%)
    all_to_all x1, blocking collectives, shards(): out = lax.all_to_all(solved.reshape(64, 8, 512), RAD, 0, 0, tiled=True)  25.8 us
    all_to_all x1, starting transfers between devices, shards(): arrived = lax.all_to_all(sent, ('core', 'x') + RAD, 0, 0, tiled=True)  21.1 us
    all_to_all x1, waiting for transfers between devices, shards(): right = lax.all_to_all(right, ('core',) + RAD + ('x',), 0, 0, tiled=True)  19.1 us
    all_to_all x1, waiting for transfers between devices, shards(): arrived = lax.all_to_all(sent, ('core', 'x') + RAD, 0, 0, tiled=True)  16.5 us
    ppermute x3, starting transfers between devices, shards(): lax.ppermute(mine, 'x', [(i, (i + shift) % 4) for i in range(4)])  10.7 us
    all_to_all x1, starting transfers between devices, shards(): right = lax.all_to_all(right, ('core',) + RAD + ('x',), 0, 0, tiled=True)  9.43 us
    ppermute x3, waiting for transfers between devices, shards(): lax.ppermute(mine, 'x', [(i, (i + shift) % 4) for i in range(4)])  6.7 us
    pallas_call x1, Pallas kernels, shards(): call(fourier_kernel, bf16(512, 2, 640), [VMEM, HBM, HBM], [pltpu.VMEM((8,...  4.64 us
  transfers between devices with their start and end apart: 5, of which 4 were waited for; matrix products, arithmetic and copies ran while one was open for 0% of the time, Pallas kernels for 2%

profile of v5, /device:TPU:8, one launch (start us, length us, event | category | flops | bytes accessed | tf_op | source)
XLA Modules:
  0.0 125.0 jit_solution(7593689808925658154)
XLA Ops:
  0.0 4.6 %shard_map.56 = bf16[512,2,640]{2,1,0:T(2,128)(2,1)} custom-call(s32[1,256]{1,0:T(1,128)} %bitcast.26, bf16[8,96,1024]{2,1,0:T(8,128)(2,1)} %forcing_hbm.1, bf16[8,64,512]{2,1,0:T(8,128)(2,1)} %previous_hbm.1), custom_call_target="tpu_custom_call" | custom-call | flops 805306368 | bytes 2097152 | tf_op jit(solution)/shard_map/pallas_call | solution.py:191
  4.7 0.0 copy-start.2
  4.7 21.1 %all-to-all-start = ((bf16[512,2,640]{2,1,0:T(2,128)(2,1)}), bf16[512,2,640]{2,1,0:T(2,128)(2,1)S(1)}, u32[]{:S(2)}, u32[]{:S(2)}) async-start(bf16[512,2,640]{2,1,0:T(2,128)(2,1)} %shard_map.56), calls=%async_computation | async-start | bytes 2621440 | tf_op jit(solution)/shard_map/all_to_all | solution.py:208
  25.8 0.0 copy-done.2
  25.8 0.0 copy-start.1
  25.9 4.9 %collective-permute-start.1 = (bf16[96,512]{1,0:T(8,128)(2,1)S(1)}, bf16[96,512]{1,0:T(8,128)(2,1)S(1)}, u32[]{:S(2)}, u32[]{:S(2)}) collective-permute-start(bf16[96,512]{1,0:T(8,128)(2,1)S(1)} %get-tuple-element.19), channel_id=1, source_target_pairs={{0,256},{128,384},{256,0},{384,128},{1,257},{129,385},{257,1},{385... | collective-permute-start | bytes 294920 | tf_op jit(solution)/shard_map/ppermute | solution.py:214
  30.8 3.1 %collective-permute-start.2 = (bf16[96,512]{1,0:T(8,128)(2,1)S(1)}, bf16[96,512]{1,0:T(8,128)(2,1)S(1)}, u32[]{:S(2)}, u32[]{:S(2)}) collective-permute-start(bf16[96,512]{1,0:T(8,128)(2,1)S(1)} %get-tuple-element.18), channel_id=1, source_target_pairs={{0,384},{128,0},{256,128},{384,256},{1,385},{129,1},{257,129},{385... | collective-permute-start | bytes 294920 | tf_op jit(solution)/shard_map/ppermute | solution.py:214
  33.9 2.8 %collective-permute-start = (bf16[96,512]{1,0:T(8,128)(2,1)S(1)}, bf16[96,512]{1,0:T(8,128)(2,1)S(1)}, u32[]{:S(2)}, u32[]{:S(2)}) collective-permute-start(bf16[96,512]{1,0:T(8,128)(2,1)S(1)} %get-tuple-element.20), channel_id=1, source_target_pairs={{0,128},{128,256},{256,384},{384,0},{1,129},{129,257},{257,385},{3... | collective-permute-start | bytes 294920 | tf_op jit(solution)/shard_map/ppermute | solution.py:214
  36.7 0.1 pad_add_fusion.place_ref
  36.7 0.0 collective-permute-done.1
  36.7 3.8 %collective-permute-done.2 = bf16[96,512]{1,0:T(8,128)(2,1)S(1)} collective-permute-done((bf16[96,512]{1,0:T(8,128)(2,1)S(1)}, bf16[96,512]{1,0:T(8,128)(2,1)S(1)}, u32[]{:S(2)}, u32[]{:S(2)}) %collective-permute-start.2) | collective-permute-done | bytes 98336 | tf_op jit(solution)/shard_map/ppermute | solution.py:214
  40.6 2.9 %collective-permute-done = bf16[96,512]{1,0:T(8,128)(2,1)S(1)} collective-permute-done((bf16[96,512]{1,0:T(8,128)(2,1)S(1)}, bf16[96,512]{1,0:T(8,128)(2,1)S(1)}, u32[]{:S(2)}, u32[]{:S(2)}) %collective-permute-start) | collective-permute-done | bytes 98336 | tf_op jit(solution)/shard_map/ppermute | solution.py:214
  43.4 0.1 pad_maximum_fusion
  43.5 2.4 %all-gather = bf16[8,96,512]{2,1,0:T(8,128)(2,1)S(1)} all-gather(bf16[4,96,512]{2,1,0:T(8,128)(2,1)S(1)} %pad_maximum_fusion), channel_id=2, replica_groups=mesh['x'=4,'core'=2,'z'=8,'y'=8] {'core'}, dimensions={0}, use_global_device_ids=true | all-gather | bytes 1179648 | tf_op jit(solution)/shard_map/all_gather | solution.py:215
  45.9 0.0 copy-done.1
  45.9 1.8 %shard_map.57 = (bf16[512,1280]{1,0:T(8,128)(2,1)S(1)}, bf16[512,512]{1,0:T(8,128)(2,1)S(1)}) custom-call(s32[1,256]{1,0:T(1,128)S(1)} %bitcast.27, s32[3]{0:T(128)S(1)} %pad_add_fusion.place_ref, bf16[2,4,96,512]{3,2,1,0:T(8,128)(2,1)S(1)} %bitcast.25), custom_call_target="tpu_custom_call" | custom-call | flops 402653184 | bytes 2097152 | tf_op jit(solution)/shard_map/pallas_call | solution.py:216
  47.7 16.5 %all-to-all-done.arrived_ref = bf16[512,2,640]{2,1,0:T(2,128)(2,1)S(1)} async-done(((bf16[512,2,640]{2,1,0:T(2,128)(2,1)}), bf16[512,2,640]{2,1,0:T(2,128)(2,1)S(1)}, u32[]{:S(2)}, u32[]{:S(2)}) %all-to-all-start) | async-done | bytes 1310752 | tf_op jit(solution)/shard_map/all_to_all | solution.py:208
  64.2 2.8 %shard_map.58 = bf16[512,2,256]{2,1,0:T(2,128)(2,1)} custom-call(bf16[512,2,640]{2,1,0:T(2,128)(2,1)S(1)} %all-to-all-done.arrived_ref, bf16[512,1280]{1,0:T(8,128)(2,1)S(1)} %get-tuple-element.15.weights_ref, bf16[512,512]{1,0:T(8,128)(2,1)S(1)} %get-tuple-element.16.parted_ref), custom_call_target="tpu_custom_call" | custom-call | flops 939524096 | bytes 2097152 | tf_op jit(solution)/shard_map/pallas_call | solution.py:227
  67.0 9.4 %all-to-all-start.1 = ((bf16[512,2,256]{2,1,0:T(2,128)(2,1)}), bf16[512,2,256]{2,1,0:T(2,128)(2,1)S(1)}, u32[]{:S(2)}, u32[]{:S(2)}) async-start(bf16[512,2,256]{2,1,0:T(2,128)(2,1)} %shard_map.58), calls=%async_computation.1 | async-start | bytes 1048576 | tf_op jit(solution)/shard_map/all_to_all | solution.py:234
  76.4 0.0 copy-start
  76.5 1.2 copy-done
  77.7 1.0 shard_map.55
  78.7 19.1 %all-to-all-done.1.right_ref = bf16[512,2,256]{2,1,0:T(2,128)(2,1)S(1)} async-done(((bf16[512,2,256]{2,1,0:T(2,128)(2,1)}), bf16[512,2,256]{2,1,0:T(2,128)(2,1)S(1)}, u32[]{:S(2)}, u32[]{:S(2)}) %all-to-all-start.1) | async-done | bytes 524320 | tf_op jit(solution)/shard_map/all_to_all | solution.py:234
  97.8 0.5 shard_map.59
  98.3 25.8 %all_to_all.15 = bf16[64,8,512]{2,1,0:T(8,128)(2,1)S(1)} all-to-all(bf16[64,8,512]{2,1,0:T(8,128)(2,1)S(1)} %bitcast.24), channel_id=1, replica_groups=mesh['x'=4,'core'=2,'z'=8,'y'=8] {'z','y'}, dimensions={0} | all-to-all | bytes 1048576 | tf_op jit(solution)/shard_map/all_to_all | solution.py:236
  124.1 0.9 copy.7
  (1 shorter events, 0.0 us)
Async XLA Ops:
  4.7 21.2 %copy-start.2 = (bf16[4,512,96]{1,2,0:T(8,128)(2,1)S(1)}, bf16[4,512,96]{1,2,0:T(8,128)(2,1)}, u32[]{:S(2)}) copy-start(bf16[4,512,96]{1,2,0:T(8,128)(2,1)} %param.6) | copy-start | bytes 1179652
  4.7 59.5 %all-to-all-start = ((bf16[512,2,640]{2,1,0:T(2,128)(2,1)}), bf16[512,2,640]{2,1,0:T(2,128)(2,1)S(1)}, u32[]{:S(2)}, u32[]{:S(2)}) async-start(bf16[512,2,640]{2,1,0:T(2,128)(2,1)} %shard_map.56), calls=%async_computation | async-start | bytes 2621440 | tf_op jit(solution)/shard_map/all_to_all | solution.py:208
  25.8 20.0 %copy-start.1 = (s32[256]{0:T(256)S(1)}, s32[256]{0:T(256)}, u32[]{:S(2)}) copy-start(s32[256]{0:T(256)} %param.7) | copy-start | bytes 3076
  25.9 10.8 %collective-permute-start.1 = (bf16[96,512]{1,0:T(8,128)(2,1)S(1)}, bf16[96,512]{1,0:T(8,128)(2,1)S(1)}, u32[]{:S(2)}, u32[]{:S(2)}) collective-permute-start(bf16[96,512]{1,0:T(8,128)(2,1)S(1)} %get-tuple-element.19), channel_id=1, source_target_pairs={{0,256},{128,384},{256,0},{384,128},{1,257},{129,385},{257,1},{385... | collective-permute-start | bytes 294920 | tf_op jit(solution)/shard_map/ppermute | solution.py:214
  30.8 9.8 %collective-permute-start.2 = (bf16[96,512]{1,0:T(8,128)(2,1)S(1)}, bf16[96,512]{1,0:T(8,128)(2,1)S(1)}, u32[]{:S(2)}, u32[]{:S(2)}) collective-permute-start(bf16[96,512]{1,0:T(8,128)(2,1)S(1)} %get-tuple-element.18), channel_id=1, source_target_pairs={{0,384},{128,0},{256,128},{384,256},{1,385},{129,1},{257,129},{385... | collective-permute-start | bytes 294920 | tf_op jit(solution)/shard_map/ppermute | solution.py:214
  33.9 9.6 %collective-permute-start = (bf16[96,512]{1,0:T(8,128)(2,1)S(1)}, bf16[96,512]{1,0:T(8,128)(2,1)S(1)}, u32[]{:S(2)}, u32[]{:S(2)}) collective-permute-start(bf16[96,512]{1,0:T(8,128)(2,1)S(1)} %get-tuple-element.20), channel_id=1, source_target_pairs={{0,128},{128,256},{256,384},{384,0},{1,129},{129,257},{257,385},{3... | collective-permute-start | bytes 294920 | tf_op jit(solution)/shard_map/ppermute | solution.py:214
  67.0 30.8 %all-to-all-start.1 = ((bf16[512,2,256]{2,1,0:T(2,128)(2,1)}), bf16[512,2,256]{2,1,0:T(2,128)(2,1)S(1)}, u32[]{:S(2)}, u32[]{:S(2)}) async-start(bf16[512,2,256]{2,1,0:T(2,128)(2,1)} %shard_map.58), calls=%async_computation.1 | async-start | bytes 1048576 | tf_op jit(solution)/shard_map/all_to_all | solution.py:234
  76.4 1.2 copy-start

commit v6 on v4

--- a/solution.py
+++ b/solution.py
@@ -80,7 +80,7 @@
         copy.wait()
 
 
-def legendre_kernel(assign_ref, place_ref, same_ref, crossed_ref, out_ref, parted_ref):
+def legendre_kernel(assign_ref, place_ref, legendre_ref, out_ref, parted_ref):
     order = jnp.sum(jnp.where(iota((1, 256), 1) == place_ref[0], assign_ref[...], 0), axis=1, keepdims=True)
     row = iota((512, 1), 0)
     core, x = (row >> 5) & 1, row & 3
@@ -88,15 +88,14 @@
     degree = (2 * x + core) * 64 + inner
     column = iota((512, 512), 1)
     kept = jnp.where((column == degree) & (degree >= order), 1.0, 0.0).astype(BF)
-    x_here, straight = place_ref[2], place_ref[3] == 0
+    x_here, zl = place_ref[2], place_ref[3]
     for h in range(3):
         rows = pl.ds(h * 32, 32)
         for core_from in range(2):
-            pieces = []
-            for x_from in range(4):
-                at = (x_here - x_from) & 3
-                near, far = same_ref[at, rows, :], crossed_ref[at, rows, :]
-                pieces.append(jnp.where(straight == (core_from == 0), near, far))
+            cross = (zl + core_from) & 1
+            pieces = [
+                legendre_ref[((x_here - x_from) & 3) * 2 + cross, rows, :] for x_from in range(4)
+            ]
             at = h * 256 + core_from * 128
             out_ref[:, at : at + 128] = nt_dot(kept, jnp.concatenate(pieces, axis=0)).astype(BF)
     out_ref[:, 768:1280] = jnp.where(column == core * 256 + x * 64 + inner, 2.0, 0.0).astype(BF)
@@ -212,16 +211,18 @@
     arrived = lax.all_to_all(sent, ("core", "x", "zh", "y"), 0, 0, tiled=True)
 
     by_order = legendre.transpose(0, 2, 1)
-    rolled = jnp.take(by_order, (x + jnp.arange(4)) % 4, axis=0)
-    two_on = lax.ppermute(rolled[2:], "x", [(i, (i + 2) % 4) for i in range(4)])
-    one_on = jnp.stack([rolled[1], two_on[1]])
-    one_on = lax.ppermute(one_on, "x", [(i, (i + 1) % 4) for i in range(4)])
-    gathered = jnp.stack([rolled[0], one_on[0], two_on[0], one_on[1]])
-    same = lax.ppermute(gathered, ("core", "zl"), [(0, 0), (1, 2), (2, 1), (3, 3)])
-    crossed = lax.ppermute(gathered, ("core", "zl"), [(0, 1), (1, 3), (2, 0), (3, 2)])
+    pieces = []
+    for shift in range(4):
+        mine = lax.dynamic_index_in_dim(by_order, (x + shift) % 4, 0, keepdims=False)
+        for cross in range(2):
+            pairs = [
+                (i, (i // 4 + shift) % 4 * 4 + i % 2 * 2 + (i // 2 % 2 ^ cross)) for i in range(16)
+            ]
+            pieces.append(lax.ppermute(mine, ("x", "core", "zl"), pairs))
+    whole = jnp.stack(pieces)
     weights, parted = call(
-        legendre_kernel, (bf16(512, 1280), bf16(512, 512)), [VMEM, SMEM, VMEM, VMEM], (), 2 * 512 * 512 * 768
-    )(orders, place, same, crossed)
+        legendre_kernel, (bf16(512, 1280), bf16(512, 512)), [VMEM, SMEM, VMEM], (), 2 * 512 * 512 * 768
+    )(orders, place, whole)
     solver, valid = call(
         inverse_kernel,
         (bf16(2, 512, 256), jax.ShapeDtypeStruct((8, 512), F32)),

time: 142 us -> 142 us (level)
  starting transfers between devices: 51.9 us -> 78.4 us
  waiting for transfers between devices: 45.3 us -> 23.1 us
  local copies, waits for them, and re-layouts: 6.3 us -> 2.28 us
    ppermute x4 -> x8, starting transfers between devices: 13.5 us -> 38.2 us  [shards(): pieces.append(lax.ppermute(mine, ('x', 'core', 'zl'), pairs))]
    ppermute x4 -> x8, waiting for transfers between devices: 27 us -> 4.7 us  [shards(): pieces.append(lax.ppermute(mine, ('x', 'core', 'zl'), pairs))]
    unnamed x14 -> x13, local copies, waits for them, and re-layouts: 4.72 us -> 1.29 us
    all_to_all x1, starting transfers between devices: 17.2 us -> 18.7 us  [shards(): lax.all_to_all(right, ('zl', 'zh', 'core', 'y', 'x'), 0, 0, tiled=True)]
  transfers between devices with their start and end apart: 6 -> 10, of which waited for: 4 -> 4; matrix products, arithmetic and copies ran while one was open for 1% -> 0% of each run, Pallas kernels for 2% -> 2%
where the time goes in v6:
time: 142 us; the launch traced here: 141 us
  starting transfers between devices  78.4 us (55%)
  blocking collectives  26.4 us (19%)
  waiting for transfers between devices  23.1 us (16%)
  Pallas kernels  10.7 us (8%)
  local copies, waits for them, and re-layouts  2.28 us (2%)
    ppermute x8, starting transfers between devices, shards(): pieces.append(lax.ppermute(mine, ('x', 'core', 'zl'), pairs))  38.2 us
    all_to_all x1, blocking collectives, shards(): out = lax.all_to_all(solved.reshape(64, 8, 512), RAD, 0, 0, tiled=True)  26.4 us
    all_to_all x1, starting transfers between devices, shards(): arrived = lax.all_to_all(sent, ('core', 'x', 'zh', 'y'), 0, 0, tiled=True)  21.5 us
    all_to_all x1, starting transfers between devices, shards(): lax.all_to_all(right, ('zl', 'zh', 'core', 'y', 'x'), 0, 0, tiled=True)  18.7 us
    all_to_all x1, waiting for transfers between devices, shards(): lax.all_to_all(right, ('zl', 'zh', 'core', 'y', 'x'), 0, 0, tiled=True)  18.4 us
    ppermute x8, waiting for transfers between devices, shards(): pieces.append(lax.ppermute(mine, ('x', 'core', 'zl'), pairs))  4.7 us
    pallas_call x1, Pallas kernels, shards(): call(fourier_kernel, bf16(256, 2, 1280), [VMEM, HBM, HBM], [pltpu.VMEM((8...  4.55 us
  transfers between devices with their start and end apart: 10, of which 4 were waited for; matrix products, arithmetic and copies ran while one was open for 0% of the time, Pallas kernels for 2%

profile of v6, /device:TPU:8, one launch (start us, length us, event | category | flops | bytes accessed | tf_op | source)
XLA Modules:
  0.0 141.3 jit_solution(7587125621770301052)
XLA Ops:
  0.0 4.6 %shard_map.56 = bf16[256,2,1280]{2,1,0:T(2,128)(2,1)} custom-call(s32[1,256]{1,0:T(1,128)} %bitcast.40, bf16[8,96,1024]{2,1,0:T(8,128)(2,1)} %forcing_hbm.1, bf16[8,64,512]{2,1,0:T(8,128)(2,1)} %previous_hbm.1), custom_call_target="tpu_custom_call" | custom-call | flops 805306368 | bytes 2097152 | tf_op jit(solution)/shard_map/pallas_call | solution.py:194
  4.6 0.0 copy-start.2
  4.6 21.5 %all-to-all-start = ((bf16[256,2,1280]{2,1,0:T(2,128)(2,1)}), bf16[256,2,1280]{2,1,0:T(2,128)(2,1)S(1)}, u32[]{:S(2)}, u32[]{:S(2)}) async-start(bf16[256,2,1280]{2,1,0:T(2,128)(2,1)} %shard_map.56), calls=%async_computation | async-start | bytes 2621440 | tf_op jit(solution)/shard_map/all_to_all | solution.py:211
  26.0 0.0 copy-start.1
  26.1 0.0 copy-done.2
  26.2 0.7 collective-permute-start
  26.8 5.7 %collective-permute-start.1 = (bf16[96,512]{1,0:T(8,128)(2,1)S(1)}, bf16[96,512]{1,0:T(8,128)(2,1)S(1)}, u32[]{:S(2)}, u32[]{:S(2)}) collective-permute-start(bf16[96,512]{1,0:T(8,128)(2,1)S(1)} %get-tuple-element.20), channel_id=1, source_target_pairs={{0,8},{8,72},{64,0},{72,64},{128,136},{136,200},{192,128},{200,192... | collective-permute-start | bytes 294920 | tf_op jit(solution)/shard_map/ppermute | solution.py:221
  32.5 3.6 %collective-permute-start.2 = (bf16[96,512]{1,0:T(8,128)(2,1)S(1)}, bf16[96,512]{1,0:T(8,128)(2,1)S(1)}, u32[]{:S(2)}, u32[]{:S(2)}) collective-permute-start(bf16[96,512]{1,0:T(8,128)(2,1)S(1)} %get-tuple-element.19), channel_id=1, source_target_pairs={{0,128},{8,192},{64,136},{72,200},{128,256},{136,320},{192,264},{2... | collective-permute-start | bytes 294920 | tf_op jit(solution)/shard_map/ppermute | solution.py:221
  36.1 3.1 %collective-permute-start.3 = (bf16[96,512]{1,0:T(8,128)(2,1)S(1)}, bf16[96,512]{1,0:T(8,128)(2,1)S(1)}, u32[]{:S(2)}, u32[]{:S(2)}) collective-permute-start(bf16[96,512]{1,0:T(8,128)(2,1)S(1)} %get-tuple-element.19), channel_id=1, source_target_pairs={{0,136},{8,200},{64,128},{72,192},{128,264},{136,328},{192,256},{2... | collective-permute-start | bytes 294920 | tf_op jit(solution)/shard_map/ppermute | solution.py:221
  39.2 3.9 %collective-permute-start.4 = (bf16[96,512]{1,0:T(8,128)(2,1)S(1)}, bf16[96,512]{1,0:T(8,128)(2,1)S(1)}, u32[]{:S(2)}, u32[]{:S(2)}) collective-permute-start(bf16[96,512]{1,0:T(8,128)(2,1)S(1)} %get-tuple-element.18), channel_id=1, source_target_pairs={{0,256},{8,320},{64,264},{72,328},{128,384},{136,448},{192,392},{2... | collective-permute-start | bytes 294920 | tf_op jit(solution)/shard_map/ppermute | solution.py:221
  43.1 0.1 pad_add_fusion.place_ref
  43.2 0.0 collective-permute-done
  43.2 16.4 %collective-permute-start.5 = (bf16[96,512]{1,0:T(8,128)(2,1)S(1)}, bf16[96,512]{1,0:T(8,128)(2,1)S(1)}, u32[]{:S(2)}, u32[]{:S(2)}) collective-permute-start(bf16[96,512]{1,0:T(8,128)(2,1)S(1)} %get-tuple-element.18), channel_id=1, source_target_pairs={{0,264},{8,328},{64,256},{72,320},{128,392},{136,456},{192,384},{2... | collective-permute-start | bytes 294920 | tf_op jit(solution)/shard_map/ppermute | solution.py:221
  59.6 0.0 collective-permute-done.1
  59.6 2.9 %collective-permute-start.6 = (bf16[96,512]{1,0:T(8,128)(2,1)S(1)}, bf16[96,512]{1,0:T(8,128)(2,1)S(1)}, u32[]{:S(2)}, u32[]{:S(2)}) collective-permute-start(bf16[96,512]{1,0:T(8,128)(2,1)S(1)} %get-tuple-element.17), channel_id=1, source_target_pairs={{0,384},{8,448},{64,392},{72,456},{128,0},{136,64},{192,8},{200,72... | collective-permute-start | bytes 294920 | tf_op jit(solution)/shard_map/ppermute | solution.py:221
  62.5 0.0 collective-permute-done.2
  62.5 2.1 %collective-permute-start.7 = (bf16[96,512]{1,0:T(8,128)(2,1)S(1)}, bf16[96,512]{1,0:T(8,128)(2,1)S(1)}, u32[]{:S(2)}, u32[]{:S(2)}) collective-permute-start(bf16[96,512]{1,0:T(8,128)(2,1)S(1)} %get-tuple-element.17), channel_id=1, source_target_pairs={{0,392},{8,456},{64,384},{72,448},{128,8},{136,72},{192,0},{200,64... | collective-permute-start | bytes 294920 | tf_op jit(solution)/shard_map/ppermute | solution.py:221
  64.6 0.0 collective-permute-done.3
  64.7 0.0 collective-permute-done.4
  64.7 0.5 collective-permute-done.5
  65.2 0.9 collective-permute-done.6
  66.2 3.2 %collective-permute-done.7 = bf16[96,512]{1,0:T(8,128)(2,1)S(1)} collective-permute-done((bf16[96,512]{1,0:T(8,128)(2,1)S(1)}, bf16[96,512]{1,0:T(8,128)(2,1)S(1)}, u32[]{:S(2)}, u32[]{:S(2)}) %collective-permute-start.7) | collective-permute-done | bytes 98336 | tf_op jit(solution)/shard_map/ppermute | solution.py:221
  69.4 0.0 copy-done.1
  69.4 1.9 %shard_map.57 = (bf16[512,1280]{1,0:T(8,128)(2,1)S(1)}, bf16[512,512]{1,0:T(8,128)(2,1)S(1)}) custom-call(s32[1,256]{1,0:T(1,128)S(1)} %bitcast.41, s32[4]{0:T(128)S(1)} %pad_add_fusion.place_ref, bf16[8,96,512]{2,1,0:T(8,128)(2,1)S(1)} %bitcast_dynamic-update-slice_fusion.legendre_ref), custom_call_target="tpu_custom_call" | custom-call | flops 402653184 | bytes 2097152 | tf_op jit(solution)/shard_map/pallas_call | solution.py:223
  71.3 0.0 all-to-all-done.arrived_ref
  71.3 2.8 %shard_map.58 = bf16[512,2,256]{2,1,0:T(2,128)(2,1)} custom-call(bf16[256,2,1280]{2,1,0:T(2,128)(2,1)S(1)} %all-to-all-done.arrived_ref, bf16[512,1280]{1,0:T(8,128)(2,1)S(1)} %get-tuple-element.15.weights_ref, bf16[512,512]{1,0:T(8,128)(2,1)S(1)} %get-tuple-element.16.parted_ref), custom_call_target="tpu_custom_call" | custom-call | flops 939524096 | bytes 2097152 | tf_op jit(solution)/shard_map/pallas_call | solution.py:234
  74.0 18.7 %all-to-all-start.1 = ((bf16[512,2,256]{2,1,0:T(2,128)(2,1)}), bf16[512,2,256]{2,1,0:T(2,128)(2,1)S(1)}, u32[]{:S(2)}, u32[]{:S(2)}) async-start(bf16[512,2,256]{2,1,0:T(2,128)(2,1)} %shard_map.58), calls=%async_computation.1 | async-start | bytes 1048576 | tf_op jit(solution)/shard_map/all_to_all | solution.py:241
  92.8 0.0 copy-start
  92.8 1.2 copy-done
  94.0 1.0 shard_map.55
  95.0 18.4 %all-to-all-done.1.right_ref = bf16[512,2,256]{2,1,0:T(2,128)(2,1)S(1)} async-done(((bf16[512,2,256]{2,1,0:T(2,128)(2,1)}), bf16[512,2,256]{2,1,0:T(2,128)(2,1)S(1)}, u32[]{:S(2)}, u32[]{:S(2)}) %all-to-all-start.1) | async-done | bytes 524320 | tf_op jit(solution)/shard_map/all_to_all | solution.py:241
  113.4 0.5 shard_map.59
  113.9 26.4 %all_to_all.15 = bf16[64,8,512]{2,1,0:T(8,128)(2,1)S(1)} all-to-all(bf16[64,8,512]{2,1,0:T(8,128)(2,1)S(1)} %bitcast.39), channel_id=1, replica_groups=mesh['x'=4,'core'=2,'zh'=4,'zl'=2,'y'=8] {'zh','zl','y'}, dimensions={0} | all-to-all | bytes 1048576 | tf_op jit(solution)/shard_map/all_to_all | solution.py:243
  140.3 0.9 copy.7
  (9 shorter events, 0.1 us)
Async XLA Ops:
  4.6 21.6 %copy-start.2 = (bf16[4,512,96]{1,2,0:T(8,128)(2,1)S(1)}, bf16[4,512,96]{1,2,0:T(8,128)(2,1)}, u32[]{:S(2)}) copy-start(bf16[4,512,96]{1,2,0:T(8,128)(2,1)} %param.6) | copy-start | bytes 1179652
  4.6 66.7 %all-to-all-start = ((bf16[256,2,1280]{2,1,0:T(2,128)(2,1)}), bf16[256,2,1280]{2,1,0:T(2,128)(2,1)S(1)}, u32[]{:S(2)}, u32[]{:S(2)}) async-start(bf16[256,2,1280]{2,1,0:T(2,128)(2,1)} %shard_map.56), calls=%async_computation | async-start | bytes 2621440 | tf_op jit(solution)/shard_map/all_to_all | solution.py:211
  26.0 43.4 %copy-start.1 = (s32[256]{0:T(256)S(1)}, s32[256]{0:T(256)}, u32[]{:S(2)}) copy-start(s32[256]{0:T(256)} %param.7) | copy-start | bytes 3076
  26.2 17.0 %collective-permute-start = (bf16[96,512]{1,0:T(8,128)(2,1)S(1)}, bf16[96,512]{1,0:T(8,128)(2,1)S(1)}, u32[]{:S(2)}, u32[]{:S(2)}) collective-permute-start(bf16[96,512]{1,0:T(8,128)(2,1)S(1)} %get-tuple-element.20), channel_id=1, source_target_pairs={{0,0},{8,64},{64,8},{72,72},{128,128},{136,192},{192,136},{200,200... | collective-permute-start | bytes 294920 | tf_op jit(solution)/shard_map/ppermute | solution.py:221
  26.8 32.8 %collective-permute-start.1 = (bf16[96,512]{1,0:T(8,128)(2,1)S(1)}, bf16[96,512]{1,0:T(8,128)(2,1)S(1)}, u32[]{:S(2)}, u32[]{:S(2)}) collective-permute-start(bf16[96,512]{1,0:T(8,128)(2,1)S(1)} %get-tuple-element.20), channel_id=1, source_target_pairs={{0,8},{8,72},{64,0},{72,64},{128,136},{136,200},{192,128},{200,192... | collective-permute-start | bytes 294920 | tf_op jit(solution)/shard_map/ppermute | solution.py:221
  32.5 30.0 %collective-permute-start.2 = (bf16[96,512]{1,0:T(8,128)(2,1)S(1)}, bf16[96,512]{1,0:T(8,128)(2,1)S(1)}, u32[]{:S(2)}, u32[]{:S(2)}) collective-permute-start(bf16[96,512]{1,0:T(8,128)(2,1)S(1)} %get-tuple-element.19), channel_id=1, source_target_pairs={{0,128},{8,192},{64,136},{72,200},{128,256},{136,320},{192,264},{2... | collective-permute-start | bytes 294920 | tf_op jit(solution)/shard_map/ppermute | solution.py:221
  36.1 28.5 %collective-permute-start.3 = (bf16[96,512]{1,0:T(8,128)(2,1)S(1)}, bf16[96,512]{1,0:T(8,128)(2,1)S(1)}, u32[]{:S(2)}, u32[]{:S(2)}) collective-permute-start(bf16[96,512]{1,0:T(8,128)(2,1)S(1)} %get-tuple-element.19), channel_id=1, source_target_pairs={{0,136},{8,200},{64,128},{72,192},{128,264},{136,328},{192,256},{2... | collective-permute-start | bytes 294920 | tf_op jit(solution)/shard_map/ppermute | solution.py:221
  39.2 25.5 %collective-permute-start.4 = (bf16[96,512]{1,0:T(8,128)(2,1)S(1)}, bf16[96,512]{1,0:T(8,128)(2,1)S(1)}, u32[]{:S(2)}, u32[]{:S(2)}) collective-permute-start(bf16[96,512]{1,0:T(8,128)(2,1)S(1)} %get-tuple-element.18), channel_id=1, source_target_pairs={{0,256},{8,320},{64,264},{72,328},{128,384},{136,448},{192,392},{2... | collective-permute-start | bytes 294920 | tf_op jit(solution)/shard_map/ppermute | solution.py:221
  43.2 22.1 %collective-permute-start.5 = (bf16[96,512]{1,0:T(8,128)(2,1)S(1)}, bf16[96,512]{1,0:T(8,128)(2,1)S(1)}, u32[]{:S(2)}, u32[]{:S(2)}) collective-permute-start(bf16[96,512]{1,0:T(8,128)(2,1)S(1)} %get-tuple-element.18), channel_id=1, source_target_pairs={{0,264},{8,328},{64,256},{72,320},{128,392},{136,456},{192,384},{2... | collective-permute-start | bytes 294920 | tf_op jit(solution)/shard_map/ppermute | solution.py:221
  59.6 6.5 %collective-permute-start.6 = (bf16[96,512]{1,0:T(8,128)(2,1)S(1)}, bf16[96,512]{1,0:T(8,128)(2,1)S(1)}, u32[]{:S(2)}, u32[]{:S(2)}) collective-permute-start(bf16[96,512]{1,0:T(8,128)(2,1)S(1)} %get-tuple-element.17), channel_id=1, source_target_pairs={{0,384},{8,448},{64,392},{72,456},{128,0},{136,64},{192,8},{200,72... | collective-permute-start | bytes 294920 | tf_op jit(solution)/shard_map/ppermute | solution.py:221
  62.5 6.9 %collective-permute-start.7 = (bf16[96,512]{1,0:T(8,128)(2,1)S(1)}, bf16[96,512]{1,0:T(8,128)(2,1)S(1)}, u32[]{:S(2)}, u32[]{:S(2)}) collective-permute-start(bf16[96,512]{1,0:T(8,128)(2,1)S(1)} %get-tuple-element.17), channel_id=1, source_target_pairs={{0,392},{8,456},{64,384},{72,448},{128,8},{136,72},{192,0},{200,64... | collective-permute-start | bytes 294920 | tf_op jit(solution)/shard_map/ppermute | solution.py:221
  74.0 39.3 %all-to-all-start.1 = ((bf16[512,2,256]{2,1,0:T(2,128)(2,1)}), bf16[512,2,256]{2,1,0:T(2,128)(2,1)S(1)}, u32[]{:S(2)}, u32[]{:S(2)}) async-start(bf16[512,2,256]{2,1,0:T(2,128)(2,1)} %shard_map.58), calls=%async_computation.1 | async-start | bytes 1048576 | tf_op jit(solution)/shard_map/all_to_all | solution.py:241
  92.8 1.2 copy-start

commit v7 on v5

v7 whole, which is shorter than its diff:
```python
import math

import jax
import jax.numpy as jnp
from jax import lax
from jax.experimental import pallas as pl
from jax.experimental.pallas import tpu as pltpu
from jax.sharding import Mesh, PartitionSpec as P

NR = 512
L = 512
LON = 1024
BF = jnp.bfloat16
F32 = jnp.float32
RAD = ("z", "y")
LAT = ("x", "core")


def nt_dot(a, b):
    return lax.dot_general(a, b, (((1,), (1,)), ((), ())), preferred_element_type=F32)


def iota(shape, dim):
    return lax.broadcasted_iota(jnp.int32, shape, dim)


def cos_sin(phase):
    quadrant = ((phase + 128) >> 8) & 3
    rest = ((phase + 128) & 255) - 128
    x = rest.astype(F32) * (2.0 * math.pi / LON)
    x2 = x * x
    sin_x = x * (1.0 + x2 * (-1.0 / 6 + x2 * (1.0 / 120 + x2 * (-1.0 / 5040 + x2 * (1.0 / 362880)))))
    cos_x = 1.0 + x2 * (-0.5 + x2 * (1.0 / 24 + x2 * (-1.0 / 720 + x2 * (1.0 / 40320))))
    swap = (quadrant & 1) == 1
    cos_part = jnp.where(swap, sin_x, cos_x)
    sin_part = jnp.where(swap, cos_x, sin_x)
    cos_sign = jnp.where((quadrant == 1) | (quadrant == 2), -1.0, 1.0)
    sin_sign = jnp.where(quadrant >= 2, -1.0, 1.0)
    return cos_part * cos_sign, sin_part * sin_sign


def fourier_kernel(
    assign_ref, forcing_hbm, previous_hbm, out_hbm, forcing_ref, previous_ref, table_ref, out_ref, in_sems, out_sems
):
    previous_copy = pltpu.make_async_copy(previous_hbm, previous_ref, in_sems.at[1])
    previous_copy.start()
    forcing_copy = pltpu.make_async_copy(forcing_hbm, forcing_ref, in_sems.at[0])
    forcing_copy.start()
    row = iota((512, 1), 0)
    slot = ((row >> 1) & 63) * 4 + (row >> 7)
    orders = jnp.sum(jnp.where(iota((512, 256), 1) == slot, assign_ref[...], 0), axis=1, keepdims=True)
    lane = iota((512, 128), 1)
    cos_now, sin_now = cos_sin((orders * lane + (row & 1) * (LON // 4)) & (LON - 1))
    cos_half, sin_half = cos_now[:, 64:65], sin_now[:, 64:65]
    sign = (1 - 2 * (row & 1)).astype(F32)
    cos_step = jnp.broadcast_to(sign * (1.0 - 2.0 * sin_half * sin_half), (512, 128))
    sin_step = jnp.broadcast_to(sign * (2.0 * sin_half * cos_half), (512, 128))
    cos_now, sin_now = cos_now * LON**-0.5, sin_now * LON**-0.5
    for q in range(LON // 128):
        table_ref[:, q * 128 : q * 128 + 128] = cos_now.astype(BF)
        cos_now, sin_now = cos_now * cos_step - sin_now * sin_step, sin_now * cos_step + cos_now * sin_step
    table = table_ref[...]
    reorder = (iota((512, 512), 1) == slot * 2 + (row & 1)).astype(BF)
    previous_copy.wait()
    previous = previous_ref[...].reshape(512, 512)
    forcing_copy.wait()
    out_copies = []
    for block in range(2):
        rows = slice(block * 256, block * 256 + 256)
        parts = []
        for h in range(3):
            part = forcing_ref[:, h * 32 : h * 32 + 32, :].reshape(256, LON)
            parts.append(nt_dot(table[rows], part).astype(BF))
        parts.append(nt_dot(reorder[rows], previous).astype(BF))
        dests = pl.ds(block * 128, 128)
        out_ref[dests] = jnp.concatenate(parts, axis=1).reshape(128, 2, 1280)
        copy = pltpu.make_async_copy(out_ref.at[dests], out_hbm.at[dests], out_sems.at[block])
        copy.start()
        out_copies.append(copy)
    for copy in out_copies:
        copy.wait()


def legendre_kernel(assign_ref, place_ref, legendre_ref, own_ref, other_ref):
    order = jnp.sum(jnp.where(iota((1, 256), 1) == place_ref[0], assign_ref[...], 0), axis=1, keepdims=True)
    x_here, core = place_ref[2], place_ref[3]
    row, column = iota((256, 1), 0), iota((256, 512), 1)
    x, rad = row & 3, row >> 2
    kept = []
    for of_core in (core, 1 - core):
        degree = (2 * x + of_core) * 64 + rad
        kept.append(jnp.where((column == degree) & (degree >= order), 1.0, 0.0).astype(BF))
    for h in range(3):
        pieces = [legendre_ref[(x_here - x_from) & 3, h * 32 : h * 32 + 32, :] for x_from in range(4)]
        pieces = jnp.concatenate(pieces, axis=0)
        own_ref[:, h * 128 : h * 128 + 128] = nt_dot(kept[0], pieces).astype(BF)
        other_ref[:, h * 128 : h * 128 + 128] = nt_dot(kept[1], pieces).astype(BF)
    own_ref[:, 384:640] = jnp.where(iota((256, 256), 1) == x * 64 + rad, 2.0, 0.0).astype(BF)


def roll(a, shift):
    return pltpu.roll(a, shift, 1)


def spectrum_kernel(arrived_ref, weights_ref, gathered_ref, out_ref, rows_ref):
    rows_ref[...] = arrived_ref[...].reshape(512, 1280)
    lane = iota((128, 128), 1)
    low_half = lane < 64
    even_quarter = (lane & 32) == 0

    def tile(block, at):
        return rows_ref[block * 128 : block * 128 + 128, at : at + 128].astype(F32)

    def place(rho, at, value):
        gathered_ref[rho * 128 : rho * 128 + 128, at : at + 128] = value.astype(BF)

    for h in range(3):
        for high in range(2):
            a = [tile(x, h * 256 + high * 128) for x in range(4)]
            b0 = jnp.where(low_half, a[0], roll(a[2], 64))
            b2 = jnp.where(low_half, roll(a[0], 64), a[2])
            b1 = jnp.where(low_half, a[1], roll(a[3], 64))
            b3 = jnp.where(low_half, roll(a[1], 64), a[3])
            at, rho = h * 128, high * 4
            place(rho, at, jnp.where(even_quarter, b0, roll(b1, 32)))
            place(rho + 1, at, jnp.where(even_quarter, roll(b0, 96), b1))
            place(rho + 2, at, jnp.where(even_quarter, b2, roll(b3, 32)))
            place(rho + 3, at, jnp.where(even_quarter, roll(b2, 96), b3))
    out_ref[...] = nt_dot(weights_ref[...], gathered_ref[:, :384]).astype(BF)
    for pair in range(4):
        for two in range(2):
            at = 768 + pair * 128
            a0, a1 = tile(two * 2, at), tile(two * 2 + 1, at)
            to = 384 + two * 128
            place(pair * 2, to, jnp.where(low_half, a0, roll(a1, 64)))
            place(pair * 2 + 1, to, jnp.where(low_half, roll(a0, 64), a1))


def own_kernel(gathered_ref, weights_ref, out_ref):
    out_ref[...] = nt_dot(weights_ref[...], gathered_ref[...])


def right_kernel(own_ref, received_ref, out_ref):
    right = (own_ref[...] + received_ref[...].astype(F32)).astype(BF)
    row, column = iota((256, 256), 0), iota((256, 256), 1)
    parted = (column == (row & 1) * 128 + (row >> 1)).astype(BF)
    parts = []
    for i in range(4):
        part = right[:, i * 256 : i * 256 + 256]
        parts.append(jnp.dot(part, parted, preferred_element_type=F32).astype(BF))
    parts = [part[:, :128] for part in parts] + [part[:, 128:] for part in parts]
    out_ref[...] = jnp.concatenate(parts, axis=1).reshape(256, 2, 512)


def inverse_kernel(assign_ref, place_ref, inverse_ref, out_ref, valid_ref):
    row, column = iota((512, 1), 0), iota((512, 512), 1)
    regroup = (column == (row & 63) * 8 + (row >> 6)).astype(BF)
    out_ref[...] = nt_dot(inverse_ref[0].astype(BF), regroup).astype(BF)
    valid = jnp.where(assign_ref[...] <= place_ref[1], 1.0, 0.0)
    row, column = iota((256, 512), 0), iota((256, 512), 1)
    doubled = (row == (column >> 1)).astype(BF)
    valid_ref[...] = jnp.dot(
        jnp.broadcast_to(valid, (8, 256)).astype(BF), doubled, preferred_element_type=F32
    )


def solve_kernel(valid_ref, inverse_ref, right_ref, out_ref):
    solved = nt_dot(inverse_ref[...], right_ref[...].reshape(512, 512))
    out_ref[...] = (solved * (valid_ref[0:1, :] * 0.5)).astype(BF)


VMEM = pl.BlockSpec(memory_space=pltpu.VMEM)
SMEM = pl.BlockSpec(memory_space=pltpu.SMEM)
HBM = pl.BlockSpec(memory_space=pltpu.HBM)


def call(kernel, out, ins, scratch=(), flops=0, vmem=24, outs=None):
    return pl.pallas_call(
        kernel,
        out_shape=out,
        in_specs=ins,
        out_specs=outs or jax.tree.map(lambda _: VMEM, out),
        scratch_shapes=list(scratch),
        compiler_params=pltpu.CompilerParams(vmem_limit_bytes=vmem * 1024 * 1024),
        cost_estimate=pl.CostEstimate(flops=flops, bytes_accessed=2 * 1024 * 1024, transcendentals=0),
    )


def bf16(*shape):
    return jax.ShapeDtypeStruct(shape, BF)


def shards(forcing, legendre, assign, inverse, previous):
    x, core, rad = lax.axis_index("x"), lax.axis_index("core"), lax.axis_index(RAD)
    orders = assign.reshape(1, 256)
    place = jnp.stack([rad * 4 + x, (x * 2 + core) * 64 + rad, x, core]).astype(jnp.int32)

    sent = call(
        fourier_kernel,
        bf16(256, 2, 1280),
        [VMEM, HBM, HBM],
        [
            pltpu.VMEM((8, 96, LON), BF),
            pltpu.VMEM((8, 64, 512), BF),
            pltpu.VMEM((512, LON), BF),
            pltpu.VMEM((256, 2, 1280), BF),
            pltpu.SemaphoreType.DMA((2,)),
            pltpu.SemaphoreType.DMA((2,)),
        ],
        2 * 512 * 768 * 1024,
        60,
        HBM,
    )(orders, forcing, previous)
    sent, legendre = lax.optimization_barrier((sent, legendre))
    arrived = lax.all_to_all(sent, ("x",) + RAD, 0, 0, tiled=True)

    by_order = legendre.transpose(0, 2, 1)
    pieces = [lax.dynamic_index_in_dim(by_order, x, 0, keepdims=False)]
    for shift in range(1, 4):
        mine = lax.dynamic_index_in_dim(by_order, (x + shift) % 4, 0, keepdims=False)
        pieces.append(lax.ppermute(mine, "x", [(i, (i + shift) % 4) for i in range(4)]))
    own_weights, other_weights = call(
        legendre_kernel, (bf16(256, 640), bf16(256, 384)), [VMEM, SMEM, VMEM], (), 2 * 512 * 512 * 384
    )(orders, place, jnp.stack(pieces))
    solver, valid = call(
        inverse_kernel,
        (bf16(512, 512), jax.ShapeDtypeStruct((8, 512), F32)),
        [VMEM, SMEM, VMEM],
        (),
        2 * 512**3,
    )(orders, place, inverse)

    gathered, other = call(
        spectrum_kernel,
        (bf16(1024, 640), bf16(256, 1024)),
        [VMEM] * 2,
        [pltpu.VMEM((512, 1280), BF)],
        2 * 256 * 384 * 1024,
    )(arrived, other_weights)
    received = lax.ppermute(other, "core", [(0, 1), (1, 0)])
    own = call(own_kernel, jax.ShapeDtypeStruct((256, 1024), F32), [VMEM] * 2, (), 2 * 256 * 640 * 1024)(
        gathered, own_weights
    )
    right = call(right_kernel, bf16(256, 2, 512), [VMEM] * 2, (), 2 * 256 * 256 * 1024)(own, received)
    right = lax.all_to_all(right, RAD + ("x",), 0, 0, tiled=True)
    solved = call(solve_kernel, bf16(512, 512), [VMEM] * 3, (), 2 * 512**3)(valid, solver, right)
    out = lax.all_to_all(solved.reshape(64, 8, 512), RAD, 0, 0, tiled=True)
    return out.transpose(1, 0, 2)


def solution(mesh):
    split = Mesh(mesh.devices.reshape(4, 2, 8, 8), LAT + RAD)
    placed = (
        P(RAD, LAT, None),
        P(RAD, None, LAT),
        P(),
        P(LAT + RAD, None, None),
        P(RAD, LAT, None),
    )
    return jax.shard_map(shards, mesh=split, in_specs=placed, out_specs=P(RAD, LAT, None), check_vma=False)
```

time: 125 us -> 127 us (1.016)
  blocking collectives: 28.2 us -> 24.5 us
  waiting for transfers between devices: 42.4 us -> 45.8 us
  starting transfers between devices: 41.3 us -> 44.3 us
    all_to_all x2, waiting for transfers between devices: 35.7 us -> 39.3 us  [the longest x1 20.3 us: shards(): right = lax.all_to_all(right, RAD + ('x',), 0, 0, tiled=True)]
    all_gather x1 -> x0, blocking collectives: 2.37 us -> none  [shards(): whole = lax.all_gather(jnp.stack(pieces), 'core', axis=0)]
    ppermute x0 -> x1, starting transfers between devices: none -> 1.92 us  [shards(): received = lax.ppermute(other, 'core', [(0, 1), (1, 0)])]
    ppermute x3, waiting for transfers between devices: 6.7 us -> 5.23 us  [shards(): lax.ppermute(mine, 'x', [(i, (i + shift) % 4) for i in range(4)])]
    pallas_call x4 -> x6, Pallas kernels: 10.3 us -> 9.97 us  [the longest x1 4.54 us: shards(): call(fourier_kernel, bf16(256, 2, 1280), [VMEM, HBM, HBM], [pltpu.VMEM((8...]
  transfers between devices with their start and end apart: 5 -> 6, of which waited for: 4 -> 5; matrix products, arithmetic and copies ran while one was open for 0% -> 0% of each run, Pallas kernels for 2% -> 2%
where the time goes in v7:
time: 127 us; the launch traced here: 126 us
  waiting for transfers between devices  45.8 us (36%)
  starting transfers between devices  44.3 us (35%)
  blocking collectives  24.5 us (19%)
  Pallas kernels  10.4 us (8%)
    all_to_all x1, blocking collectives, shards(): out = lax.all_to_all(solved.reshape(64, 8, 512), RAD, 0, 0, tiled=True)  24.5 us
    all_to_all x1, starting transfers between devices, shards(): arrived = lax.all_to_all(sent, ('x',) + RAD, 0, 0, tiled=True)  21.5 us
    all_to_all x1, waiting for transfers between devices, shards(): right = lax.all_to_all(right, RAD + ('x',), 0, 0, tiled=True)  20.3 us
    all_to_all x1, waiting for transfers between devices, shards(): arrived = lax.all_to_all(sent, ('x',) + RAD, 0, 0, tiled=True)  19 us
    ppermute x3, starting transfers between devices, shards(): lax.ppermute(mine, 'x', [(i, (i + shift) % 4) for i in range(4)])  11.5 us
    all_to_all x1, starting transfers between devices, shards(): right = lax.all_to_all(right, RAD + ('x',), 0, 0, tiled=True)  9.4 us
    ppermute x3, waiting for transfers between devices, shards(): lax.ppermute(mine, 'x', [(i, (i + shift) % 4) for i in range(4)])  5.23 us
    pallas_call x1, Pallas kernels, shards(): call(fourier_kernel, bf16(256, 2, 1280), [VMEM, HBM, HBM], [pltpu.VMEM((8...  4.54 us
  transfers between devices with their start and end apart: 6, of which 5 were waited for; matrix products, arithmetic and copies ran while one was open for 0% of the time, Pallas kernels for 2%

profile of v7, /device:TPU:8, one launch (start us, length us, event | category | flops | bytes accessed | tf_op | source)
XLA Modules:
  0.0 126.4 jit_solution(3953616994130138959)
XLA Ops:
  0.0 4.5 %shard_map.56 = bf16[256,2,1280]{2,1,0:T(2,128)(2,1)} custom-call(s32[1,256]{1,0:T(1,128)} %bitcast.25, bf16[8,96,1024]{2,1,0:T(8,128)(2,1)} %forcing_hbm.1, bf16[8,64,512]{2,1,0:T(8,128)(2,1)} %previous_hbm.1), custom_call_target="tpu_custom_call" | custom-call | flops 805306368 | bytes 2097152 | tf_op jit(solution)/shard_map/pallas_call | solution.py:198
  4.5 0.0 copy-start.2
  4.6 21.5 %all-to-all-start = ((bf16[256,2,1280]{2,1,0:T(2,128)(2,1)}), bf16[256,2,1280]{2,1,0:T(2,128)(2,1)S(1)}, u32[]{:S(2)}, u32[]{:S(2)}) async-start(bf16[256,2,1280]{2,1,0:T(2,128)(2,1)} %shard_map.56), calls=%async_computation | async-start | bytes 2621440 | tf_op jit(solution)/shard_map/all_to_all | solution.py:215
  26.1 0.0 copy-start.1
  26.1 0.0 copy-done.2
  26.2 5.6 %collective-permute-start.1 = (bf16[96,512]{1,0:T(8,128)(2,1)S(1)}, bf16[96,512]{1,0:T(8,128)(2,1)S(1)}, u32[]{:S(2)}, u32[]{:S(2)}) collective-permute-start(bf16[96,512]{1,0:T(8,128)(2,1)S(1)} %get-tuple-element.23), channel_id=1, source_target_pairs={{0,256},{128,384},{256,0},{384,128},{1,257},{129,385},{257,1},{385... | collective-permute-start | bytes 294920 | tf_op jit(solution)/shard_map/ppermute | solution.py:221
  31.8 2.6 %collective-permute-start.2 = (bf16[96,512]{1,0:T(8,128)(2,1)S(1)}, bf16[96,512]{1,0:T(8,128)(2,1)S(1)}, u32[]{:S(2)}, u32[]{:S(2)}) collective-permute-start(bf16[96,512]{1,0:T(8,128)(2,1)S(1)} %get-tuple-element.22), channel_id=1, source_target_pairs={{0,384},{128,0},{256,128},{384,256},{1,385},{129,1},{257,129},{385... | collective-permute-start | bytes 294920 | tf_op jit(solution)/shard_map/ppermute | solution.py:221
  34.5 3.2 %collective-permute-start = (bf16[96,512]{1,0:T(8,128)(2,1)S(1)}, bf16[96,512]{1,0:T(8,128)(2,1)S(1)}, u32[]{:S(2)}, u32[]{:S(2)}) collective-permute-start(bf16[96,512]{1,0:T(8,128)(2,1)S(1)} %get-tuple-element.24), channel_id=1, source_target_pairs={{0,128},{128,256},{256,384},{384,0},{1,129},{129,257},{257,385},{3... | collective-permute-start | bytes 294920 | tf_op jit(solution)/shard_map/ppermute | solution.py:221
  37.7 0.1 pad_add_fusion.place_ref
  37.8 0.0 collective-permute-done.1
  37.8 2.9 %collective-permute-done.2 = bf16[96,512]{1,0:T(8,128)(2,1)S(1)} collective-permute-done((bf16[96,512]{1,0:T(8,128)(2,1)S(1)}, bf16[96,512]{1,0:T(8,128)(2,1)S(1)}, u32[]{:S(2)}, u32[]{:S(2)}) %collective-permute-start.2) | collective-permute-done | bytes 98336 | tf_op jit(solution)/shard_map/ppermute | solution.py:221
  40.6 2.3 %collective-permute-done = bf16[96,512]{1,0:T(8,128)(2,1)S(1)} collective-permute-done((bf16[96,512]{1,0:T(8,128)(2,1)S(1)}, bf16[96,512]{1,0:T(8,128)(2,1)S(1)}, u32[]{:S(2)}, u32[]{:S(2)}) %collective-permute-start) | collective-permute-done | bytes 98336 | tf_op jit(solution)/shard_map/ppermute | solution.py:221
  43.0 0.1 pad_maximum_fusion.legendre_ref
  43.0 0.0 copy-done.1
  43.1 1.2 shard_map.57
  44.3 19.0 %all-to-all-done.arrived_ref = bf16[256,2,1280]{2,1,0:T(2,128)(2,1)S(1)} async-done(((bf16[256,2,1280]{2,1,0:T(2,128)(2,1)}), bf16[256,2,1280]{2,1,0:T(2,128)(2,1)S(1)}, u32[]{:S(2)}, u32[]{:S(2)}) %all-to-all-start) | async-done | bytes 1310752 | tf_op jit(solution)/shard_map/all_to_all | solution.py:215
  63.3 1.2 shard_map.58
  64.5 1.9 %collective-permute-start.3 = (bf16[256,1024]{1,0:T(8,128)(2,1)S(1)}, bf16[256,1024]{1,0:T(8,128)(2,1)S(1)}, u32[]{:S(2)}, u32[]{:S(2)}) collective-permute-start(bf16[256,1024]{1,0:T(8,128)(2,1)S(1)} %get-tuple-element.20), channel_id=1, source_target_pairs={{0,64},{64,0},{1,65},{65,1},{2,66},{66,2},{3,67},{67,3},{4,68},{68... | collective-permute-start | bytes 1572872 | tf_op jit(solution)/shard_map/ppermute | solution.py:240
  66.4 0.6 shard_map.59.own_ref
  67.0 0.0 copy-start
  67.1 1.3 collective-permute-done.3.received_ref
  68.3 1.4 %shard_map.60 = bf16[256,2,512]{2,1,0:T(2,128)(2,1)} custom-call(f32[256,1024]{1,0:T(8,128)S(1)} %shard_map.59.own_ref, bf16[256,1024]{1,0:T(8,128)(2,1)S(1)} %collective-permute-done.3.received_ref), custom_call_target="tpu_custom_call" | custom-call | flops 134217728 | bytes 2097152 | tf_op jit(solution)/shard_map/pallas_call | solution.py:244
  69.7 9.4 %all-to-all-start.1 = ((bf16[256,2,512]{2,1,0:T(2,128)(2,1)}), bf16[256,2,512]{2,1,0:T(2,128)(2,1)S(1)}, u32[]{:S(2)}, u32[]{:S(2)}) async-start(bf16[256,2,512]{2,1,0:T(2,128)(2,1)} %shard_map.60), calls=%async_computation.1 | async-start | bytes 1048576 | tf_op jit(solution)/shard_map/all_to_all | solution.py:245
  79.1 0.0 copy-done
  79.1 1.0 shard_map.55
  80.1 20.3 %all-to-all-done.1.right_ref = bf16[256,2,512]{2,1,0:T(2,128)(2,1)S(1)} async-done(((bf16[256,2,512]{2,1,0:T(2,128)(2,1)}), bf16[256,2,512]{2,1,0:T(2,128)(2,1)S(1)}, u32[]{:S(2)}, u32[]{:S(2)}) %all-to-all-start.1) | async-done | bytes 524320 | tf_op jit(solution)/shard_map/all_to_all | solution.py:245
  100.4 0.5 shard_map.61
  100.9 24.5 %all_to_all.15 = bf16[64,8,512]{2,1,0:T(8,128)(2,1)S(1)} all-to-all(bf16[64,8,512]{2,1,0:T(8,128)(2,1)S(1)} %bitcast.24), channel_id=1, replica_groups=mesh['x'=4,'core'=2,'z'=8,'y'=8] {'z','y'}, dimensions={0} | all-to-all | bytes 1048576 | tf_op jit(solution)/shard_map/all_to_all | solution.py:247
  125.5 0.9 copy.7
  (1 shorter events, 0.0 us)
Async XLA Ops:
  4.5 21.6 %copy-start.2 = (bf16[4,512,96]{1,2,0:T(8,128)(2,1)S(1)}, bf16[4,512,96]{1,2,0:T(8,128)(2,1)}, u32[]{:S(2)}) copy-start(bf16[4,512,96]{1,2,0:T(8,128)(2,1)} %param.6) | copy-start | bytes 1179652
  4.6 58.7 %all-to-all-start = ((bf16[256,2,1280]{2,1,0:T(2,128)(2,1)}), bf16[256,2,1280]{2,1,0:T(2,128)(2,1)S(1)}, u32[]{:S(2)}, u32[]{:S(2)}) async-start(bf16[256,2,1280]{2,1,0:T(2,128)(2,1)} %shard_map.56), calls=%async_computation | async-start | bytes 2621440 | tf_op jit(solution)/shard_map/all_to_all | solution.py:215
  26.1 17.0 %copy-start.1 = (s32[256]{0:T(256)S(1)}, s32[256]{0:T(256)}, u32[]{:S(2)}) copy-start(s32[256]{0:T(256)} %param.7) | copy-start | bytes 3076
  26.2 11.6 %collective-permute-start.1 = (bf16[96,512]{1,0:T(8,128)(2,1)S(1)}, bf16[96,512]{1,0:T(8,128)(2,1)S(1)}, u32[]{:S(2)}, u32[]{:S(2)}) collective-permute-start(bf16[96,512]{1,0:T(8,128)(2,1)S(1)} %get-tuple-element.23), channel_id=1, source_target_pairs={{0,256},{128,384},{256,0},{384,128},{1,257},{129,385},{257,1},{385... | collective-permute-start | bytes 294920 | tf_op jit(solution)/shard_map/ppermute | solution.py:221
  31.8 8.8 %collective-permute-start.2 = (bf16[96,512]{1,0:T(8,128)(2,1)S(1)}, bf16[96,512]{1,0:T(8,128)(2,1)S(1)}, u32[]{:S(2)}, u32[]{:S(2)}) collective-permute-start(bf16[96,512]{1,0:T(8,128)(2,1)S(1)} %get-tuple-element.22), channel_id=1, source_target_pairs={{0,384},{128,0},{256,128},{384,256},{1,385},{129,1},{257,129},{385... | collective-permute-start | bytes 294920 | tf_op jit(solution)/shard_map/ppermute | solution.py:221
  34.5 8.5 %collective-permute-start = (bf16[96,512]{1,0:T(8,128)(2,1)S(1)}, bf16[96,512]{1,0:T(8,128)(2,1)S(1)}, u32[]{:S(2)}, u32[]{:S(2)}) collective-permute-start(bf16[96,512]{1,0:T(8,128)(2,1)S(1)} %get-tuple-element.24), channel_id=1, source_target_pairs={{0,128},{128,256},{256,384},{384,0},{1,129},{129,257},{257,385},{3... | collective-permute-start | bytes 294920 | tf_op jit(solution)/shard_map/ppermute | solution.py:221
  64.5 3.8 %collective-permute-start.3 = (bf16[256,1024]{1,0:T(8,128)(2,1)S(1)}, bf16[256,1024]{1,0:T(8,128)(2,1)S(1)}, u32[]{:S(2)}, u32[]{:S(2)}) collective-permute-start(bf16[256,1024]{1,0:T(8,128)(2,1)S(1)} %get-tuple-element.20), channel_id=1, source_target_pairs={{0,64},{64,0},{1,65},{65,1},{2,66},{66,2},{3,67},{67,3},{4,68},{68... | collective-permute-start | bytes 1572872 | tf_op jit(solution)/shard_map/ppermute | solution.py:240
  67.0 12.0 %copy-start = (f32[1,512,512]{2,1,0:T(8,128)S(1)}, f32[1,512,512]{2,1,0:T(8,128)}, u32[]{:S(2)}) copy-start(f32[1,512,512]{2,1,0:T(8,128)} %inverse_ref.1) | copy-start | bytes 3145732
  69.7 30.7 %all-to-all-start.1 = ((bf16[256,2,512]{2,1,0:T(2,128)(2,1)}), bf16[256,2,512]{2,1,0:T(2,128)(2,1)S(1)}, u32[]{:S(2)}, u32[]{:S(2)}) async-start(bf16[256,2,512]{2,1,0:T(2,128)(2,1)} %shard_map.60), calls=%async_computation.1 | async-start | bytes 1048576 | tf_op jit(solution)/shard_map/all_to_all | solution.py:245

commit v8 on v7

--- a/solution.py
+++ b/solution.py
@@ -136,12 +136,9 @@
             place(pair * 2 + 1, to, jnp.where(low_half, roll(a0, 64), a1))
 
 
-def own_kernel(gathered_ref, weights_ref, out_ref):
-    out_ref[...] = nt_dot(weights_ref[...], gathered_ref[...])
-
-
-def right_kernel(own_ref, received_ref, out_ref):
-    right = (own_ref[...] + received_ref[...].astype(F32)).astype(BF)
+def right_kernel(place_ref, gathered_ref, weights_ref, received_ref, out_ref):
+    own = nt_dot(weights_ref[...], gathered_ref[...])
+    right = (own + received_ref[1 - place_ref[3]].astype(F32)).astype(BF)
     row, column = iota((256, 256), 0), iota((256, 256), 1)
     parted = (column == (row & 1) * 128 + (row >> 1)).astype(BF)
     parts = []
@@ -237,11 +234,10 @@
         [pltpu.VMEM((512, 1280), BF)],
         2 * 256 * 384 * 1024,
     )(arrived, other_weights)
-    received = lax.ppermute(other, "core", [(0, 1), (1, 0)])
-    own = call(own_kernel, jax.ShapeDtypeStruct((256, 1024), F32), [VMEM] * 2, (), 2 * 256 * 640 * 1024)(
-        gathered, own_weights
-    )
-    right = call(right_kernel, bf16(256, 2, 512), [VMEM] * 2, (), 2 * 256 * 256 * 1024)(own, received)
+    received = lax.all_gather(other, "core", axis=0)
+    right = call(
+        right_kernel, bf16(256, 2, 512), [SMEM, VMEM, VMEM, VMEM], (), 2 * 256 * 640 * 1024
+    )(place, gathered, own_weights, received)
     right = lax.all_to_all(right, RAD + ("x",), 0, 0, tiled=True)
     solved = call(solve_kernel, bf16(512, 512), [VMEM] * 3, (), 2 * 512**3)(valid, solver, right)
     out = lax.all_to_all(solved.reshape(64, 8, 512), RAD, 0, 0, tiled=True)

time: 127 us -> 158 us (1.24)
  between operations: 0.22 us -> 13.6 us
  waiting for transfers between devices: 45.8 us -> 53.4 us
  starting transfers between devices: 44.3 us -> 51.1 us
  local copies, waits for them, and re-layouts: 1 us -> 3.44 us
    all_gather x0 -> x1, waiting for transfers between devices: none -> 9.96 us  [shards(): received = lax.all_gather(other, 'core', axis=0)]
    all_to_all x1, starting transfers between devices: 9.4 us -> 18.1 us  [shards(): right = lax.all_to_all(right, RAD + ('x',), 0, 0, tiled=True)]
    unnamed x6 -> x8, local copies, waits for them, and re-layouts: 0.02 us -> 2.46 us
    ppermute x1 -> x0, starting transfers between devices: 1.92 us -> none  [shards(): received = lax.ppermute(other, 'core', [(0, 1), (1, 0)])]
  transfers between devices with their start and end apart: 6 -> 6, of which waited for: 5 -> 5; matrix products, arithmetic and copies ran while one was open for 0% -> 0% of each run, Pallas kernels for 2% -> 1%
where the time goes in v8:
time: 158 us
  waiting for transfers between devices  53.4 us (34%)
  starting transfers between devices  51.1 us (32%)
  blocking collectives  24.6 us (16%)
  between operations  13.6 us (9%)
  Pallas kernels  11.6 us (7%)
  local copies, waits for them, and re-layouts  3.44 us (2%)
    all_to_all x1, blocking collectives, shards(): out = lax.all_to_all(solved.reshape(64, 8, 512), RAD, 0, 0, tiled=True)  24.6 us
    all_to_all x1, starting transfers between devices, shards(): arrived = lax.all_to_all(sent, ('x',) + RAD, 0, 0, tiled=True)  21.5 us
    all_to_all x1, waiting for transfers between devices, shards(): right = lax.all_to_all(right, RAD + ('x',), 0, 0, tiled=True)  19.2 us
    all_to_all x1, waiting for transfers between devices, shards(): arrived = lax.all_to_all(sent, ('x',) + RAD, 0, 0, tiled=True)  19.1 us
    all_to_all x1, starting transfers between devices, shards(): right = lax.all_to_all(right, RAD + ('x',), 0, 0, tiled=True)  18.1 us
    ppermute x3, starting transfers between devices, shards(): lax.ppermute(mine, 'x', [(i, (i + shift) % 4) for i in range(4)])  11.5 us
    all_gather x1, waiting for transfers between devices, shards(): received = lax.all_gather(other, 'core', axis=0)  9.96 us
    ppermute x3, waiting for transfers between devices, shards(): lax.ppermute(mine, 'x', [(i, (i + shift) % 4) for i in range(4)])  5.12 us
  transfers between devices with their start and end apart: 6, of which 5 were waited for; matrix products, arithmetic and copies ran while one was open for 0% of the time, Pallas kernels for 1%

profile of v8, /device:TPU:8, one launch (start us, length us, event | category | flops | bytes accessed | tf_op | source)
XLA Modules:
  0.0 157.9 jit_solution(16448449411893226544)
XLA Ops:
  6.5 4.6 %shard_map.56 = bf16[256,2,1280]{2,1,0:T(2,128)(2,1)} custom-call(s32[1,256]{1,0:T(1,128)} %bitcast.27, bf16[8,96,1024]{2,1,0:T(8,128)(2,1)} %forcing_hbm.1, bf16[8,64,512]{2,1,0:T(8,128)(2,1)} %previous_hbm.1), custom_call_target="tpu_custom_call" | custom-call | flops 805306368 | bytes 2097152 | tf_op jit(solution)/shard_map/pallas_call | solution.py:195
  11.1 0.0 copy-start.3
  11.1 21.5 %all-to-all-start = ((bf16[256,2,1280]{2,1,0:T(2,128)(2,1)}), bf16[256,2,1280]{2,1,0:T(2,128)(2,1)S(1)}, u32[]{:S(2)}, u32[]{:S(2)}) async-start(bf16[256,2,1280]{2,1,0:T(2,128)(2,1)} %shard_map.56), calls=%async_computation | async-start | bytes 2621440 | tf_op jit(solution)/shard_map/all_to_all | solution.py:212
  32.6 0.0 copy-start.2
  32.6 0.0 all-gather.3.cloned.1.call-start
  32.7 0.0 copy-done.3
  32.8 5.6 %collective-permute-start.1 = (bf16[96,512]{1,0:T(8,128)(2,1)S(1)}, bf16[96,512]{1,0:T(8,128)(2,1)S(1)}, u32[]{:S(2)}, u32[]{:S(2)}) collective-permute-start(bf16[96,512]{1,0:T(8,128)(2,1)S(1)} %get-tuple-element.23), channel_id=1, source_target_pairs={{0,256},{128,384},{256,0},{384,128},{1,257},{129,385},{257,1},{385... | collective-permute-start | bytes 294920 | tf_op jit(solution)/shard_map/ppermute | solution.py:218
  38.4 2.6 %collective-permute-start.2 = (bf16[96,512]{1,0:T(8,128)(2,1)S(1)}, bf16[96,512]{1,0:T(8,128)(2,1)S(1)}, u32[]{:S(2)}, u32[]{:S(2)}) collective-permute-start(bf16[96,512]{1,0:T(8,128)(2,1)S(1)} %get-tuple-element.22), channel_id=1, source_target_pairs={{0,384},{128,0},{256,128},{384,256},{1,385},{129,1},{257,129},{385... | collective-permute-start | bytes 294920 | tf_op jit(solution)/shard_map/ppermute | solution.py:218
  41.1 3.2 %collective-permute-start = (bf16[96,512]{1,0:T(8,128)(2,1)S(1)}, bf16[96,512]{1,0:T(8,128)(2,1)S(1)}, u32[]{:S(2)}, u32[]{:S(2)}) collective-permute-start(bf16[96,512]{1,0:T(8,128)(2,1)S(1)} %get-tuple-element.24), channel_id=1, source_target_pairs={{0,128},{128,256},{256,384},{384,0},{1,129},{129,257},{257,385},{3... | collective-permute-start | bytes 294920 | tf_op jit(solution)/shard_map/ppermute | solution.py:218
  44.3 0.1 pad_add_fusion.place_ref
  44.4 0.0 collective-permute-done.1
  44.4 2.9 %collective-permute-done.2 = bf16[96,512]{1,0:T(8,128)(2,1)S(1)} collective-permute-done((bf16[96,512]{1,0:T(8,128)(2,1)S(1)}, bf16[96,512]{1,0:T(8,128)(2,1)S(1)}, u32[]{:S(2)}, u32[]{:S(2)}) %collective-permute-start.2) | collective-permute-done | bytes 98336 | tf_op jit(solution)/shard_map/ppermute | solution.py:218
  47.2 2.3 %collective-permute-done = bf16[96,512]{1,0:T(8,128)(2,1)S(1)} collective-permute-done((bf16[96,512]{1,0:T(8,128)(2,1)S(1)}, bf16[96,512]{1,0:T(8,128)(2,1)S(1)}, u32[]{:S(2)}, u32[]{:S(2)}) %collective-permute-start) | collective-permute-done | bytes 98336 | tf_op jit(solution)/shard_map/ppermute | solution.py:218
  49.5 0.1 pad_maximum_fusion.legendre_ref
  49.5 0.0 copy-done.2
  49.5 1.2 shard_map.57
  50.7 19.1 %all-to-all-done.arrived_ref = bf16[256,2,1280]{2,1,0:T(2,128)(2,1)S(1)} async-done(((bf16[256,2,1280]{2,1,0:T(2,128)(2,1)}), bf16[256,2,1280]{2,1,0:T(2,128)(2,1)S(1)}, u32[]{:S(2)}, u32[]{:S(2)}) %all-to-all-start) | async-done | bytes 1310752 | tf_op jit(solution)/shard_map/all_to_all | solution.py:212
  69.8 2.0 %shard_map.58 = (bf16[1024,640]{1,0:T(8,128)(2,1)S(1)}, bf16[256,1024]{1,0:T(8,128)(2,1)}) custom-call(bf16[256,2,1280]{2,1,0:T(2,128)(2,1)S(1)} %all-to-all-done.arrived_ref, bf16[256,384]{1,0:T(8,128)(2,1)S(1)} %get-tuple-element.17.weights_ref), custom_call_target="tpu_custom_call" | custom-call | flops 201326592 | bytes 2097152 | tf_op jit(solution)/shard_map/pallas_call | solution.py:230
  71.8 0.0 all-gather.3.cloned.1.call-update
  71.9 10.0 %all-gather.3.cloned.1.call-done = bf16[512,1024]{1,0:T(8,128)(2,1)} async-done(((bf16[256,1024]{1,0:T(8,128)(2,1)}), bf16[512,1024]{1,0:T(8,128)(2,1)}) %all-gather.3.cloned.1.call-update) | async-done | bytes 1048592 | tf_op jit(solution)/shard_map/all_gather | solution.py:237
  81.8 0.0 copy-start.1
  81.8 1.2 copy-done.1
  83.0 2.3 %shard_map.59 = bf16[256,2,512]{2,1,0:T(2,128)(2,1)} custom-call(s32[4]{0:T(128)S(1)} %pad_add_fusion.place_ref, bf16[1024,640]{1,0:T(8,128)(2,1)S(1)} %get-tuple-element.18.gathered_ref, bf16[256,640]{1,0:T(8,128)(2,1)S(1)} %get-tuple-element.19.weights_ref, bf16[2,256,1024]{2,1,0:T(8,128)(2,1)S(1)} %bitcast.26), custom_call_target="tpu_custom_call" | custom-call | flops 335544320 | bytes 2097152 | tf_op jit(solution)/shard_map/pallas_call | solution.py:238
  85.4 18.1 %all-to-all-start.1 = ((bf16[256,2,512]{2,1,0:T(2,128)(2,1)}), bf16[256,2,512]{2,1,0:T(2,128)(2,1)S(1)}, u32[]{:S(2)}, u32[]{:S(2)}) async-start(bf16[256,2,512]{2,1,0:T(2,128)(2,1)} %shard_map.59), calls=%async_computation.1 | async-start | bytes 1048576 | tf_op jit(solution)/shard_map/all_to_all | solution.py:241
  103.5 0.0 copy-start
  103.5 1.2 copy-done
  104.7 1.0 shard_map.55
  105.7 19.2 %all-to-all-done.1.right_ref = bf16[256,2,512]{2,1,0:T(2,128)(2,1)S(1)} async-done(((bf16[256,2,512]{2,1,0:T(2,128)(2,1)}), bf16[256,2,512]{2,1,0:T(2,128)(2,1)S(1)}, u32[]{:S(2)}, u32[]{:S(2)}) %all-to-all-start.1) | async-done | bytes 524320 | tf_op jit(solution)/shard_map/all_to_all | solution.py:241
  125.0 0.5 shard_map.60
  125.4 24.6 %all_to_all.15 = bf16[64,8,512]{2,1,0:T(8,128)(2,1)S(1)} all-to-all(bf16[64,8,512]{2,1,0:T(8,128)(2,1)S(1)} %bitcast.25), channel_id=1, replica_groups=mesh['x'=4,'core'=2,'z'=8,'y'=8] {'z','y'}, dimensions={0} | all-to-all | bytes 1048576 | tf_op jit(solution)/shard_map/all_to_all | solution.py:243
  150.1 0.9 copy.7
  (1 shorter events, 0.0 us)
Async XLA Ops:
  11.1 21.6 %copy-start.3 = (bf16[4,512,96]{1,2,0:T(8,128)(2,1)S(1)}, bf16[4,512,96]{1,2,0:T(8,128)(2,1)}, u32[]{:S(2)}) copy-start(bf16[4,512,96]{1,2,0:T(8,128)(2,1)} %param.6) | copy-start | bytes 1179652
  11.1 58.7 %all-to-all-start = ((bf16[256,2,1280]{2,1,0:T(2,128)(2,1)}), bf16[256,2,1280]{2,1,0:T(2,128)(2,1)S(1)}, u32[]{:S(2)}, u32[]{:S(2)}) async-start(bf16[256,2,1280]{2,1,0:T(2,128)(2,1)} %shard_map.56), calls=%async_computation | async-start | bytes 2621440 | tf_op jit(solution)/shard_map/all_to_all | solution.py:212
  32.6 16.9 %copy-start.2 = (s32[256]{0:T(256)S(1)}, s32[256]{0:T(256)}, u32[]{:S(2)}) copy-start(s32[256]{0:T(256)} %param.7) | copy-start | bytes 3076
  32.6 49.2 %all-gather.3.cloned.1.call-start = ((), (), s32[]{:S(2)}) async-start(), calls=%async_computation.3 | async-start | bytes 1572864 | tf_op jit(solution)/shard_map/all_gather | solution.py:237
  32.8 11.6 %collective-permute-start.1 = (bf16[96,512]{1,0:T(8,128)(2,1)S(1)}, bf16[96,512]{1,0:T(8,128)(2,1)S(1)}, u32[]{:S(2)}, u32[]{:S(2)}) collective-permute-start(bf16[96,512]{1,0:T(8,128)(2,1)S(1)} %get-tuple-element.23), channel_id=1, source_target_pairs={{0,256},{128,384},{256,0},{384,128},{1,257},{129,385},{257,1},{385... | collective-permute-start | bytes 294920 | tf_op jit(solution)/shard_map/ppermute | solution.py:218
  38.4 8.8 %collective-permute-start.2 = (bf16[96,512]{1,0:T(8,128)(2,1)S(1)}, bf16[96,512]{1,0:T(8,128)(2,1)S(1)}, u32[]{:S(2)}, u32[]{:S(2)}) collective-permute-start(bf16[96,512]{1,0:T(8,128)(2,1)S(1)} %get-tuple-element.22), channel_id=1, source_target_pairs={{0,384},{128,0},{256,128},{384,256},{1,385},{129,1},{257,129},{385... | collective-permute-start | bytes 294920 | tf_op jit(solution)/shard_map/ppermute | solution.py:218
  41.1 8.4 %collective-permute-start = (bf16[96,512]{1,0:T(8,128)(2,1)S(1)}, bf16[96,512]{1,0:T(8,128)(2,1)S(1)}, u32[]{:S(2)}, u32[]{:S(2)}) collective-permute-start(bf16[96,512]{1,0:T(8,128)(2,1)S(1)} %get-tuple-element.24), channel_id=1, source_target_pairs={{0,128},{128,256},{256,384},{384,0},{1,129},{129,257},{257,385},{3... | collective-permute-start | bytes 294920 | tf_op jit(solution)/shard_map/ppermute | solution.py:218
  81.8 1.2 copy-start.1
  85.4 39.6 %all-to-all-start.1 = ((bf16[256,2,512]{2,1,0:T(2,128)(2,1)}), bf16[256,2,512]{2,1,0:T(2,128)(2,1)S(1)}, u32[]{:S(2)}, u32[]{:S(2)}) async-start(bf16[256,2,512]{2,1,0:T(2,128)(2,1)} %shard_map.59), calls=%async_computation.1 | async-start | bytes 1048576 | tf_op jit(solution)/shard_map/all_to_all | solution.py:241
  103.5 1.2 copy-start
Sparse Core Ops, SparseCore 0:
  72.0 9.7 all-gather.2

commit v9 on v5

--- a/solution.py
+++ b/solution.py
@@ -224,6 +224,7 @@
         2 * 512**3,
     )(orders, place, inverse)
 
+    weights, parted, solver, valid = lax.optimization_barrier((weights, parted, solver, valid))
     right = call(
         spectrum_kernel,
         bf16(512, 2, 256),

time: 125 us -> 126 us (level)
  blocking collectives: 28.2 us -> 59.3 us
  waiting for transfers between devices: 42.4 us -> 21.1 us
  starting transfers between devices: 41.3 us -> 31.2 us
    all_to_all x0 -> x1, blocking collectives: none -> 31.2 us  [shards(): right = lax.all_to_all(right, ('core',) + RAD + ('x',), 0, 0, tiled=True)]
    all_to_all x1 -> x0, waiting for transfers between devices: 19.1 us -> none  [shards(): right = lax.all_to_all(right, ('core',) + RAD + ('x',), 0, 0, tiled=True)]
    all_to_all x1 -> x0, starting transfers between devices: 9.43 us -> none  [shards(): right = lax.all_to_all(right, ('core',) + RAD + ('x',), 0, 0, tiled=True)]
    all_to_all x1, waiting for transfers between devices: 16.5 us -> 13.5 us  [shards(): arrived = lax.all_to_all(sent, ('core', 'x') + RAD, 0, 0, tiled=True)]
  transfers between devices with their start and end apart: 5 -> 4, of which waited for: 4 -> 4; matrix products, arithmetic and copies ran while one was open for 0% -> 1% of each run, Pallas kernels for 2% -> 2%
where the time goes in v9:
time: 126 us
  blocking collectives  59.3 us (47%)
  starting transfers between devices  31.2 us (25%)
  waiting for transfers between devices  21.1 us (17%)
  Pallas kernels  9.93 us (8%)
  local copies, waits for them, and re-layouts  2.83 us (2%)
    all_to_all x1, blocking collectives, shards(): right = lax.all_to_all(right, ('core',) + RAD + ('x',), 0, 0, tiled=True)  31.2 us
    all_to_all x1, blocking collectives, shards(): out = lax.all_to_all(solved.reshape(64, 8, 512), RAD, 0, 0, tiled=True)  25.7 us
    all_to_all x1, starting transfers between devices, shards(): arrived = lax.all_to_all(sent, ('core', 'x') + RAD, 0, 0, tiled=True)  21.1 us
    all_to_all x1, waiting for transfers between devices, shards(): arrived = lax.all_to_all(sent, ('core', 'x') + RAD, 0, 0, tiled=True)  13.5 us
    ppermute x3, starting transfers between devices, shards(): lax.ppermute(mine, 'x', [(i, (i + shift) % 4) for i in range(4)])  10.1 us
    ppermute x3, waiting for transfers between devices, shards(): lax.ppermute(mine, 'x', [(i, (i + shift) % 4) for i in range(4)])  7.54 us
    pallas_call x1, Pallas kernels, shards(): call(fourier_kernel, bf16(512, 2, 640), [VMEM, HBM, HBM], [pltpu.VMEM((8,...  4.64 us
  transfers between devices with their start and end apart: 4, of which 4 were waited for; matrix products, arithmetic and copies ran while one was open for 1% of the time, Pallas kernels for 2%

profile of v9, /device:TPU:8, one launch (start us, length us, event | category | flops | bytes accessed | tf_op | source)
XLA Modules:
  0.0 125.6 jit_solution(17120777383356091024)
XLA Ops:
  0.0 4.6 %shard_map.55 = bf16[512,2,640]{2,1,0:T(2,128)(2,1)} custom-call(s32[1,256]{1,0:T(1,128)} %bitcast.26, bf16[8,96,1024]{2,1,0:T(8,128)(2,1)} %forcing_hbm.1, bf16[8,64,512]{2,1,0:T(8,128)(2,1)} %previous_hbm.1), custom_call_target="tpu_custom_call" | custom-call | flops 805306368 | bytes 2097152 | tf_op jit(solution)/shard_map/pallas_call | solution.py:191
  4.7 0.0 copy-start.4
  4.7 0.0 copy-start
  4.7 0.0 copy-start.3
  4.7 21.1 %all-to-all-start = ((bf16[512,2,640]{2,1,0:T(2,128)(2,1)}), bf16[512,2,640]{2,1,0:T(2,128)(2,1)S(1)}, u32[]{:S(2)}, u32[]{:S(2)}) async-start(bf16[512,2,640]{2,1,0:T(2,128)(2,1)} %shard_map.55), calls=%async_computation | async-start | bytes 2621440 | tf_op jit(solution)/shard_map/all_to_all | solution.py:208
  25.9 0.0 copy-done.4
  25.9 4.6 %collective-permute-start.2 = (bf16[96,512]{1,0:T(8,128)(2,1)S(1)}, bf16[96,512]{1,0:T(8,128)(2,1)S(1)}, u32[]{:S(2)}, u32[]{:S(2)}) collective-permute-start(bf16[96,512]{1,0:T(8,128)(2,1)S(1)} %get-tuple-element.26), channel_id=1, source_target_pairs={{0,384},{128,0},{256,128},{384,256},{1,385},{129,1},{257,129},{385... | collective-permute-start | bytes 294920 | tf_op jit(solution)/shard_map/ppermute | solution.py:214
  30.5 2.8 %collective-permute-start.1 = (bf16[96,512]{1,0:T(8,128)(2,1)S(1)}, bf16[96,512]{1,0:T(8,128)(2,1)}, u32[]{:S(2)}, u32[]{:S(2)}) collective-permute-start(bf16[96,512]{1,0:T(8,128)(2,1)S(1)} %get-tuple-element.27), channel_id=1, source_target_pairs={{0,256},{128,384},{256,0},{384,128},{1,257},{129,385},{257,1},{385... | collective-permute-start | bytes 294920 | tf_op jit(solution)/shard_map/ppermute | solution.py:214
  33.3 2.8 %collective-permute-start = (bf16[96,512]{1,0:T(8,128)(2,1)S(1)}, bf16[96,512]{1,0:T(8,128)(2,1)}, u32[]{:S(2)}, u32[]{:S(2)}) collective-permute-start(bf16[96,512]{1,0:T(8,128)(2,1)S(1)} %get-tuple-element.28), channel_id=1, source_target_pairs={{0,128},{128,256},{256,384},{384,0},{1,129},{129,257},{257,385},{3... | collective-permute-start | bytes 294920 | tf_op jit(solution)/shard_map/ppermute | solution.py:214
  36.1 0.1 pad_add_fusion.place_ref
  36.1 0.0 copy-done
  36.1 0.0 copy-done.3
  36.1 1.0 shard_map.57
  37.2 1.9 %collective-permute-done.2 = bf16[96,512]{1,0:T(8,128)(2,1)S(1)} collective-permute-done((bf16[96,512]{1,0:T(8,128)(2,1)S(1)}, bf16[96,512]{1,0:T(8,128)(2,1)S(1)}, u32[]{:S(2)}, u32[]{:S(2)}) %collective-permute-start.2) | collective-permute-done | bytes 98336 | tf_op jit(solution)/shard_map/ppermute | solution.py:214
  39.0 3.0 %collective-permute-done.1 = bf16[96,512]{1,0:T(8,128)(2,1)} collective-permute-done((bf16[96,512]{1,0:T(8,128)(2,1)S(1)}, bf16[96,512]{1,0:T(8,128)(2,1)}, u32[]{:S(2)}, u32[]{:S(2)}) %collective-permute-start.1) | collective-permute-done | bytes 98336 | tf_op jit(solution)/shard_map/ppermute | solution.py:214
  42.0 2.7 %collective-permute-done = bf16[96,512]{1,0:T(8,128)(2,1)} collective-permute-done((bf16[96,512]{1,0:T(8,128)(2,1)S(1)}, bf16[96,512]{1,0:T(8,128)(2,1)}, u32[]{:S(2)}, u32[]{:S(2)}) %collective-permute-start) | collective-permute-done | bytes 98336 | tf_op jit(solution)/shard_map/ppermute | solution.py:214
  44.7 1.0 pad_maximum_fusion
  45.7 2.4 %all-gather = bf16[8,96,512]{2,1,0:T(8,128)(2,1)S(1)} all-gather(bf16[4,96,512]{2,1,0:T(8,128)(2,1)S(1)} %pad_maximum_fusion), channel_id=2, replica_groups=mesh['x'=4,'core'=2,'z'=8,'y'=8] {'core'}, dimensions={0}, use_global_device_ids=true | all-gather | bytes 1179648 | tf_op jit(solution)/shard_map/all_gather | solution.py:215
  48.1 1.8 %shard_map.56 = (bf16[512,1280]{1,0:T(8,128)(2,1)S(1)}, bf16[512,512]{1,0:T(8,128)(2,1)S(1)}) custom-call(s32[1,256]{1,0:T(1,128)S(1)} %bitcast.28, s32[3]{0:T(128)S(1)} %pad_add_fusion.place_ref, bf16[2,4,96,512]{3,2,1,0:T(8,128)(2,1)S(1)} %bitcast.25), custom_call_target="tpu_custom_call" | custom-call | flops 402653184 | bytes 2097152 | tf_op jit(solution)/shard_map/pallas_call | solution.py:216
  49.9 0.0 copy-start.1
  49.9 0.8 copy-done.1
  50.7 13.5 %all-to-all-done.arrived_ref = bf16[512,2,640]{2,1,0:T(2,128)(2,1)S(1)} async-done(((bf16[512,2,640]{2,1,0:T(2,128)(2,1)}), bf16[512,2,640]{2,1,0:T(2,128)(2,1)S(1)}, u32[]{:S(2)}, u32[]{:S(2)}) %all-to-all-start) | async-done | bytes 1310752 | tf_op jit(solution)/shard_map/all_to_all | solution.py:208
  64.2 0.0 copy-start.2
  64.2 1.0 copy-done.2
  65.3 2.0 %shard_map.58 = bf16[512,2,256]{2,1,0:T(2,128)(2,1)S(1)} custom-call(bf16[512,2,640]{2,1,0:T(2,128)(2,1)S(1)} %all-to-all-done.arrived_ref, bf16[512,1280]{1,0:T(8,128)(2,1)S(1)} %get-tuple-element.23.weights_ref, bf16[512,512]{1,0:T(8,128)(2,1)S(1)} %copy-done.2), custom_call_target="tpu_custom_call" | custom-call | flops 939524096 | bytes 2097152 | tf_op jit(solution)/shard_map/pallas_call | solution.py:228
  67.3 31.2 %all_to_all.15.right_ref = bf16[512,2,256]{2,1,0:T(2,128)(2,1)S(1)} all-to-all(bf16[512,2,256]{2,1,0:T(2,128)(2,1)S(1)} %shard_map.58), channel_id=1, replica_groups=mesh['x'=4,'core'=2,'z'=8,'y'=8] {'core','z','y','x'}, dimensions={0} | all-to-all | bytes 1048576 | tf_op jit(solution)/shard_map/all_to_all | solution.py:235
  98.4 0.5 shard_map.59
  98.9 25.7 %all_to_all.16 = bf16[64,8,512]{2,1,0:T(8,128)(2,1)S(1)} all-to-all(bf16[64,8,512]{2,1,0:T(8,128)(2,1)S(1)} %bitcast.24), channel_id=1, replica_groups=mesh['x'=4,'core'=2,'z'=8,'y'=8] {'z','y'}, dimensions={0} | all-to-all | bytes 1048576 | tf_op jit(solution)/shard_map/all_to_all | solution.py:237
  124.7 0.9 copy.7
  (1 shorter events, 0.0 us)
Async XLA Ops:
  4.7 21.2 %copy-start.4 = (bf16[4,512,96]{1,2,0:T(8,128)(2,1)S(1)}, bf16[4,512,96]{1,2,0:T(8,128)(2,1)}, u32[]{:S(2)}) copy-start(bf16[4,512,96]{1,2,0:T(8,128)(2,1)} %param.6) | copy-start | bytes 1179652
  4.7 31.5 %copy-start = (f32[1,512,512]{2,1,0:T(8,128)S(1)}, f32[1,512,512]{2,1,0:T(8,128)}, u32[]{:S(2)}) copy-start(f32[1,512,512]{2,1,0:T(8,128)} %inverse_ref.1) | copy-start | bytes 3145732
  4.7 31.5 %copy-start.3 = (s32[256]{0:T(256)S(1)}, s32[256]{0:T(256)}, u32[]{:S(2)}) copy-start(s32[256]{0:T(256)} %param.7) | copy-start | bytes 3076
  4.7 59.5 %all-to-all-start = ((bf16[512,2,640]{2,1,0:T(2,128)(2,1)}), bf16[512,2,640]{2,1,0:T(2,128)(2,1)S(1)}, u32[]{:S(2)}, u32[]{:S(2)}) async-start(bf16[512,2,640]{2,1,0:T(2,128)(2,1)} %shard_map.55), calls=%async_computation | async-start | bytes 2621440 | tf_op jit(solution)/shard_map/all_to_all | solution.py:208
  25.9 13.1 %collective-permute-start.2 = (bf16[96,512]{1,0:T(8,128)(2,1)S(1)}, bf16[96,512]{1,0:T(8,128)(2,1)S(1)}, u32[]{:S(2)}, u32[]{:S(2)}) collective-permute-start(bf16[96,512]{1,0:T(8,128)(2,1)S(1)} %get-tuple-element.26), channel_id=1, source_target_pairs={{0,384},{128,0},{256,128},{384,256},{1,385},{129,1},{257,129},{385... | collective-permute-start | bytes 294920 | tf_op jit(solution)/shard_map/ppermute | solution.py:214
  30.5 11.5 %collective-permute-start.1 = (bf16[96,512]{1,0:T(8,128)(2,1)S(1)}, bf16[96,512]{1,0:T(8,128)(2,1)}, u32[]{:S(2)}, u32[]{:S(2)}) collective-permute-start(bf16[96,512]{1,0:T(8,128)(2,1)S(1)} %get-tuple-element.27), channel_id=1, source_target_pairs={{0,256},{128,384},{256,0},{384,128},{1,257},{129,385},{257,1},{385... | collective-permute-start | bytes 294920 | tf_op jit(solution)/shard_map/ppermute | solution.py:214
  33.3 11.4 %collective-permute-start = (bf16[96,512]{1,0:T(8,128)(2,1)S(1)}, bf16[96,512]{1,0:T(8,128)(2,1)}, u32[]{:S(2)}, u32[]{:S(2)}) collective-permute-start(bf16[96,512]{1,0:T(8,128)(2,1)S(1)} %get-tuple-element.28), channel_id=1, source_target_pairs={{0,128},{128,256},{256,384},{384,0},{1,129},{129,257},{257,385},{3... | collective-permute-start | bytes 294920 | tf_op jit(solution)/shard_map/ppermute | solution.py:214
  49.9 0.8 copy-start.1
  64.2 1.0 copy-start.2

commit v10 on v5

--- a/solution.py
+++ b/solution.py
@@ -85,7 +85,7 @@
         copy.wait()
 
 
-def legendre_kernel(assign_ref, place_ref, legendre_ref, out_ref, parted_ref):
+def legendre_kernel(assign_ref, place_ref, legendre_ref, out_ref):
     order = jnp.sum(jnp.where(iota((1, 256), 1) == place_ref[0], assign_ref[...], 0), axis=1, keepdims=True)
     row = iota((512, 1), 0)
     core, x, inner = row >> 8, row & 3, (row >> 2) & 63
@@ -100,14 +100,13 @@
             at = h * 256 + core_from * 128
             out_ref[:, at : at + 128] = nt_dot(kept, jnp.concatenate(pieces, axis=0)).astype(BF)
     out_ref[:, 768:1280] = jnp.where(column == core * 256 + x * 64 + inner, 2.0, 0.0).astype(BF)
-    parted_ref[...] = (column == (row & 1) * 256 + (row >> 1)).astype(BF)
 
 
 def roll(a, shift):
     return pltpu.roll(a, shift, 1)
 
 
-def spectrum_kernel(arrived_ref, weights_ref, parted_ref, out_ref, rows_ref, gathered_ref):
+def spectrum_kernel(arrived_ref, weights_ref, out_ref, rows_ref, gathered_ref):
     rows_ref[...] = arrived_ref[...].reshape(1024, 640)
     lane = iota((128, 128), 1)
     low_half = lane < 64
@@ -139,8 +138,14 @@
             place(pair * 2, to, jnp.where(low_half, a0, roll(a1, 64)))
             place(pair * 2 + 1, to, jnp.where(low_half, roll(a0, 64), a1))
     right = nt_dot(weights_ref[...], gathered_ref[...]).astype(BF)
-    right = jnp.dot(right, parted_ref[...], preferred_element_type=F32).astype(BF)
-    out_ref[...] = right.reshape(512, 2, 256)
+    row, column = iota((256, 1), 0), iota((256, 256), 1)
+    parted = (column == (row & 1) * 128 + (row >> 1)).astype(BF)
+    parts = []
+    for i in range(2):
+        part = right[:, i * 256 : i * 256 + 256]
+        parts.append(jnp.dot(part, parted, preferred_element_type=F32).astype(BF))
+    parts = [part[:, :128] for part in parts] + [part[:, 128:] for part in parts]
+    out_ref[...] = jnp.concatenate(parts, axis=1).reshape(512, 2, 256)
 
 
 def inverse_kernel(assign_ref, place_ref, inverse_ref, out_ref, valid_ref):
@@ -167,7 +172,7 @@
 HBM = pl.BlockSpec(memory_space=pltpu.HBM)
 
 
-def call(kernel, out, ins, scratch=(), flops=0, vmem=24, outs=None):
+def call(kernel, out, ins, scratch=(), flops=0, vmem=16, outs=None):
     return pl.pallas_call(
         kernel,
         out_shape=out,
@@ -213,9 +218,9 @@
         mine = lax.dynamic_index_in_dim(by_order, (x + shift) % 4, 0, keepdims=False)
         pieces.append(lax.ppermute(mine, "x", [(i, (i + shift) % 4) for i in range(4)]))
     whole = lax.all_gather(jnp.stack(pieces), "core", axis=0)
-    weights, parted = call(
-        legendre_kernel, (bf16(512, 1280), bf16(512, 512)), [VMEM, SMEM, VMEM], (), 2 * 512 * 512 * 768
-    )(orders, place, whole)
+    weights = call(legendre_kernel, bf16(512, 1280), [VMEM, SMEM, VMEM], (), 2 * 512 * 512 * 768)(
+        orders, place, whole
+    )
     solver, valid = call(
         inverse_kernel,
         (bf16(2, 512, 256), jax.ShapeDtypeStruct((8, 512), F32)),
@@ -224,13 +229,14 @@
         2 * 512**3,
     )(orders, place, inverse)
 
+    weights, solver, valid = lax.optimization_barrier((weights, solver, valid))
     right = call(
         spectrum_kernel,
         bf16(512, 2, 256),
-        [VMEM] * 3,
+        [VMEM] * 2,
         [pltpu.VMEM((1024, 640), BF), pltpu.VMEM((512, 1280), BF)],
-        2 * 512 * 512 * 1792,
-    )(arrived, weights, parted)
+        2 * 512 * 512 * 1536,
+    )(arrived, weights)
     right = lax.all_to_all(right, ("core",) + RAD + ("x",), 0, 0, tiled=True)
     solved = call(solve_kernel, bf16(512, 512), [VMEM] * 3, (), 2 * 512**3)(valid, solver, right)
     out = lax.all_to_all(solved.reshape(64, 8, 512), RAD, 0, 0, tiled=True)

time: 125 us -> 125 us (level)
  blocking collectives: 28.2 us -> 59.3 us
  waiting for transfers between devices: 42.4 us -> 22 us
  starting transfers between devices: 41.3 us -> 31.2 us
    all_to_all x0 -> x1, blocking collectives: none -> 31.2 us  [shards(): right = lax.all_to_all(right, ('core',) + RAD + ('x',), 0, 0, tiled=True)]
    all_to_all x1 -> x0, waiting for transfers between devices: 19.1 us -> none  [shards(): right = lax.all_to_all(right, ('core',) + RAD + ('x',), 0, 0, tiled=True)]
    all_to_all x1 -> x0, starting transfers between devices: 9.43 us -> none  [shards(): right = lax.all_to_all(right, ('core',) + RAD + ('x',), 0, 0, tiled=True)]
    all_to_all x1, waiting for transfers between devices: 16.5 us -> 14.5 us  [shards(): arrived = lax.all_to_all(sent, ('core', 'x') + RAD, 0, 0, tiled=True)]
  transfers between devices with their start and end apart: 5 -> 4, of which waited for: 4 -> 4; matrix products, arithmetic and copies ran while one was open for 0% -> 1% of each run, Pallas kernels for 2% -> 2%
where the time goes in v10:
time: 125 us; the launch traced here: 124 us
  blocking collectives  59.3 us (47%)
  starting transfers between devices  31.2 us (25%)
  waiting for transfers between devices  22 us (18%)
  Pallas kernels  9.7 us (8%)
    all_to_all x1, blocking collectives, shards(): right = lax.all_to_all(right, ('core',) + RAD + ('x',), 0, 0, tiled=True)  31.2 us
    all_to_all x1, blocking collectives, shards(): out = lax.all_to_all(solved.reshape(64, 8, 512), RAD, 0, 0, tiled=True)  25.7 us
    all_to_all x1, starting transfers between devices, shards(): arrived = lax.all_to_all(sent, ('core', 'x') + RAD, 0, 0, tiled=True)  21.1 us
    all_to_all x1, waiting for transfers between devices, shards(): arrived = lax.all_to_all(sent, ('core', 'x') + RAD, 0, 0, tiled=True)  14.5 us
    ppermute x3, starting transfers between devices, shards(): lax.ppermute(mine, 'x', [(i, (i + shift) % 4) for i in range(4)])  10.1 us
    ppermute x3, waiting for transfers between devices, shards(): lax.ppermute(mine, 'x', [(i, (i + shift) % 4) for i in range(4)])  7.54 us
    pallas_call x1, Pallas kernels, shards(): call(fourier_kernel, bf16(512, 2, 640), [VMEM, HBM, HBM], [pltpu.VMEM((8,...  4.64 us
  transfers between devices with their start and end apart: 4, of which 4 were waited for; matrix products, arithmetic and copies ran while one was open for 1% of the time, Pallas kernels for 2%

profile of v10, /device:TPU:8, one launch (start us, length us, event | category | flops | bytes accessed | tf_op | source)
XLA Modules:
  0.0 124.4 jit_solution(6192488433884423347)
XLA Ops:
  0.0 4.6 %shard_map.55 = bf16[512,2,640]{2,1,0:T(2,128)(2,1)} custom-call(s32[1,256]{1,0:T(1,128)} %bitcast.26, bf16[8,96,1024]{2,1,0:T(8,128)(2,1)} %forcing_hbm.1, bf16[8,64,512]{2,1,0:T(8,128)(2,1)} %previous_hbm.1), custom_call_target="tpu_custom_call" | custom-call | flops 805306368 | bytes 2097152 | tf_op jit(solution)/shard_map/pallas_call | solution.py:196
  4.6 0.0 copy-start.2
  4.7 0.0 copy-start
  4.7 0.0 copy-start.1
  4.7 21.1 %all-to-all-start = ((bf16[512,2,640]{2,1,0:T(2,128)(2,1)}), bf16[512,2,640]{2,1,0:T(2,128)(2,1)S(1)}, u32[]{:S(2)}, u32[]{:S(2)}) async-start(bf16[512,2,640]{2,1,0:T(2,128)(2,1)} %shard_map.55), calls=%async_computation | async-start | bytes 2621440 | tf_op jit(solution)/shard_map/all_to_all | solution.py:213
  25.8 0.0 copy-done.2
  25.9 4.6 %collective-permute-start.2 = (bf16[96,512]{1,0:T(8,128)(2,1)S(1)}, bf16[96,512]{1,0:T(8,128)(2,1)S(1)}, u32[]{:S(2)}, u32[]{:S(2)}) collective-permute-start(bf16[96,512]{1,0:T(8,128)(2,1)S(1)} %get-tuple-element.20), channel_id=1, source_target_pairs={{0,384},{128,0},{256,128},{384,256},{1,385},{129,1},{257,129},{385... | collective-permute-start | bytes 294920 | tf_op jit(solution)/shard_map/ppermute | solution.py:219
  30.5 2.8 %collective-permute-start.1 = (bf16[96,512]{1,0:T(8,128)(2,1)S(1)}, bf16[96,512]{1,0:T(8,128)(2,1)}, u32[]{:S(2)}, u32[]{:S(2)}) collective-permute-start(bf16[96,512]{1,0:T(8,128)(2,1)S(1)} %get-tuple-element.21), channel_id=1, source_target_pairs={{0,256},{128,384},{256,0},{384,128},{1,257},{129,385},{257,1},{385... | collective-permute-start | bytes 294920 | tf_op jit(solution)/shard_map/ppermute | solution.py:219
  33.3 2.8 %collective-permute-start = (bf16[96,512]{1,0:T(8,128)(2,1)S(1)}, bf16[96,512]{1,0:T(8,128)(2,1)}, u32[]{:S(2)}, u32[]{:S(2)}) collective-permute-start(bf16[96,512]{1,0:T(8,128)(2,1)S(1)} %get-tuple-element.22), channel_id=1, source_target_pairs={{0,128},{128,256},{256,384},{384,0},{1,129},{129,257},{257,385},{3... | collective-permute-start | bytes 294920 | tf_op jit(solution)/shard_map/ppermute | solution.py:219
  36.1 0.1 pad_add_fusion.place_ref
  36.1 0.0 copy-done
  36.1 0.0 copy-done.1
  36.1 1.0 shard_map.57
  37.2 1.8 %collective-permute-done.2 = bf16[96,512]{1,0:T(8,128)(2,1)S(1)} collective-permute-done((bf16[96,512]{1,0:T(8,128)(2,1)S(1)}, bf16[96,512]{1,0:T(8,128)(2,1)S(1)}, u32[]{:S(2)}, u32[]{:S(2)}) %collective-permute-start.2) | collective-permute-done | bytes 98336 | tf_op jit(solution)/shard_map/ppermute | solution.py:219
  39.0 3.0 %collective-permute-done.1 = bf16[96,512]{1,0:T(8,128)(2,1)} collective-permute-done((bf16[96,512]{1,0:T(8,128)(2,1)S(1)}, bf16[96,512]{1,0:T(8,128)(2,1)}, u32[]{:S(2)}, u32[]{:S(2)}) %collective-permute-start.1) | collective-permute-done | bytes 98336 | tf_op jit(solution)/shard_map/ppermute | solution.py:219
  42.0 2.7 %collective-permute-done = bf16[96,512]{1,0:T(8,128)(2,1)} collective-permute-done((bf16[96,512]{1,0:T(8,128)(2,1)S(1)}, bf16[96,512]{1,0:T(8,128)(2,1)}, u32[]{:S(2)}, u32[]{:S(2)}) %collective-permute-start) | collective-permute-done | bytes 98336 | tf_op jit(solution)/shard_map/ppermute | solution.py:219
  44.7 1.0 pad_maximum_fusion
  45.7 2.4 %all-gather = bf16[8,96,512]{2,1,0:T(8,128)(2,1)S(1)} all-gather(bf16[4,96,512]{2,1,0:T(8,128)(2,1)S(1)} %pad_maximum_fusion), channel_id=2, replica_groups=mesh['x'=4,'core'=2,'z'=8,'y'=8] {'core'}, dimensions={0}, use_global_device_ids=true | all-gather | bytes 1179648 | tf_op jit(solution)/shard_map/all_gather | solution.py:220
  48.1 1.7 %shard_map.56.weights_ref = bf16[512,1280]{1,0:T(8,128)(2,1)S(1)} custom-call(s32[1,256]{1,0:T(1,128)S(1)} %bitcast.28, s32[3]{0:T(128)S(1)} %pad_add_fusion.place_ref, bf16[2,4,96,512]{3,2,1,0:T(8,128)(2,1)S(1)} %bitcast.24), custom_call_target="tpu_custom_call" | custom-call | flops 402653184 | bytes 2097152 | tf_op jit(solution)/shard_map/pallas_call | solution.py:221
  49.8 14.5 %all-to-all-done.arrived_ref = bf16[512,2,640]{2,1,0:T(2,128)(2,1)S(1)} async-done(((bf16[512,2,640]{2,1,0:T(2,128)(2,1)}), bf16[512,2,640]{2,1,0:T(2,128)(2,1)S(1)}, u32[]{:S(2)}, u32[]{:S(2)}) %all-to-all-start) | async-done | bytes 1310752 | tf_op jit(solution)/shard_map/all_to_all | solution.py:213
  64.2 1.9 %shard_map.58 = bf16[512,2,256]{2,1,0:T(2,128)(2,1)S(1)} custom-call(bf16[512,2,640]{2,1,0:T(2,128)(2,1)S(1)} %all-to-all-done.arrived_ref, bf16[512,1280]{1,0:T(8,128)(2,1)S(1)} %shard_map.56.weights_ref), custom_call_target="tpu_custom_call" | custom-call | flops 805306368 | bytes 2097152 | tf_op jit(solution)/shard_map/pallas_call | solution.py:233
  66.1 31.2 %all_to_all.15.right_ref = bf16[512,2,256]{2,1,0:T(2,128)(2,1)S(1)} all-to-all(bf16[512,2,256]{2,1,0:T(2,128)(2,1)S(1)} %shard_map.58), channel_id=1, replica_groups=mesh['x'=4,'core'=2,'z'=8,'y'=8] {'core','z','y','x'}, dimensions={0} | all-to-all | bytes 1048576 | tf_op jit(solution)/shard_map/all_to_all | solution.py:240
  97.3 0.5 shard_map.59
  97.8 25.7 %all_to_all.16 = bf16[64,8,512]{2,1,0:T(8,128)(2,1)S(1)} all-to-all(bf16[64,8,512]{2,1,0:T(8,128)(2,1)S(1)} %bitcast.25), channel_id=1, replica_groups=mesh['x'=4,'core'=2,'z'=8,'y'=8] {'z','y'}, dimensions={0} | all-to-all | bytes 1048576 | tf_op jit(solution)/shard_map/all_to_all | solution.py:242
  123.5 0.9 copy.7
  (1 shorter events, 0.0 us)
Async XLA Ops:
  4.6 21.2 %copy-start.2 = (bf16[4,512,96]{1,2,0:T(8,128)(2,1)S(1)}, bf16[4,512,96]{1,2,0:T(8,128)(2,1)}, u32[]{:S(2)}) copy-start(bf16[4,512,96]{1,2,0:T(8,128)(2,1)} %param.6) | copy-start | bytes 1179652
  4.7 31.5 %copy-start = (f32[1,512,512]{2,1,0:T(8,128)S(1)}, f32[1,512,512]{2,1,0:T(8,128)}, u32[]{:S(2)}) copy-start(f32[1,512,512]{2,1,0:T(8,128)} %inverse_ref.1) | copy-start | bytes 3145732
  4.7 31.5 %copy-start.1 = (s32[256]{0:T(256)S(1)}, s32[256]{0:T(256)}, u32[]{:S(2)}) copy-start(s32[256]{0:T(256)} %param.7) | copy-start | bytes 3076
  4.7 59.5 %all-to-all-start = ((bf16[512,2,640]{2,1,0:T(2,128)(2,1)}), bf16[512,2,640]{2,1,0:T(2,128)(2,1)S(1)}, u32[]{:S(2)}, u32[]{:S(2)}) async-start(bf16[512,2,640]{2,1,0:T(2,128)(2,1)} %shard_map.55), calls=%async_computation | async-start | bytes 2621440 | tf_op jit(solution)/shard_map/all_to_all | solution.py:213
  25.9 13.1 %collective-permute-start.2 = (bf16[96,512]{1,0:T(8,128)(2,1)S(1)}, bf16[96,512]{1,0:T(8,128)(2,1)S(1)}, u32[]{:S(2)}, u32[]{:S(2)}) collective-permute-start(bf16[96,512]{1,0:T(8,128)(2,1)S(1)} %get-tuple-element.20), channel_id=1, source_target_pairs={{0,384},{128,0},{256,128},{384,256},{1,385},{129,1},{257,129},{385... | collective-permute-start | bytes 294920 | tf_op jit(solution)/shard_map/ppermute | solution.py:219
  30.5 11.5 %collective-permute-start.1 = (bf16[96,512]{1,0:T(8,128)(2,1)S(1)}, bf16[96,512]{1,0:T(8,128)(2,1)}, u32[]{:S(2)}, u32[]{:S(2)}) collective-permute-start(bf16[96,512]{1,0:T(8,128)(2,1)S(1)} %get-tuple-element.21), channel_id=1, source_target_pairs={{0,256},{128,384},{256,0},{384,128},{1,257},{129,385},{257,1},{385... | collective-permute-start | bytes 294920 | tf_op jit(solution)/shard_map/ppermute | solution.py:219
  33.3 11.5 %collective-permute-start = (bf16[96,512]{1,0:T(8,128)(2,1)S(1)}, bf16[96,512]{1,0:T(8,128)(2,1)}, u32[]{:S(2)}, u32[]{:S(2)}) collective-permute-start(bf16[96,512]{1,0:T(8,128)(2,1)S(1)} %get-tuple-element.22), channel_id=1, source_target_pairs={{0,128},{128,256},{256,384},{384,0},{1,129},{129,257},{257,385},{3... | collective-permute-start | bytes 294920 | tf_op jit(solution)/shard_map/ppermute | solution.py:219

commit v11 on v8

--- a/solution.py
+++ b/solution.py
@@ -102,7 +102,7 @@
     return pltpu.roll(a, shift, 1)
 
 
-def spectrum_kernel(arrived_ref, weights_ref, gathered_ref, out_ref, rows_ref):
+def spectrum_kernel(arrived_ref, weights_ref, gathered_ref, first_ref, second_ref, rows_ref):
     rows_ref[...] = arrived_ref[...].reshape(512, 1280)
     lane = iota((128, 128), 1)
     low_half = lane < 64
@@ -126,7 +126,9 @@
             place(rho + 1, at, jnp.where(even_quarter, roll(b0, 96), b1))
             place(rho + 2, at, jnp.where(even_quarter, b2, roll(b3, 32)))
             place(rho + 3, at, jnp.where(even_quarter, roll(b2, 96), b3))
-    out_ref[...] = nt_dot(weights_ref[...], gathered_ref[:, :384]).astype(BF)
+    other = nt_dot(weights_ref[...], gathered_ref[:, :384]).astype(BF)
+    first_ref[...] = other[:128]
+    second_ref[...] = other[128:]
     for pair in range(4):
         for two in range(2):
             at = 768 + pair * 128
@@ -136,9 +138,11 @@
             place(pair * 2 + 1, to, jnp.where(low_half, roll(a0, 64), a1))
 
 
-def right_kernel(place_ref, gathered_ref, weights_ref, received_ref, out_ref):
+def right_kernel(place_ref, gathered_ref, weights_ref, first_ref, second_ref, out_ref):
     own = nt_dot(weights_ref[...], gathered_ref[...])
-    right = (own + received_ref[1 - place_ref[3]].astype(F32)).astype(BF)
+    from_core = 1 - place_ref[3]
+    received = jnp.concatenate([first_ref[from_core], second_ref[from_core]], axis=0)
+    right = (own + received.astype(F32)).astype(BF)
     row, column = iota((256, 256), 0), iota((256, 256), 1)
     parted = (column == (row & 1) * 128 + (row >> 1)).astype(BF)
     parts = []
@@ -171,7 +175,7 @@
 HBM = pl.BlockSpec(memory_space=pltpu.HBM)
 
 
-def call(kernel, out, ins, scratch=(), flops=0, vmem=24, outs=None):
+def call(kernel, out, ins, scratch=(), flops=0, vmem=16, outs=None):
     return pl.pallas_call(
         kernel,
         out_shape=out,
@@ -227,17 +231,22 @@
         2 * 512**3,
     )(orders, place, inverse)
 
-    gathered, other = call(
+    own_weights, other_weights, solver, valid = lax.optimization_barrier(
+        (own_weights, other_weights, solver, valid)
+    )
+    gathered, first, second = call(
         spectrum_kernel,
-        (bf16(1024, 640), bf16(256, 1024)),
+        (bf16(1024, 640), bf16(128, 1024), bf16(128, 1024)),
         [VMEM] * 2,
         [pltpu.VMEM((512, 1280), BF)],
         2 * 256 * 384 * 1024,
     )(arrived, other_weights)
-    received = lax.all_gather(other, "core", axis=0)
+    first = lax.all_gather(first, "core", axis=0)
+    first, second = lax.optimization_barrier((first, second))
+    second = lax.all_gather(second, "core", axis=0)
     right = call(
-        right_kernel, bf16(256, 2, 512), [SMEM, VMEM, VMEM, VMEM], (), 2 * 256 * 640 * 1024
-    )(place, gathered, own_weights, received)
+        right_kernel, bf16(256, 2, 512), [SMEM, VMEM, VMEM, VMEM, VMEM], (), 2 * 256 * 640 * 1024
+    )(place, gathered, own_weights, first, second)
     right = lax.all_to_all(right, RAD + ("x",), 0, 0, tiled=True)
     solved = call(solve_kernel, bf16(512, 512), [VMEM] * 3, (), 2 * 512**3)(valid, solver, right)
     out = lax.all_to_all(solved.reshape(64, 8, 512), RAD, 0, 0, tiled=True)

time: 158 us -> 127 us (0.80)
  blocking collectives: 24.6 us -> 59.3 us
  waiting for transfers between devices: 53.4 us -> 22.9 us
  starting transfers between devices: 51.1 us -> 32.4 us
  between operations: 13.6 us -> 0.19 us
  local copies, waits for them, and re-layouts: 3.44 us -> 1 us
  Pallas kernels: 11.6 us -> 10 us
    all_to_all x0 -> x1, blocking collectives: none -> 30.5 us  [shards(): right = lax.all_to_all(right, RAD + ('x',), 0, 0, tiled=True)]
    all_to_all x1 -> x0, waiting for transfers between devices: 19.2 us -> none  [shards(): right = lax.all_to_all(right, RAD + ('x',), 0, 0, tiled=True)]
    all_to_all x1 -> x0, starting transfers between devices: 18.1 us -> none  [shards(): right = lax.all_to_all(right, RAD + ('x',), 0, 0, tiled=True)]
    all_gather x1 -> x0, waiting for transfers between devices: 9.96 us -> none  [shards(): received = lax.all_gather(other, 'core', axis=0)]
    all_gather x0 -> x2, blocking collectives: none -> 4.35 us  [the longest x1 2.18 us: shards(): first = lax.all_gather(first, 'core', axis=0)]
    all_to_all x1, waiting for transfers between devices: 19.1 us -> 15.9 us  [shards(): arrived = lax.all_to_all(sent, ('x',) + RAD, 0, 0, tiled=True)]
    unnamed x8 -> x6, local copies, waits for them, and re-layouts: 2.46 us -> 0.02 us
    ppermute x3, waiting for transfers between devices: 5.12 us -> 7.02 us  [shards(): lax.ppermute(mine, 'x', [(i, (i + shift) % 4) for i in range(4)])]
  transfers between devices with their start and end apart: 6 -> 4, of which waited for: 5 -> 4; matrix products, arithmetic and copies ran while one was open for 0% -> 1% of each run, Pallas kernels for 1% -> 2%
where the time goes in v11:
time: 127 us
  blocking collectives  59.3 us (47%)
  starting transfers between devices  32.4 us (26%)
  waiting for transfers between devices  22.9 us (18%)
  Pallas kernels  10 us (8%)
    all_to_all x1, blocking collectives, shards(): right = lax.all_to_all(right, RAD + ('x',), 0, 0, tiled=True)  30.5 us
    all_to_all x1, blocking collectives, shards(): out = lax.all_to_all(solved.reshape(64, 8, 512), RAD, 0, 0, tiled=True)  24.4 us
    all_to_all x1, starting transfers between devices, shards(): arrived = lax.all_to_all(sent, ('x',) + RAD, 0, 0, tiled=True)  21.5 us
    all_to_all x1, waiting for transfers between devices, shards(): arrived = lax.all_to_all(sent, ('x',) + RAD, 0, 0, tiled=True)  15.9 us
    ppermute x3, starting transfers between devices, shards(): lax.ppermute(mine, 'x', [(i, (i + shift) % 4) for i in range(4)])  10.9 us
    ppermute x3, waiting for transfers between devices, shards(): lax.ppermute(mine, 'x', [(i, (i + shift) % 4) for i in range(4)])  7.02 us
    pallas_call x1, Pallas kernels, shards(): call(fourier_kernel, bf16(256, 2, 1280), [VMEM, HBM, HBM], [pltpu.VMEM((8...  4.54 us
  transfers between devices with their start and end apart: 4, of which 4 were waited for; matrix products, arithmetic and copies ran while one was open for 1% of the time, Pallas kernels for 2%

profile of v11, /device:TPU:8, one launch (start us, length us, event | category | flops | bytes accessed | tf_op | source)
XLA Modules:
  0.0 126.8 jit_solution(11906770297616997921)
XLA Ops:
  0.0 4.5 %shard_map.55 = bf16[256,2,1280]{2,1,0:T(2,128)(2,1)} custom-call(s32[1,256]{1,0:T(1,128)} %bitcast.29, bf16[8,96,1024]{2,1,0:T(8,128)(2,1)} %forcing_hbm.1, bf16[8,64,512]{2,1,0:T(8,128)(2,1)} %previous_hbm.1), custom_call_target="tpu_custom_call" | custom-call | flops 805306368 | bytes 2097152 | tf_op jit(solution)/shard_map/pallas_call | solution.py:199
  4.5 0.0 copy-start.2
  4.6 0.0 copy-start
  4.6 0.0 copy-start.1
  4.6 21.5 %all-to-all-start = ((bf16[256,2,1280]{2,1,0:T(2,128)(2,1)}), bf16[256,2,1280]{2,1,0:T(2,128)(2,1)S(1)}, u32[]{:S(2)}, u32[]{:S(2)}) async-start(bf16[256,2,1280]{2,1,0:T(2,128)(2,1)} %shard_map.55), calls=%async_computation | async-start | bytes 2621440 | tf_op jit(solution)/shard_map/all_to_all | solution.py:216
  26.1 0.0 copy-done.2
  26.2 5.8 %collective-permute-start.2 = (bf16[96,512]{1,0:T(8,128)(2,1)S(1)}, bf16[96,512]{1,0:T(8,128)(2,1)S(1)}, u32[]{:S(2)}, u32[]{:S(2)}) collective-permute-start(bf16[96,512]{1,0:T(8,128)(2,1)S(1)} %get-tuple-element.36), channel_id=1, source_target_pairs={{0,384},{128,0},{256,128},{384,256},{1,385},{129,1},{257,129},{385... | collective-permute-start | bytes 294920 | tf_op jit(solution)/shard_map/ppermute | solution.py:222
  32.0 1.9 %collective-permute-start.1 = (bf16[96,512]{1,0:T(8,128)(2,1)S(1)}, bf16[96,512]{1,0:T(8,128)(2,1)S(1)}, u32[]{:S(2)}, u32[]{:S(2)}) collective-permute-start(bf16[96,512]{1,0:T(8,128)(2,1)S(1)} %get-tuple-element.37), channel_id=1, source_target_pairs={{0,256},{128,384},{256,0},{384,128},{1,257},{129,385},{257,1},{385... | collective-permute-start | bytes 294920 | tf_op jit(solution)/shard_map/ppermute | solution.py:222
  33.9 3.2 %collective-permute-start = (bf16[96,512]{1,0:T(8,128)(2,1)S(1)}, bf16[96,512]{1,0:T(8,128)(2,1)}, u32[]{:S(2)}, u32[]{:S(2)}) collective-permute-start(bf16[96,512]{1,0:T(8,128)(2,1)S(1)} %get-tuple-element.38), channel_id=1, source_target_pairs={{0,128},{128,256},{256,384},{384,0},{1,129},{129,257},{257,385},{3... | collective-permute-start | bytes 294920 | tf_op jit(solution)/shard_map/ppermute | solution.py:222
  37.1 0.1 pad_add_fusion.place_ref
  37.2 0.0 copy-done
  37.2 0.0 copy-done.1
  37.2 1.0 shard_map.57
  38.2 0.9 collective-permute-done.2
  39.1 3.7 %collective-permute-done.1 = bf16[96,512]{1,0:T(8,128)(2,1)S(1)} collective-permute-done((bf16[96,512]{1,0:T(8,128)(2,1)S(1)}, bf16[96,512]{1,0:T(8,128)(2,1)S(1)}, u32[]{:S(2)}, u32[]{:S(2)}) %collective-permute-start.1) | collective-permute-done | bytes 98336 | tf_op jit(solution)/shard_map/ppermute | solution.py:222
  42.8 2.4 %collective-permute-done = bf16[96,512]{1,0:T(8,128)(2,1)} collective-permute-done((bf16[96,512]{1,0:T(8,128)(2,1)S(1)}, bf16[96,512]{1,0:T(8,128)(2,1)}, u32[]{:S(2)}, u32[]{:S(2)}) %collective-permute-start) | collective-permute-done | bytes 98336 | tf_op jit(solution)/shard_map/ppermute | solution.py:222
  45.2 0.9 pad_maximum_fusion.legendre_ref
  46.2 1.2 shard_map.56
  47.4 15.9 %all-to-all-done.arrived_ref = bf16[256,2,1280]{2,1,0:T(2,128)(2,1)S(1)} async-done(((bf16[256,2,1280]{2,1,0:T(2,128)(2,1)}), bf16[256,2,1280]{2,1,0:T(2,128)(2,1)S(1)}, u32[]{:S(2)}, u32[]{:S(2)}) %all-to-all-start) | async-done | bytes 1310752 | tf_op jit(solution)/shard_map/all_to_all | solution.py:216
  63.3 1.2 shard_map.58
  64.5 2.2 %all-gather = bf16[256,1024]{1,0:T(8,128)(2,1)S(1)} all-gather(bf16[128,1024]{1,0:T(8,128)(2,1)S(1)} %get-tuple-element.31), channel_id=2, replica_groups=mesh['x'=4,'core'=2,'z'=8,'y'=8] {'core'}, dimensions={0}, use_global_device_ids=true | all-gather | bytes 786432 | tf_op jit(solution)/shard_map/all_gather | solution.py:244
  66.7 2.2 %all-gather.1 = bf16[256,1024]{1,0:T(8,128)(2,1)S(1)} all-gather(bf16[128,1024]{1,0:T(8,128)(2,1)S(1)} %get-tuple-element.34), channel_id=3, replica_groups=mesh['x'=4,'core'=2,'z'=8,'y'=8] {'core'}, dimensions={0}, use_global_device_ids=true | all-gather | bytes 786432 | tf_op jit(solution)/shard_map/all_gather | solution.py:246
  68.9 1.6 %shard_map.59 = bf16[256,2,512]{2,1,0:T(2,128)(2,1)S(1)} custom-call(s32[4]{0:T(128)S(1)} %pad_add_fusion.place_ref, bf16[1024,640]{1,0:T(8,128)(2,1)S(1)} %get-tuple-element.29.gathered_ref, bf16[256,640]{1,0:T(8,128)(2,1)S(1)} %get-tuple-element.30.weights_ref, bf16[2,128,1024]{2,1,0:T(8,128)(2,1)S(1)} %bitcast.27, bf16[2,128,1024]{2,1,0:T(8,128)(2,1)S(1)} %bitcast.28), custom_call_target="tpu_custom_call" | custom-call | flops 335544320 | bytes 2097152 | tf_op jit(solution)/shard_map/pallas_call | solution.py:247
  70.4 30.5 %all_to_all.15.right_ref = bf16[256,2,512]{2,1,0:T(2,128)(2,1)S(1)} all-to-all(bf16[256,2,512]{2,1,0:T(2,128)(2,1)S(1)} %shard_map.59), channel_id=1, replica_groups=mesh['x'=4,'core'=2,'z'=8,'y'=8] {'z','y','x'}, dimensions={0} | all-to-all | bytes 1048576 | tf_op jit(solution)/shard_map/all_to_all | solution.py:250
  100.9 0.5 shard_map.60
  101.4 24.4 %all_to_all.16 = bf16[64,8,512]{2,1,0:T(8,128)(2,1)S(1)} all-to-all(bf16[64,8,512]{2,1,0:T(8,128)(2,1)S(1)} %bitcast.26), channel_id=1, replica_groups=mesh['x'=4,'core'=2,'z'=8,'y'=8] {'z','y'}, dimensions={0} | all-to-all | bytes 1048576 | tf_op jit(solution)/shard_map/all_to_all | solution.py:252
  125.9 0.9 copy.7
  (1 shorter events, 0.0 us)
Async XLA Ops:
  4.5 21.6 %copy-start.2 = (bf16[4,512,96]{1,2,0:T(8,128)(2,1)S(1)}, bf16[4,512,96]{1,2,0:T(8,128)(2,1)}, u32[]{:S(2)}) copy-start(bf16[4,512,96]{1,2,0:T(8,128)(2,1)} %param.6) | copy-start | bytes 1179652
  4.6 32.6 %copy-start = (f32[1,512,512]{2,1,0:T(8,128)S(1)}, f32[1,512,512]{2,1,0:T(8,128)}, u32[]{:S(2)}) copy-start(f32[1,512,512]{2,1,0:T(8,128)} %inverse_ref.1) | copy-start | bytes 3145732
  4.6 32.6 %copy-start.1 = (s32[256]{0:T(256)S(1)}, s32[256]{0:T(256)}, u32[]{:S(2)}) copy-start(s32[256]{0:T(256)} %param.7) | copy-start | bytes 3076
  4.6 58.7 %all-to-all-start = ((bf16[256,2,1280]{2,1,0:T(2,128)(2,1)}), bf16[256,2,1280]{2,1,0:T(2,128)(2,1)S(1)}, u32[]{:S(2)}, u32[]{:S(2)}) async-start(bf16[256,2,1280]{2,1,0:T(2,128)(2,1)} %shard_map.55), calls=%async_computation | async-start | bytes 2621440 | tf_op jit(solution)/shard_map/all_to_all | solution.py:216
  26.2 12.9 %collective-permute-start.2 = (bf16[96,512]{1,0:T(8,128)(2,1)S(1)}, bf16[96,512]{1,0:T(8,128)(2,1)S(1)}, u32[]{:S(2)}, u32[]{:S(2)}) collective-permute-start(bf16[96,512]{1,0:T(8,128)(2,1)S(1)} %get-tuple-element.36), channel_id=1, source_target_pairs={{0,384},{128,0},{256,128},{384,256},{1,385},{129,1},{257,129},{385... | collective-permute-start | bytes 294920 | tf_op jit(solution)/shard_map/ppermute | solution.py:222
  32.0 10.9 %collective-permute-start.1 = (bf16[96,512]{1,0:T(8,128)(2,1)S(1)}, bf16[96,512]{1,0:T(8,128)(2,1)S(1)}, u32[]{:S(2)}, u32[]{:S(2)}) collective-permute-start(bf16[96,512]{1,0:T(8,128)(2,1)S(1)} %get-tuple-element.37), channel_id=1, source_target_pairs={{0,256},{128,384},{256,0},{384,128},{1,257},{129,385},{257,1},{385... | collective-permute-start | bytes 294920 | tf_op jit(solution)/shard_map/ppermute | solution.py:222
  33.9 11.3 %collective-permute-start = (bf16[96,512]{1,0:T(8,128)(2,1)S(1)}, bf16[96,512]{1,0:T(8,128)(2,1)}, u32[]{:S(2)}, u32[]{:S(2)}) collective-permute-start(bf16[96,512]{1,0:T(8,128)(2,1)S(1)} %get-tuple-element.38), channel_id=1, source_target_pairs={{0,128},{128,256},{256,384},{384,0},{1,129},{129,257},{257,385},{3... | collective-permute-start | bytes 294920 | tf_op jit(solution)/shard_map/ppermute | solution.py:222

commit v12 on v10

--- a/solution.py
+++ b/solution.py
@@ -47,7 +47,7 @@
     forcing_copy = pltpu.make_async_copy(forcing_hbm, forcing_ref, in_sems.at[0])
     forcing_copy.start()
     row = iota((512, 1), 0)
-    slot = ((row >> 1) & 63) * 4 + (row >> 7)
+    slot = row >> 1
     orders = jnp.sum(jnp.where(iota((512, 256), 1) == slot, assign_ref[...], 0), axis=1, keepdims=True)
     lane = iota((512, 128), 1)
     cos_now, sin_now = cos_sin((orders * lane + (row & 1) * (LON // 4)) & (LON - 1))
@@ -60,9 +60,8 @@
         table_ref[:, q * 128 : q * 128 + 128] = cos_now.astype(BF)
         cos_now, sin_now = cos_now * cos_step - sin_now * sin_step, sin_now * cos_step + cos_now * sin_step
     table = table_ref[...]
-    reorder = (iota((512, 512), 1) == slot * 2 + (row & 1)).astype(BF)
     previous_copy.wait()
-    previous = previous_ref[...].reshape(512, 512)
+    previous = previous_ref[...].reshape(512, 512).T
     forcing_copy.wait()
     out_copies = []
     for block in range(2):
@@ -71,7 +70,7 @@
         for h in range(3):
             part = forcing_ref[:, h * 32 : h * 32 + 32, :].reshape(256, LON)
             parts.append(nt_dot(table[rows], part).astype(BF))
-        before = nt_dot(reorder[rows], previous).astype(BF)
+        before = previous[rows]
         for half in range(2):
             dests = pl.ds(half * 256 + block * 128, 128)
             pieces = [part[:, half * 128 : half * 128 + 128] for part in parts]
@@ -107,7 +106,9 @@
 
 
 def spectrum_kernel(arrived_ref, weights_ref, out_ref, rows_ref, gathered_ref):
-    rows_ref[...] = arrived_ref[...].reshape(1024, 640)
+    for block in range(8):
+        rows = slice(block * 128, block * 128 + 128)
+        rows_ref[rows] = arrived_ref[block // 4, :, block % 4].reshape(128, 640)
     lane = iota((128, 128), 1)
     low_half = lane < 64
     even_quarter = (lane & 32) == 0
@@ -210,7 +211,7 @@
         HBM,
     )(orders, forcing, previous)
     sent, legendre = lax.optimization_barrier((sent, legendre))
-    arrived = lax.all_to_all(sent, ("core", "x") + RAD, 0, 0, tiled=True)
+    arrived = lax.all_to_all(sent, ("core",) + RAD + ("x",), 0, 0, tiled=True)
 
     by_order = legendre.transpose(0, 2, 1)
     pieces = [lax.dynamic_index_in_dim(by_order, x, 0, keepdims=False)]
@@ -236,7 +237,7 @@
         [VMEM] * 2,
         [pltpu.VMEM((1024, 640), BF), pltpu.VMEM((512, 1280), BF)],
         2 * 512 * 512 * 1536,
-    )(arrived, weights)
+    )(arrived.reshape(2, 64, 4, 2, 640), weights)
     right = lax.all_to_all(right, ("core",) + RAD + ("x",), 0, 0, tiled=True)
     solved = call(solve_kernel, bf16(512, 512), [VMEM] * 3, (), 2 * 512**3)(valid, solver, right)
     out = lax.all_to_all(solved.reshape(64, 8, 512), RAD, 0, 0, tiled=True)

time: 125 us -> 124 us (level)
  waiting for transfers between devices: 22 us -> 20.6 us
    all_to_all x1, waiting for transfers between devices: 14.5 us -> 12.8 us  [shards(): arrived = lax.all_to_all(sent, ('core',) + RAD + ('x',), 0, 0, tiled=True)]
where the time goes in v12:
time: 124 us; the launch traced here: 123 us
  blocking collectives  59.8 us (48%)
  starting transfers between devices  31.2 us (25%)
  waiting for transfers between devices  20.6 us (17%)
  Pallas kernels  9.42 us (8%)
    all_to_all x1, blocking collectives, shards(): right = lax.all_to_all(right, ('core',) + RAD + ('x',), 0, 0, tiled=True)  31.7 us
    all_to_all x1, blocking collectives, shards(): out = lax.all_to_all(solved.reshape(64, 8, 512), RAD, 0, 0, tiled=True)  25.7 us
    all_to_all x1, starting transfers between devices, shards(): arrived = lax.all_to_all(sent, ('core',) + RAD + ('x',), 0, 0, tiled=True)  21.1 us
    all_to_all x1, waiting for transfers between devices, shards(): arrived = lax.all_to_all(sent, ('core',) + RAD + ('x',), 0, 0, tiled=True)  12.8 us
    ppermute x3, starting transfers between devices, shards(): lax.ppermute(mine, 'x', [(i, (i + shift) % 4) for i in range(4)])  10.1 us
    ppermute x3, waiting for transfers between devices, shards(): lax.ppermute(mine, 'x', [(i, (i + shift) % 4) for i in range(4)])  7.82 us
    pallas_call x1, Pallas kernels, shards(): call(fourier_kernel, bf16(512, 2, 640), [VMEM, HBM, HBM], [pltpu.VMEM((8,...  4.36 us
  transfers between devices with their start and end apart: 4, of which 4 were waited for; matrix products, arithmetic and copies ran while one was open for 1% of the time, Pallas kernels for 2%

profile of v12, /device:TPU:8, one launch (start us, length us, event | category | flops | bytes accessed | tf_op | source)
XLA Modules:
  0.0 123.3 jit_solution(8094467775737498831)
XLA Ops:
  0.0 4.4 %shard_map.55 = bf16[512,2,640]{2,1,0:T(2,128)(2,1)} custom-call(s32[1,256]{1,0:T(1,128)} %bitcast.28, bf16[8,96,1024]{2,1,0:T(8,128)(2,1)} %forcing_hbm.1, bf16[8,64,512]{2,1,0:T(8,128)(2,1)} %previous_hbm.1), custom_call_target="tpu_custom_call" | custom-call | flops 805306368 | bytes 2097152 | tf_op jit(solution)/shard_map/pallas_call | solution.py:197
  4.4 0.0 copy-start.2
  4.4 0.0 copy-start
  4.4 0.0 copy-start.1
  4.4 21.1 %all-to-all-start = ((bf16[512,2,640]{2,1,0:T(2,128)(2,1)}), bf16[512,2,640]{2,1,0:T(2,128)(2,1)S(1)}, u32[]{:S(2)}, u32[]{:S(2)}) async-start(bf16[512,2,640]{2,1,0:T(2,128)(2,1)} %shard_map.55), calls=%async_computation | async-start | bytes 2621440 | tf_op jit(solution)/shard_map/all_to_all | solution.py:214
  25.6 0.0 copy-done.2
  25.6 4.6 %collective-permute-start.2 = (bf16[96,512]{1,0:T(8,128)(2,1)S(1)}, bf16[96,512]{1,0:T(8,128)(2,1)S(1)}, u32[]{:S(2)}, u32[]{:S(2)}) collective-permute-start(bf16[96,512]{1,0:T(8,128)(2,1)S(1)} %get-tuple-element.20), channel_id=1, source_target_pairs={{0,384},{128,0},{256,128},{384,256},{1,385},{129,1},{257,129},{385... | collective-permute-start | bytes 294920 | tf_op jit(solution)/shard_map/ppermute | solution.py:220
  30.2 2.8 %collective-permute-start.1 = (bf16[96,512]{1,0:T(8,128)(2,1)S(1)}, bf16[96,512]{1,0:T(8,128)(2,1)}, u32[]{:S(2)}, u32[]{:S(2)}) collective-permute-start(bf16[96,512]{1,0:T(8,128)(2,1)S(1)} %get-tuple-element.21), channel_id=1, source_target_pairs={{0,256},{128,384},{256,0},{384,128},{1,257},{129,385},{257,1},{385... | collective-permute-start | bytes 294920 | tf_op jit(solution)/shard_map/ppermute | solution.py:220
  33.0 2.8 %collective-permute-start = (bf16[96,512]{1,0:T(8,128)(2,1)S(1)}, bf16[96,512]{1,0:T(8,128)(2,1)}, u32[]{:S(2)}, u32[]{:S(2)}) collective-permute-start(bf16[96,512]{1,0:T(8,128)(2,1)S(1)} %get-tuple-element.22), channel_id=1, source_target_pairs={{0,128},{128,256},{256,384},{384,0},{1,129},{129,257},{257,385},{3... | collective-permute-start | bytes 294920 | tf_op jit(solution)/shard_map/ppermute | solution.py:220
  35.8 0.1 pad_add_fusion.place_ref
  35.9 0.0 copy-done
  35.9 0.0 copy-done.1
  35.9 1.0 shard_map.57
  36.9 1.7 %collective-permute-done.2 = bf16[96,512]{1,0:T(8,128)(2,1)S(1)} collective-permute-done((bf16[96,512]{1,0:T(8,128)(2,1)S(1)}, bf16[96,512]{1,0:T(8,128)(2,1)S(1)}, u32[]{:S(2)}, u32[]{:S(2)}) %collective-permute-start.2) | collective-permute-done | bytes 98336 | tf_op jit(solution)/shard_map/ppermute | solution.py:220
  38.6 2.5 %collective-permute-done.1 = bf16[96,512]{1,0:T(8,128)(2,1)} collective-permute-done((bf16[96,512]{1,0:T(8,128)(2,1)S(1)}, bf16[96,512]{1,0:T(8,128)(2,1)}, u32[]{:S(2)}, u32[]{:S(2)}) %collective-permute-start.1) | collective-permute-done | bytes 98336 | tf_op jit(solution)/shard_map/ppermute | solution.py:220
  41.1 3.6 %collective-permute-done = bf16[96,512]{1,0:T(8,128)(2,1)} collective-permute-done((bf16[96,512]{1,0:T(8,128)(2,1)S(1)}, bf16[96,512]{1,0:T(8,128)(2,1)}, u32[]{:S(2)}, u32[]{:S(2)}) %collective-permute-start) | collective-permute-done | bytes 98336 | tf_op jit(solution)/shard_map/ppermute | solution.py:220
  44.7 1.0 pad_maximum_fusion
  45.7 2.4 %all-gather = bf16[8,96,512]{2,1,0:T(8,128)(2,1)S(1)} all-gather(bf16[4,96,512]{2,1,0:T(8,128)(2,1)S(1)} %pad_maximum_fusion), channel_id=2, replica_groups=mesh['x'=4,'core'=2,'z'=8,'y'=8] {'core'}, dimensions={0}, use_global_device_ids=true | all-gather | bytes 1179648 | tf_op jit(solution)/shard_map/all_gather | solution.py:221
  48.1 1.7 %shard_map.56.weights_ref = bf16[512,1280]{1,0:T(8,128)(2,1)S(1)} custom-call(s32[1,256]{1,0:T(1,128)S(1)} %bitcast.30, s32[3]{0:T(128)S(1)} %pad_add_fusion.place_ref, bf16[2,4,96,512]{3,2,1,0:T(8,128)(2,1)S(1)} %bitcast.26), custom_call_target="tpu_custom_call" | custom-call | flops 402653184 | bytes 2097152 | tf_op jit(solution)/shard_map/pallas_call | solution.py:222
  49.7 12.8 %all-to-all-done = bf16[512,2,640]{2,1,0:T(2,128)(2,1)S(1)} async-done(((bf16[512,2,640]{2,1,0:T(2,128)(2,1)}), bf16[512,2,640]{2,1,0:T(2,128)(2,1)S(1)}, u32[]{:S(2)}, u32[]{:S(2)}) %all-to-all-start) | async-done | bytes 1310752 | tf_op jit(solution)/shard_map/all_to_all | solution.py:214
  62.5 1.9 %shard_map.58 = bf16[512,2,256]{2,1,0:T(2,128)(2,1)S(1)} custom-call(bf16[2,64,4,2,640]{4,3,2,1,0:T(2,128)(2,1)S(1)} %bitcast.25, bf16[512,1280]{1,0:T(8,128)(2,1)S(1)} %shard_map.56.weights_ref), custom_call_target="tpu_custom_call" | custom-call | flops 805306368 | bytes 2097152 | tf_op jit(solution)/shard_map/pallas_call | solution.py:234
  64.4 31.7 %all_to_all.15.right_ref = bf16[512,2,256]{2,1,0:T(2,128)(2,1)S(1)} all-to-all(bf16[512,2,256]{2,1,0:T(2,128)(2,1)S(1)} %shard_map.58), channel_id=1, replica_groups=mesh['x'=4,'core'=2,'z'=8,'y'=8] {'core','z','y','x'}, dimensions={0} | all-to-all | bytes 1048576 | tf_op jit(solution)/shard_map/all_to_all | solution.py:241
  96.1 0.5 shard_map.59
  96.6 25.7 %all_to_all.16 = bf16[64,8,512]{2,1,0:T(8,128)(2,1)S(1)} all-to-all(bf16[64,8,512]{2,1,0:T(8,128)(2,1)S(1)} %bitcast.27), channel_id=1, replica_groups=mesh['x'=4,'core'=2,'z'=8,'y'=8] {'z','y'}, dimensions={0} | all-to-all | bytes 1048576 | tf_op jit(solution)/shard_map/all_to_all | solution.py:243
  122.3 0.9 copy.7
  (1 shorter events, 0.0 us)
Async XLA Ops:
  4.4 21.2 %copy-start.2 = (bf16[4,512,96]{1,2,0:T(8,128)(2,1)S(1)}, bf16[4,512,96]{1,2,0:T(8,128)(2,1)}, u32[]{:S(2)}) copy-start(bf16[4,512,96]{1,2,0:T(8,128)(2,1)} %param.6) | copy-start | bytes 1179652
  4.4 31.5 %copy-start = (f32[1,512,512]{2,1,0:T(8,128)S(1)}, f32[1,512,512]{2,1,0:T(8,128)}, u32[]{:S(2)}) copy-start(f32[1,512,512]{2,1,0:T(8,128)} %inverse_ref.1) | copy-start | bytes 3145732
  4.4 31.5 %copy-start.1 = (s32[256]{0:T(256)S(1)}, s32[256]{0:T(256)}, u32[]{:S(2)}) copy-start(s32[256]{0:T(256)} %param.7) | copy-start | bytes 3076
  4.4 58.1 %all-to-all-start = ((bf16[512,2,640]{2,1,0:T(2,128)(2,1)}), bf16[512,2,640]{2,1,0:T(2,128)(2,1)S(1)}, u32[]{:S(2)}, u32[]{:S(2)}) async-start(bf16[512,2,640]{2,1,0:T(2,128)(2,1)} %shard_map.55), calls=%async_computation | async-start | bytes 2621440 | tf_op jit(solution)/shard_map/all_to_all | solution.py:214
  25.6 12.9 %collective-permute-start.2 = (bf16[96,512]{1,0:T(8,128)(2,1)S(1)}, bf16[96,512]{1,0:T(8,128)(2,1)S(1)}, u32[]{:S(2)}, u32[]{:S(2)}) collective-permute-start(bf16[96,512]{1,0:T(8,128)(2,1)S(1)} %get-tuple-element.20), channel_id=1, source_target_pairs={{0,384},{128,0},{256,128},{384,256},{1,385},{129,1},{257,129},{385... | collective-permute-start | bytes 294920 | tf_op jit(solution)/shard_map/ppermute | solution.py:220
  30.2 10.9 %collective-permute-start.1 = (bf16[96,512]{1,0:T(8,128)(2,1)S(1)}, bf16[96,512]{1,0:T(8,128)(2,1)}, u32[]{:S(2)}, u32[]{:S(2)}) collective-permute-start(bf16[96,512]{1,0:T(8,128)(2,1)S(1)} %get-tuple-element.21), channel_id=1, source_target_pairs={{0,256},{128,384},{256,0},{384,128},{1,257},{129,385},{257,1},{385... | collective-permute-start | bytes 294920 | tf_op jit(solution)/shard_map/ppermute | solution.py:220
  33.0 11.7 %collective-permute-start = (bf16[96,512]{1,0:T(8,128)(2,1)S(1)}, bf16[96,512]{1,0:T(8,128)(2,1)}, u32[]{:S(2)}, u32[]{:S(2)}) collective-permute-start(bf16[96,512]{1,0:T(8,128)(2,1)S(1)} %get-tuple-element.22), channel_id=1, source_target_pairs={{0,128},{128,256},{256,384},{384,0},{1,129},{129,257},{257,385},{3... | collective-permute-start | bytes 294920 | tf_op jit(solution)/shard_map/ppermute | solution.py:220

commit v13 on v12

--- a/solution.py
+++ b/solution.py
@@ -59,7 +59,6 @@
     for q in range(LON // 128):
         table_ref[:, q * 128 : q * 128 + 128] = cos_now.astype(BF)
         cos_now, sin_now = cos_now * cos_step - sin_now * sin_step, sin_now * cos_step + cos_now * sin_step
-    table = table_ref[...]
     previous_copy.wait()
     previous = previous_ref[...].reshape(512, 512).T
     forcing_copy.wait()
@@ -69,7 +68,7 @@
         parts = []
         for h in range(3):
             part = forcing_ref[:, h * 32 : h * 32 + 32, :].reshape(256, LON)
-            parts.append(nt_dot(table[rows], part).astype(BF))
+            parts.append(nt_dot(table_ref[rows, :], part).astype(BF))
         before = previous[rows]
         for half in range(2):
             dests = pl.ds(half * 256 + block * 128, 128)

time: 124 us -> 124 us (level)
  no operation moved by 1% of the time
where the time goes in v13:
time: 124 us; the launch traced here: 123 us
  blocking collectives  59.8 us (48%)
  starting transfers between devices  31.2 us (25%)
  waiting for transfers between devices  20.6 us (17%)
  Pallas kernels  9.41 us (8%)
    all_to_all x1, blocking collectives, shards(): right = lax.all_to_all(right, ('core',) + RAD + ('x',), 0, 0, tiled=True)  31.7 us
    all_to_all x1, blocking collectives, shards(): out = lax.all_to_all(solved.reshape(64, 8, 512), RAD, 0, 0, tiled=True)  25.7 us
    all_to_all x1, starting transfers between devices, shards(): arrived = lax.all_to_all(sent, ('core',) + RAD + ('x',), 0, 0, tiled=True)  21.1 us
    all_to_all x1, waiting for transfers between devices, shards(): arrived = lax.all_to_all(sent, ('core',) + RAD + ('x',), 0, 0, tiled=True)  12.8 us
    ppermute x3, starting transfers between devices, shards(): lax.ppermute(mine, 'x', [(i, (i + shift) % 4) for i in range(4)])  10.1 us
    ppermute x3, waiting for transfers between devices, shards(): lax.ppermute(mine, 'x', [(i, (i + shift) % 4) for i in range(4)])  7.82 us
    pallas_call x1, Pallas kernels, shards(): call(fourier_kernel, bf16(512, 2, 640), [VMEM, HBM, HBM], [pltpu.VMEM((8,...  4.36 us
  transfers between devices with their start and end apart: 4, of which 4 were waited for; matrix products, arithmetic and copies ran while one was open for 1% of the time, Pallas kernels for 2%

profile of v13, /device:TPU:8, one launch (start us, length us, event | category | flops | bytes accessed | tf_op | source)
XLA Modules:
  0.0 123.3 jit_solution(14409085053605702202)
XLA Ops:
  0.0 4.4 %shard_map.55 = bf16[512,2,640]{2,1,0:T(2,128)(2,1)} custom-call(s32[1,256]{1,0:T(1,128)} %bitcast.28, bf16[8,96,1024]{2,1,0:T(8,128)(2,1)} %forcing_hbm.1, bf16[8,64,512]{2,1,0:T(8,128)(2,1)} %previous_hbm.1), custom_call_target="tpu_custom_call" | custom-call | flops 805306368 | bytes 2097152 | tf_op jit(solution)/shard_map/pallas_call | solution.py:196
  4.4 0.0 copy-start.2
  4.4 0.0 copy-start
  4.4 0.0 copy-start.1
  4.4 21.1 %all-to-all-start = ((bf16[512,2,640]{2,1,0:T(2,128)(2,1)}), bf16[512,2,640]{2,1,0:T(2,128)(2,1)S(1)}, u32[]{:S(2)}, u32[]{:S(2)}) async-start(bf16[512,2,640]{2,1,0:T(2,128)(2,1)} %shard_map.55), calls=%async_computation | async-start | bytes 2621440 | tf_op jit(solution)/shard_map/all_to_all | solution.py:213
  25.6 0.0 copy-done.2
  25.6 4.6 %collective-permute-start.2 = (bf16[96,512]{1,0:T(8,128)(2,1)S(1)}, bf16[96,512]{1,0:T(8,128)(2,1)S(1)}, u32[]{:S(2)}, u32[]{:S(2)}) collective-permute-start(bf16[96,512]{1,0:T(8,128)(2,1)S(1)} %get-tuple-element.20), channel_id=1, source_target_pairs={{0,384},{128,0},{256,128},{384,256},{1,385},{129,1},{257,129},{385... | collective-permute-start | bytes 294920 | tf_op jit(solution)/shard_map/ppermute | solution.py:219
  30.2 2.8 %collective-permute-start.1 = (bf16[96,512]{1,0:T(8,128)(2,1)S(1)}, bf16[96,512]{1,0:T(8,128)(2,1)}, u32[]{:S(2)}, u32[]{:S(2)}) collective-permute-start(bf16[96,512]{1,0:T(8,128)(2,1)S(1)} %get-tuple-element.21), channel_id=1, source_target_pairs={{0,256},{128,384},{256,0},{384,128},{1,257},{129,385},{257,1},{385... | collective-permute-start | bytes 294920 | tf_op jit(solution)/shard_map/ppermute | solution.py:219
  33.0 2.8 %collective-permute-start = (bf16[96,512]{1,0:T(8,128)(2,1)S(1)}, bf16[96,512]{1,0:T(8,128)(2,1)}, u32[]{:S(2)}, u32[]{:S(2)}) collective-permute-start(bf16[96,512]{1,0:T(8,128)(2,1)S(1)} %get-tuple-element.22), channel_id=1, source_target_pairs={{0,128},{128,256},{256,384},{384,0},{1,129},{129,257},{257,385},{3... | collective-permute-start | bytes 294920 | tf_op jit(solution)/shard_map/ppermute | solution.py:219
  35.8 0.1 pad_add_fusion.place_ref
  35.8 0.0 copy-done
  35.9 0.0 copy-done.1
  35.9 1.0 shard_map.57
  36.9 1.7 %collective-permute-done.2 = bf16[96,512]{1,0:T(8,128)(2,1)S(1)} collective-permute-done((bf16[96,512]{1,0:T(8,128)(2,1)S(1)}, bf16[96,512]{1,0:T(8,128)(2,1)S(1)}, u32[]{:S(2)}, u32[]{:S(2)}) %collective-permute-start.2) | collective-permute-done | bytes 98336 | tf_op jit(solution)/shard_map/ppermute | solution.py:219
  38.6 2.5 %collective-permute-done.1 = bf16[96,512]{1,0:T(8,128)(2,1)} collective-permute-done((bf16[96,512]{1,0:T(8,128)(2,1)S(1)}, bf16[96,512]{1,0:T(8,128)(2,1)}, u32[]{:S(2)}, u32[]{:S(2)}) %collective-permute-start.1) | collective-permute-done | bytes 98336 | tf_op jit(solution)/shard_map/ppermute | solution.py:219
  41.1 3.6 %collective-permute-done = bf16[96,512]{1,0:T(8,128)(2,1)} collective-permute-done((bf16[96,512]{1,0:T(8,128)(2,1)S(1)}, bf16[96,512]{1,0:T(8,128)(2,1)}, u32[]{:S(2)}, u32[]{:S(2)}) %collective-permute-start) | collective-permute-done | bytes 98336 | tf_op jit(solution)/shard_map/ppermute | solution.py:219
  44.7 1.0 pad_maximum_fusion
  45.7 2.4 %all-gather = bf16[8,96,512]{2,1,0:T(8,128)(2,1)S(1)} all-gather(bf16[4,96,512]{2,1,0:T(8,128)(2,1)S(1)} %pad_maximum_fusion), channel_id=2, replica_groups=mesh['x'=4,'core'=2,'z'=8,'y'=8] {'core'}, dimensions={0}, use_global_device_ids=true | all-gather | bytes 1179648 | tf_op jit(solution)/shard_map/all_gather | solution.py:220
  48.1 1.7 %shard_map.56.weights_ref = bf16[512,1280]{1,0:T(8,128)(2,1)S(1)} custom-call(s32[1,256]{1,0:T(1,128)S(1)} %bitcast.30, s32[3]{0:T(128)S(1)} %pad_add_fusion.place_ref, bf16[2,4,96,512]{3,2,1,0:T(8,128)(2,1)S(1)} %bitcast.26), custom_call_target="tpu_custom_call" | custom-call | flops 402653184 | bytes 2097152 | tf_op jit(solution)/shard_map/pallas_call | solution.py:221
  49.7 12.8 %all-to-all-done = bf16[512,2,640]{2,1,0:T(2,128)(2,1)S(1)} async-done(((bf16[512,2,640]{2,1,0:T(2,128)(2,1)}), bf16[512,2,640]{2,1,0:T(2,128)(2,1)S(1)}, u32[]{:S(2)}, u32[]{:S(2)}) %all-to-all-start) | async-done | bytes 1310752 | tf_op jit(solution)/shard_map/all_to_all | solution.py:213
  62.5 1.9 %shard_map.58 = bf16[512,2,256]{2,1,0:T(2,128)(2,1)S(1)} custom-call(bf16[2,64,4,2,640]{4,3,2,1,0:T(2,128)(2,1)S(1)} %bitcast.25, bf16[512,1280]{1,0:T(8,128)(2,1)S(1)} %shard_map.56.weights_ref), custom_call_target="tpu_custom_call" | custom-call | flops 805306368 | bytes 2097152 | tf_op jit(solution)/shard_map/pallas_call | solution.py:233
  64.4 31.7 %all_to_all.15.right_ref = bf16[512,2,256]{2,1,0:T(2,128)(2,1)S(1)} all-to-all(bf16[512,2,256]{2,1,0:T(2,128)(2,1)S(1)} %shard_map.58), channel_id=1, replica_groups=mesh['x'=4,'core'=2,'z'=8,'y'=8] {'core','z','y','x'}, dimensions={0} | all-to-all | bytes 1048576 | tf_op jit(solution)/shard_map/all_to_all | solution.py:240
  96.1 0.5 shard_map.59
  96.6 25.7 %all_to_all.16 = bf16[64,8,512]{2,1,0:T(8,128)(2,1)S(1)} all-to-all(bf16[64,8,512]{2,1,0:T(8,128)(2,1)S(1)} %bitcast.27), channel_id=1, replica_groups=mesh['x'=4,'core'=2,'z'=8,'y'=8] {'z','y'}, dimensions={0} | all-to-all | bytes 1048576 | tf_op jit(solution)/shard_map/all_to_all | solution.py:242
  122.3 0.9 copy.7
  (1 shorter events, 0.0 us)
Async XLA Ops:
  4.4 21.2 %copy-start.2 = (bf16[4,512,96]{1,2,0:T(8,128)(2,1)S(1)}, bf16[4,512,96]{1,2,0:T(8,128)(2,1)}, u32[]{:S(2)}) copy-start(bf16[4,512,96]{1,2,0:T(8,128)(2,1)} %param.6) | copy-start | bytes 1179652
  4.4 31.5 %copy-start = (f32[1,512,512]{2,1,0:T(8,128)S(1)}, f32[1,512,512]{2,1,0:T(8,128)}, u32[]{:S(2)}) copy-start(f32[1,512,512]{2,1,0:T(8,128)} %inverse_ref.1) | copy-start | bytes 3145732
  4.4 31.5 %copy-start.1 = (s32[256]{0:T(256)S(1)}, s32[256]{0:T(256)}, u32[]{:S(2)}) copy-start(s32[256]{0:T(256)} %param.7) | copy-start | bytes 3076
  4.4 58.1 %all-to-all-start = ((bf16[512,2,640]{2,1,0:T(2,128)(2,1)}), bf16[512,2,640]{2,1,0:T(2,128)(2,1)S(1)}, u32[]{:S(2)}, u32[]{:S(2)}) async-start(bf16[512,2,640]{2,1,0:T(2,128)(2,1)} %shard_map.55), calls=%async_computation | async-start | bytes 2621440 | tf_op jit(solution)/shard_map/all_to_all | solution.py:213
  25.6 12.9 %collective-permute-start.2 = (bf16[96,512]{1,0:T(8,128)(2,1)S(1)}, bf16[96,512]{1,0:T(8,128)(2,1)S(1)}, u32[]{:S(2)}, u32[]{:S(2)}) collective-permute-start(bf16[96,512]{1,0:T(8,128)(2,1)S(1)} %get-tuple-element.20), channel_id=1, source_target_pairs={{0,384},{128,0},{256,128},{384,256},{1,385},{129,1},{257,129},{385... | collective-permute-start | bytes 294920 | tf_op jit(solution)/shard_map/ppermute | solution.py:219
  30.2 10.9 %collective-permute-start.1 = (bf16[96,512]{1,0:T(8,128)(2,1)S(1)}, bf16[96,512]{1,0:T(8,128)(2,1)}, u32[]{:S(2)}, u32[]{:S(2)}) collective-permute-start(bf16[96,512]{1,0:T(8,128)(2,1)S(1)} %get-tuple-element.21), channel_id=1, source_target_pairs={{0,256},{128,384},{256,0},{384,128},{1,257},{129,385},{257,1},{385... | collective-permute-start | bytes 294920 | tf_op jit(solution)/shard_map/ppermute | solution.py:219
  33.0 11.7 %collective-permute-start = (bf16[96,512]{1,0:T(8,128)(2,1)S(1)}, bf16[96,512]{1,0:T(8,128)(2,1)}, u32[]{:S(2)}, u32[]{:S(2)}) collective-permute-start(bf16[96,512]{1,0:T(8,128)(2,1)S(1)} %get-tuple-element.22), channel_id=1, source_target_pairs={{0,128},{128,256},{256,384},{384,0},{1,129},{129,257},{257,385},{3... | collective-permute-start | bytes 294920 | tf_op jit(solution)/shard_map/ppermute | solution.py:219
